TPU v7x, 32 devices: a whole 2x2x4 slice. The times are simulated.
32 devices in a mesh: seq: 8 (over z, y), neur: 4 (over x, core).
Axes of the slice: x: 2, y: 2, z: 4, core: 2. Of those that a mesh axis runs over, the one named last changes fastest.
Arguments:
- tokens: bfloat16 [8, 704, 2000], P('seq', None, 'neur'), may hold values from -8 to 8
- w_first: bfloat16 [2000, 2000], P(None, 'neur'), may hold values from -0.125 to 0.125
- gain_first: float32 [2000], P('neur'), may hold values from 0.5 to 1.5
- shift_first: float32 [2000], P('neur'), may hold values from -0.5 to 0.5
- decay_first: float32 [2000], P('neur'), may hold values from 0 to 0.999
- w_second: bfloat16 [2000, 2000], P(None, 'neur'), may hold values from -0.125 to 0.125
- gain_second: float32 [2000], P('neur'), may hold values from 0.5 to 1.5
- shift_second: float32 [2000], P('neur'), may hold values from -0.5 to 0.5
- decay_second: float32 [2000], P('neur'), may hold values from 0 to 0.999
- cotangent: bfloat16 [8, 704, 2000], P('seq', None, 'neur'), may hold values from -6 to 6
- running_mean: float32 [2, 2000], P(None, 'neur'), may hold values from -6 to 6
- running_var: float32 [2, 2000], P(None, 'neur'), may hold values from 0.5 to 2
Outputs:
- first_out: bfloat16 [8, 704, 2000], P('seq', None, 'neur')
- second_out: bfloat16 [8, 704, 2000], P('seq', None, 'neur')
- input_grad: float32 [8, 704, 2000], P('seq', None, 'neur')
- grad_w_first: float32 [2000, 2000], P(None, 'neur')
- grad_w_second: float32 [2000, 2000], P(None, 'neur')
- grad_gain: float32 [2, 2000], P(None, 'neur')
- grad_shift: float32 [2, 2000], P(None, 'neur')
- grad_decay: float32 [2, 2000], P(None, 'neur')
- new_mean: float32 [2, 2000], P(None, 'neur')
- new_var: float32 [2, 2000], P(None, 'neur')
All inputs are finite; a program needn't handle non-finite values.
Results may differ from a plain program's by a relative error of at most 0.0053.
Values may be sent and summed in bfloat16 or wider, within the bound.
No kernel may reach another device: no remote copies, remote signals or barrier semaphores. Data moves between devices by JAX's collectives and lax.ppermute only.
A program may use at most 128 MiB of HBM per device.

v0:
```python
import functools
import math

import jax
import jax.numpy as jnp
from jax import lax
from jax.experimental import pallas as pl
from jax.experimental.pallas import tpu as pltpu
from jax.sharding import PartitionSpec as P

EPSILON = 1e-05
MOMENTUM = 0.1
LANE = 128
CHUNKS = 32
GROUPS = CHUNKS // 8
TOLERANCE = 1e-5
LOG2E = math.log2(math.e)
LN2 = math.log(2.0)
F32 = jnp.float32
BF16 = jnp.bfloat16
VMEM_BYTES = 50 * 1024 * 1024


def call(kernel, outs, scratch=(), flops=0, nbytes=0):
    return pl.pallas_call(
        kernel,
        out_shape=outs,
        scratch_shapes=list(scratch),
        compiler_params=pltpu.CompilerParams(vmem_limit_bytes=VMEM_BYTES),
        cost_estimate=pl.CostEstimate(flops=flops, bytes_accessed=nbytes, transcendentals=0),
    )


def shape(*dims, dtype=F32):
    return jax.ShapeDtypeStruct(dims, dtype)


def tiles_of(width):
    return [(j, j * LANE, min(LANE, width - j * LANE)) for j in range(-(-width // LANE))]


def dot(a, b):
    return jnp.dot(a, b, preferred_element_type=F32)


def dot_nt(a, b):
    return lax.dot_general(a, b, (((1,), (1,)), ((), ())), preferred_element_type=F32)


def block_kernel(w_ref, out_ref, mate_ref):
    here = lax.axis_index("neur")
    blocks, width, _ = out_ref.shape
    real = w_ref.shape[0] // blocks
    out_ref[...] = jnp.zeros(out_ref.shape, BF16)
    for b in range(blocks):
        out_ref[b, :real, : w_ref.shape[1]] = w_ref[b * real : (b + 1) * real, :]
    for i, k in enumerate((1, 3)):
        mate_ref[i] = out_ref[here ^ k]


def means_of(x_ref):
    length = x_ref.shape[0]
    return dot(jnp.ones((16, length), BF16), x_ref[...])[:1] * (1.0 / length)


def project_early(own_ref, mate_ref, w_ref, part_ref, means_ref):
    here = lax.axis_index("neur")
    k = own_ref.shape[1]
    means_ref[...] = jnp.zeros(means_ref.shape, F32)
    means_ref[0:1, :k] = means_of(own_ref)
    means_ref[1:2, :k] = means_of(mate_ref)
    for c in range(0, part_ref.shape[1], 256):
        part_ref[:, c : c + 256] = dot(own_ref[...], w_ref[here, :k, c : c + 256]) + dot(
            mate_ref[...], w_ref[here ^ 1, :k, c : c + 256]
        )


def project_late(part_ref, means_ref, far_ref, cross_ref, w_ref, proj_ref, stats_ref):
    here = lax.axis_index("neur")
    k = far_ref.shape[1]
    peers, _, width = stats_ref.shape
    far, cross = means_of(far_ref), means_of(cross_ref)
    for p in range(peers):
        stats_ref[p, 2:4, :] = means_ref[0:2, :]
        stats_ref[p, 4:8, :] = jnp.zeros((4, width), F32)
        stats_ref[p, 4:5, :k] = far
        stats_ref[p, 5:6, :k] = cross
    length = proj_ref.shape[0]
    for c in range(0, part_ref.shape[1], 256):
        y = (
            part_ref[:, c : c + 256]
            + dot(far_ref[...], w_ref[here ^ 2, :k, c : c + 256])
            + dot(cross_ref[...], w_ref[here ^ 3, :k, c : c + 256])
        )
        proj_ref[:, c : c + 256] = y
        mean = jnp.sum(y, axis=0, keepdims=True) * (1.0 / length)
        off = y - mean
        spread = jnp.sum(off * off, axis=0, keepdims=True)
        for p in range(stats_ref.shape[0]):
            stats_ref[p, 0:1, c : c + 256] = mean
            stats_ref[p, 1:2, c : c + 256] = spread


def merged(stats_ref, length, sum_ref):
    peers = stats_ref.shape[0]
    means = [stats_ref[p, 0:1, :] for p in range(peers)]
    mean = sum(means[1:], means[0]) * (1.0 / peers)
    total = None
    for p in range(peers):
        off = means[p] - mean
        term = stats_ref[p, 1:2, :] + off * off * float(length)
        total = term if total is None else total + term
    var = total * (1.0 / (peers * length))
    inverse = lax.rsqrt(var + EPSILON)
    features = stats_ref[0, 2:6, :]
    for p in range(1, peers):
        features = features + stats_ref[p, 2:6, :]
    sum_ref[0:1, :] = mean
    sum_ref[1:2, :] = var
    sum_ref[2:3, :] = inverse
    sum_ref[3:4, :] = jnp.zeros_like(mean)
    sum_ref[4:8, :] = features * (1.0 / peers)
    return mean, var, inverse


def spread_rows(row, tiles):
    return [jnp.broadcast_to(row[:, c : c + LANE], (8, LANE)) for _, c, _ in tiles]


def load_step(ref, step, tiles, lead=0):
    steps = (ref.shape[1] - lead) // CHUNKS
    return [
        ref[j, pl.ds(lead + step + g * 8 * steps, 8, stride=steps), :]
        for j, _, _ in tiles
        for g in range(GROUPS)
    ]


def store_step(ref, step, tiles, values, lead=0):
    steps = (ref.shape[1] - lead) // CHUNKS
    i = 0
    for j, _, _ in tiles:
        for g in range(GROUPS):
            ref[j, pl.ds(lead + step + g * 8 * steps, 8, stride=steps), :] = values[i]
            i += 1


def load_edges(ref, tiles):
    return [ref[g * 8 : g * 8 + 8, c : c + LANE] for _, c, _ in tiles for g in range(GROUPS)]


def store_edges(ref, tiles, values):
    i = 0
    for _, c, _ in tiles:
        for g in range(GROUPS):
            ref[g * 8 : g * 8 + 8, c : c + LANE] = values[i]
            i += 1


def power(x, n):
    out = None
    while n:
        if n & 1:
            out = x if out is None else out * x
        x = x * x
        n >>= 1
    return out


def run_chunks(drive_ref, state_ref, start, decay, tiles, steps, store):
    u2 = [d * LOG2E for d in decay for _ in range(GROUPS)]

    def body(step, carry):
        state, slope = carry
        drive = load_step(drive_ref, step, tiles)
        before = [d + u * s for d, u, s in zip(drive, u2, state)]
        soft = [jnp.log(1.0 + jnp.exp2(b)) for b in before]
        state = [jnp.where(b > 25.0, b * LN2, s) for b, s in zip(before, soft)]
        slope = [a + (b - s * LOG2E) for a, b, s in zip(slope, before, state)]
        if store:
            store_step(state_ref, step, tiles, state, lead=8)
        return state, slope

    zero = [jnp.zeros((8, LANE), F32) for _ in start]
    state, slope = lax.fori_loop(0, steps, body, (start, zero))
    top = [power(d, steps) for d in decay for _ in range(GROUPS)]
    return state, [t * jnp.exp2(a) for t, a in zip(top, slope)]


def run_line(drive_ref, decay, tiles, steps):
    u = [d for d in decay for _ in range(GROUPS)]

    def body(step, line):
        return [d + a * s for d, a, s in zip(load_step(drive_ref, step, tiles), u, line)]

    line = lax.fori_loop(0, steps, body, [jnp.zeros((8, LANE), F32) for _ in u])
    return [a * LN2 for a in line]


def solve(drive_ref, state_ref, decay_row, tiles, edges):
    from_zero, zero_slope, line_end, start_ref, end_ref, slope_ref = edges
    steps = drive_ref.shape[1] // CHUNKS
    decay = spread_rows(decay_row, tiles)
    width = start_ref.shape[1]
    top = power(decay_row, steps)

    end, slope = run_chunks(drive_ref, state_ref, [jnp.zeros((8, LANE), F32)] * (len(tiles) * GROUPS), decay, tiles, steps, False)
    store_edges(from_zero, tiles, end)
    store_edges(zero_slope, tiles, slope)
    store_edges(line_end, tiles, run_line(drive_ref, decay, tiles, steps))

    def sweep(newton):
        first = jnp.zeros((1, width), F32)
        old = first
        start_ref[0:1, :] = first
        worst = None
        for c in range(CHUNKS - 1):
            at = pl.ds(c, 1)
            value = jnp.maximum(
                from_zero[at, :] + zero_slope[at, :] * first, line_end[at, :] + top * first
            )
            if newton:
                reached = end_ref[at, :]
                value = jnp.maximum(value, reached + slope_ref[at, :] * (first - old))
                old = start_ref[c + 1 : c + 2, :]
                miss = jnp.abs(reached - old) - TOLERANCE * jnp.maximum(old, 1.0)
                worst = miss if worst is None else jnp.maximum(worst, miss)
            start_ref[c + 1 : c + 2, :] = value
            first = value
        return worst

    sweep(False)

    def again(carry):
        count, worst = carry
        return jnp.logical_and(worst > 0.0, count < CHUNKS + 1)

    def newton(carry):
        count, _ = carry
        end, slope = run_chunks(
            drive_ref, state_ref, load_edges(start_ref, tiles), decay, tiles, steps, True
        )
        store_edges(end_ref, tiles, end)
        store_edges(slope_ref, tiles, slope)
        return count + 1, jnp.max(sweep(True))

    lax.while_loop(again, newton, (jnp.int32(0), jnp.float32(1.0)))


def run_back(grad_ref, sigma_ref, start, decay, tiles, steps, store):
    u = [d for d in decay for _ in range(GROUPS)]

    def body(i, carry):
        z, prod = carry
        step = steps - 1 - i
        gs = load_step(grad_ref, step, tiles)
        sig = load_step(sigma_ref, step, tiles)
        z = [s * (g + a * v) for s, g, a, v in zip(sig, gs, u, z)]
        if store:
            store_step(grad_ref, step, tiles, z)
            return z, prod
        return z, [p * (s * a) for p, s, a in zip(prod, sig, u)]

    ones = [] if store else [jnp.ones((8, LANE), F32) for _ in start]
    return lax.fori_loop(0, steps, body, (start, ones))


def solve_back(grad_ref, sigma_ref, decay_row, tiles, edges):
    _, _, _, start_ref, end_ref, slope_ref = edges
    steps = grad_ref.shape[1] // CHUNKS
    decay = spread_rows(decay_row, tiles)
    zero = [jnp.zeros((8, LANE), F32)] * (len(tiles) * GROUPS)
    end, slope = run_back(grad_ref, sigma_ref, zero, decay, tiles, steps, False)
    store_edges(end_ref, tiles, end)
    store_edges(slope_ref, tiles, slope)
    value = jnp.zeros((1, start_ref.shape[1]), F32)
    for c in range(CHUNKS - 1, -1, -1):
        start_ref[c : c + 1, :] = value
        value = end_ref[c : c + 1, :] + slope_ref[c : c + 1, :] * value
    run_back(grad_ref, sigma_ref, load_edges(start_ref, tiles), decay, tiles, steps, True)


BLOCK = 88


def row_blocks(length, body):
    @pl.loop(0, length // BLOCK)
    def _(i):
        body(pl.ds(pl.multiple_of(i * BLOCK, 8), BLOCK))


def fill_drive(proj_ref, drive_ref, mean, inverse, gain, shift, tiles):
    scale = inverse * gain * LOG2E
    offset = shift * LOG2E

    def body(rows):
        for j, c, _ in tiles:
            at = slice(c, c + LANE)
            drive_ref[j, rows, :] = (proj_ref[rows, at] - mean[:, at]) * scale[:, at] + offset[:, at]

    row_blocks(proj_ref.shape[0], body)


def fill_sigma(drive_ref, prev_ref, decay_row, tiles, length):
    u2 = decay_row * LOG2E

    def body(i, _):
        for j, c, _w in tiles:
            rows = pl.ds(pl.multiple_of(i * BLOCK, 8), BLOCK)
            before = drive_ref[j, rows, :] + u2[:, c : c + LANE] * prev_ref[j, pl.ds(i * BLOCK + 7, BLOCK), :]
            drive_ref[j, rows, :] = 1.0 / (1.0 + jnp.exp2(-before))
        return 0

    lax.fori_loop(0, length // BLOCK, body, 0)


def finish_back(grad_ref, state_ref, proj_ref, mean, inverse, tiles, gb_ref, sums_ref):
    length, width = proj_ref.shape
    zero = tuple(jnp.zeros((1, LANE), F32) for _ in tiles)

    def body(i, carry):
        shift, gain, decay = (list(x) for x in carry)
        rows = pl.ds(pl.multiple_of(i * BLOCK, 8), BLOCK)
        for j, c, _w in tiles:
            at = slice(c, c + LANE)
            gb = grad_ref[j, rows, :]
            gb_ref[rows, at] = gb
            shift[j] = shift[j] + jnp.sum(gb, axis=0, keepdims=True)
            gain[j] = gain[j] + jnp.sum(gb * (proj_ref[rows, at] - mean[:, at]), axis=0, keepdims=True)
            decay[j] = decay[j] + jnp.sum(
                gb * state_ref[j, pl.ds(i * BLOCK + 7, BLOCK), :], axis=0, keepdims=True
            )
        return tuple(shift), tuple(gain), tuple(decay)

    shift, gain, decay = lax.fori_loop(0, length // BLOCK, body, (zero, zero, zero))
    for j, c, _ in tiles:
        at = slice(c, c + LANE)
        scaled = gain[j] * inverse[:, at]
        for p in range(sums_ref.shape[0]):
            sums_ref[p, 0:1, at] = shift[j]
            sums_ref[p, 1:2, at] = scaled
            sums_ref[p, 2:3, at] = decay[j]


def clear(state_ref, tiles):
    for j, _, _ in tiles:
        state_ref[j, 0:8, :] = jnp.zeros((8, LANE), F32)


def put_states(state_ref, out_ref, tiles, wide_ref=None):
    def body(i, _):
        rows = pl.ds(pl.multiple_of(i * 16, 16), 16)
        for j, c, w in tiles:
            s = state_ref[j, pl.ds(pl.multiple_of(8 + i * 16, 8), 16), :]
            out_ref[rows, c : c + w] = s[:, :w].astype(BF16)
            if wide_ref is not None:
                wide_ref[rows, c : c + LANE] = s
        return 0

    lax.fori_loop(0, out_ref.shape[0] // 16, body, 0)


def forward_kernel(stats_ref, proj_ref, par_ref, out_ref, wide_ref, sum_ref, drive, state, *edges):
    length, width = proj_ref.shape
    tiles = tiles_of(width)
    outs = tiles_of(out_ref.shape[1])
    mean, var, inverse = merged(stats_ref, length, sum_ref)
    gain, shift, decay = par_ref[0:1, :], par_ref[1:2, :], par_ref[2:3, :]
    fill_drive(proj_ref, drive, mean, inverse, gain, shift, tiles)
    clear(state, tiles)
    solve(drive, state, decay, tiles, edges)
    put_states(state, out_ref, outs, wide_ref)


def turn_kernel(
    stats_ref,
    proj_ref,
    par_ref,
    cot_ref,
    first_ref,
    rmean_ref,
    rvar_ref,
    out_ref,
    gb_ref,
    sums_ref,
    sum_ref,
    nmean_ref,
    nvar_ref,
    drive,
    state,
    grad,
    *edges,
):
    length, width = proj_ref.shape
    tiles = tiles_of(width)
    outs = tiles_of(out_ref.shape[1])
    mean, var, inverse = merged(stats_ref, length, sum_ref)
    gain, shift, decay = par_ref[0:1, :], par_ref[1:2, :], par_ref[2:3, :]
    real = out_ref.shape[1]
    count = float(stats_ref.shape[0] * length)
    for row, m, v in ((0, first_ref[0:1, :], first_ref[1:2, :]), (1, mean, var)):
        nmean_ref[row : row + 1, :] = (1.0 - MOMENTUM) * rmean_ref[row : row + 1, :] + MOMENTUM * m[:, :real]
        nvar_ref[row : row + 1, :] = (1.0 - MOMENTUM) * rvar_ref[row : row + 1, :] + (
            MOMENTUM * v[:, :real]
        ) * (count / (count - 1.0))
    fill_drive(proj_ref, drive, mean, inverse, gain, shift, tiles)
    clear(state, tiles)
    solve(drive, state, decay, tiles, edges)
    put_states(state, out_ref, outs)
    fill_sigma(drive, state, decay, tiles, length)
    for j, _, w in outs:
        if w < LANE:
            grad[j] = jnp.zeros(grad.shape[1:], F32)

    def load_cot(i, _):
        rows = pl.ds(pl.multiple_of(i * 16, 16), 16)
        for j, c, w in outs:
            grad[j, rows, :w] = cot_ref[rows, c : c + w].astype(F32)
        return 0

    lax.fori_loop(0, length // 16, load_cot, 0)
    solve_back(grad, drive, decay, tiles, edges)
    finish_back(grad, state, proj_ref, mean, inverse, tiles, gb_ref, sums_ref)


def back_kernel(
    keep_ref, got_ref, proj_ref, wide_ref, sum_ref, par_ref, gb_ref, sums_ref, drive, state, grad, *edges
):
    length, width = proj_ref.shape
    tiles = tiles_of(width)
    mean, inverse = sum_ref[0:1, :], sum_ref[2:3, :]
    gain, shift, decay = par_ref[0:1, :], par_ref[1:2, :], par_ref[2:3, :]
    fill_drive(proj_ref, drive, mean, inverse, gain, shift, tiles)
    clear(state, tiles)

    def load(i, _):
        rows = pl.ds(pl.multiple_of(i * 16, 16), 16)
        for j, c, _w in tiles:
            at = slice(c, c + LANE)
            grad[j, rows, :] = keep_ref[rows, at] + got_ref[rows, at].astype(F32)
            state[j, pl.ds(pl.multiple_of(8 + i * 16, 8), 16), :] = wide_ref[rows, at]
        return 0

    lax.fori_loop(0, length // 16, load, 0)
    fill_sigma(drive, state, decay, tiles, length)
    solve_back(grad, drive, decay, tiles, edges)
    finish_back(grad, state, proj_ref, mean, inverse, tiles, gb_ref, sums_ref)


def total_of(sums_ref):
    peers = sums_ref.shape[0]
    out = sums_ref[0]
    for p in range(1, peers):
        out = out + sums_ref[p]
    return out


def grad_kernel(sums_ref, gb_ref, proj_ref, sum_ref, par_ref, g_ref, total_ref):
    length, _ = proj_ref.shape
    total = total_of(sums_ref)
    total_ref[...] = total
    count = float(sums_ref.shape[0] * length)
    mean, inverse = sum_ref[0:1, :], sum_ref[2:3, :]
    scale = par_ref[0:1, :] * inverse
    base = total[0:1, :] * (1.0 / count)
    lean = total[1:2, :] * (1.0 / count) * inverse

    def body(i, summed):
        rows = pl.ds(pl.multiple_of(i * 16, 16), 16)
        g = scale * (gb_ref[rows, :] - base - (proj_ref[rows, :] - mean) * lean)
        g_ref[rows, :] = g.astype(BF16)
        return summed + (g[:8] + g[8:])

    summed = lax.fori_loop(0, length // 16, body, jnp.zeros((8, g_ref.shape[1]), F32))
    total_ref[7:8, :] = jnp.sum(summed, axis=0, keepdims=True)


def send_kernel(g_ref, mate_ref, w_ref, wmate_ref, out_ref):
    here = lax.axis_index("neur")
    for c in range(0, out_ref.shape[1], 256):
        at = slice(c, c + 256)
        out_ref[:, at] = (
            dot_nt(g_ref[...], w_ref[here ^ 2, at, :]) + dot_nt(mate_ref[...], wmate_ref[1, at, :])
        ).astype(BF16)


def keep_kernel(g_ref, mate_ref, w_ref, wmate_ref, out_ref):
    here = lax.axis_index("neur")
    for c in range(0, out_ref.shape[1], 256):
        at = slice(c, c + 256)
        out_ref[:, at] = dot_nt(g_ref[...], w_ref[here, at, :]) + dot_nt(
            mate_ref[...], wmate_ref[0, at, :]
        )


def outer(a, b):
    return lax.dot_general(
        a, b, (((0,), (0,)), ((), ())), precision=lax.Precision.HIGHEST, preferred_element_type=F32
    )


def weight_kernel(own_ref, mate_ref, far_ref, cross_ref, g_ref, sum_ref, total_ref, *refs):
    outs, hold = refs[:-1], refs[-1]
    place = lax.axis_index("seq") & 7
    half, width = outs[0].shape
    alone = lax.broadcasted_iota(jnp.int32, (8, width), 0) == 0
    summed = jnp.where(alone, total_ref[7:8, :], 0.0)
    for k, x_ref in enumerate((own_ref, mate_ref, far_ref, cross_ref)):
        real = x_ref.shape[1]
        mean = jnp.where(alone, sum_ref[4 + k : 5 + k, :], 0.0)[:, :real]
        part = lax.dot_general(
            x_ref[...], g_ref[...], (((0,), (0,)), ((), ())), preferred_element_type=F32
        )
        part = (part - outer(mean, summed)).astype(BF16)
        hold[(2 * k) ^ place] = part[:half]
        rest = part[half:]
        hold[(2 * k + 1) ^ place, : rest.shape[0], :] = rest
    for r, out in enumerate(outs):
        out[...] = hold[r]


def spread_kernel(*refs):
    shares, out_ref, hold = refs[:-2], refs[-2], refs[-1]
    place, here = lax.axis_index("seq") & 7, lax.axis_index("neur")
    for r, share in enumerate(shares):
        hold[r] = share[...]
    half = shares[0].shape[0]
    block = out_ref.shape[0] // 4
    width = out_ref.shape[1]
    for b in range(4):
        for h in range(2):
            low, high = b * block + h * half, min(b * block + h * half + half, (b + 1) * block)
            which = (((here ^ b) * 2) + h) ^ place
            out_ref[low:high, :] = hold[which, : high - low, :width].astype(F32)


def half_sum(a, b):
    return (a.astype(F32) + b.astype(F32)).astype(BF16)


def swap(x, bit, axis="seq"):
    n = lax.axis_size(axis)
    return lax.ppermute(x, axis, [(i, i ^ bit) for i in range(n)])


def reduce_shares(shares):
    part = {(r >> 2 & 1, r >> 1 & 1, r & 1): v for r, v in enumerate(shares)}
    got = {q: swap(part[(1,) + q], 4) for q in ((1, 1), (1, 0), (0, 1), (0, 0))}
    mine = {q: half_sum(part[(0,) + q], v) for q, v in got.items()}
    first = half_sum(mine[(0, 1)], swap(mine[(1, 1)], 2))
    last = half_sum(mine[(0, 0)], swap(mine[(1, 0)], 2))
    return half_sum(last, swap(first, 1))


def gather_shares(v):
    out = {0: v}
    out[1] = swap(v, 1)
    out[2] = swap(v, 2)
    out[4] = swap(v, 4)
    out[3] = swap(out[1], 2)
    out[6] = swap(out[2], 4)
    out[5] = swap(out[1], 4)
    out[7] = swap(out[3], 4)
    return [out[r] for r in range(8)]


def per_device(devices_seq, *args):
    (
        tokens,
        w_first,
        gain_first,
        shift_first,
        decay_first,
        w_second,
        gain_second,
        shift_second,
        decay_second,
        cotangent,
        running_mean,
        running_var,
    ) = args
    _, length, real = tokens.shape
    width = -(-real // LANE) * LANE
    tiles = len(tiles_of(width))
    peers = devices_seq
    here = lax.axis_index("neur")
    tokens, cotangent = tokens[0], cotangent[0]

    def blocks(w):
        return call(
            block_kernel,
            [shape(4, width, width, dtype=BF16), shape(2, width, width, dtype=BF16)],
            nbytes=5 << 20,
        )(w)

    def params(*rows):
        return jnp.pad(jnp.stack(rows), ((0, 5), (0, width - real)))

    scans = [
        pltpu.VMEM((tiles, length, LANE), F32),
        pltpu.VMEM((tiles, length + 8, LANE), F32),
    ]
    grads = [pltpu.VMEM((tiles, length, LANE), F32)]
    edges = [pltpu.VMEM((CHUNKS, width), F32)] * 6
    big = 2 * length * real * real

    def share(stats):
        return lax.all_to_all(stats, "seq", 0, 0, tiled=True)

    def project(own, make):
        far = swap(own, 2, "neur")
        mate = swap(own, 1, "neur")
        w4, ready = make()
        part, means = call(
            project_early, [shape(length, width), shape(8, width)], flops=2 * big, nbytes=4 << 20
        )(own, mate, w4)
        far, part, ready = lax.optimization_barrier((far, part, ready))
        cross = swap(far, 1, "neur")
        proj, stats = call(
            project_late, [shape(length, width), shape(peers, 8, width)], flops=2 * big, nbytes=6 << 20
        )(part, means, far, cross, w4)
        return (own, mate, far, cross), proj, share(stats), ready

    def back(sums, gb, proj, summary, par, w4, wm):
        g, total = call(
            grad_kernel, [shape(length, width, dtype=BF16), shape(8, width)], nbytes=5 << 20
        )(share(sums), gb, proj, summary, par)
        mate = swap(g, 1, "neur")
        send = call(send_kernel, shape(length, width, dtype=BF16), flops=2 * big, nbytes=4 << 20)(
            g, mate, w4, wm
        )
        got = swap(send, 2, "neur")
        keep = call(keep_kernel, shape(length, width), flops=2 * big, nbytes=4 << 20)(g, mate, w4, wm)
        return g, total, keep, got

    def weights(x, g, summary, total):
        half = width // 2
        shares = call(
            weight_kernel,
            [shape(half, width, dtype=BF16)] * 8,
            [pltpu.VMEM((8, half, width), BF16)],
            flops=4 * big,
            nbytes=6 << 20,
        )(*x, g, summary, total)
        if peers == 8:
            shares = gather_shares(reduce_shares(shares))
        else:
            place = lax.axis_index("seq")
            order = jnp.stack([lax.dynamic_index_in_dim(jnp.stack(shares), (place & 7) ^ r, 0, False) for r in range(8)])
            whole = lax.psum(order, "seq")
            shares = [lax.dynamic_index_in_dim(whole, (place & 7) ^ r, 0, False) for r in range(8)]
        return call(
            spread_kernel,
            shape(4 * real, real),
            [pltpu.VMEM((8, half, width), BF16)],
            nbytes=6 << 20,
        )(*shares)

    def prepare():
        first, first_give = blocks(w_first)
        second, second_give = blocks(w_second)
        return first, (
            first,
            second,
            swap(first_give, 1, "neur"),
            swap(second_give, 1, "neur"),
            params(gain_first, shift_first, decay_first),
            params(gain_second, shift_second, decay_second),
        )

    first_x, first_proj, first_stats, ready = project(tokens, prepare)
    first_w, second_w, first_mate, second_mate, first_par, second_par = ready
    first_out, first_wide, first_sum = call(
        forward_kernel,
        [shape(length, real, dtype=BF16), shape(length, width), shape(8, width)],
        scans + edges,
        nbytes=8 << 20,
    )(first_stats, first_proj, first_par)

    second_x, second_proj, second_stats, _ = project(first_out, lambda: (second_w, ()))
    second_out, second_gb, second_sums, second_sum, new_mean, new_var = call(
        turn_kernel,
        [
            shape(length, real, dtype=BF16),
            shape(length, width),
            shape(peers, 8, width),
            shape(8, width),
            shape(2, real),
            shape(2, real),
        ],
        scans + grads + edges,
        nbytes=12 << 20,
    )(second_stats, second_proj, second_par, cotangent, first_sum, running_mean, running_var)

    second_g, second_total, keep, got = back(
        second_sums, second_gb, second_proj, second_sum, second_par, second_w, second_mate
    )
    grad_w_second = weights(second_x, second_g, second_sum, second_total)
    first_gb, first_sums = call(
        back_kernel,
        [shape(length, width), shape(peers, 8, width)],
        scans + grads + edges,
        nbytes=10 << 20,
    )(keep, got, first_proj, first_wide, first_sum, first_par)
    first_g, first_total, keep, got = back(
        first_sums, first_gb, first_proj, first_sum, first_par, first_w, first_mate
    )
    grad_w_first = weights(first_x, first_g, first_sum, first_total)
    input_grad = (keep + got.astype(F32))[:, :real]

    def pair(row):
        return jnp.stack([first_total[row, :real], second_total[row, :real]])

    return (
        first_out[None],
        second_out[None],
        input_grad[None],
        grad_w_first,
        grad_w_second,
        pair(1),
        pair(0),
        pair(2),
        new_mean,
        new_var,
    )


def solution(mesh):
    rows, line, flat = P("seq", None, "neur"), P("neur"), P(None, "neur")
    return jax.shard_map(
        functools.partial(per_device, mesh.shape["seq"]),
        mesh=mesh,
        in_specs=(rows, flat, line, line, line, flat, line, line, line, rows, flat, flat),
        out_specs=(rows, rows, rows) + (flat,) * 7,
        check_vma=False,
    )
```

profile of v0, /device:TPU:0, one launch (start us, length us, event | category | flops | bytes accessed | tf_op | source)
XLA Modules:
  0.0 361.5 jit_solution(3159711081904392203)
XLA Ops:
  6.6 2.9 collective-permute-start
  13.9 11.9 %collective-permute-done.far_ref = bf16[704,500]{1,0:T(8,128)(2,1)S(1)} collective-permute-done((bf16[704,500]{1,0:T(8,128)(2,1)S(1)}, bf16[704,500]{1,0:T(8,128)(2,1)S(1)}, u32[]{:S(2)}, u32[]{:S(2)}) %collective-permute-start) | collective-permute-done | bytes 704032 | tf_op jit(solution)/shard_map/ppermute | solution.py:543
  28.1 3.6 shard_map.198
  31.8 13.2 %all_to_all.20.stats_ref = f32[8,8,512]{2,1,0:T(8,128)S(1)} all-to-all(f32[8,8,512]{2,1,0:T(8,128)S(1)} %get-tuple-element.71), channel_id=1, replica_groups=mesh['seq'=8,'neur'=4] {'seq'}, dimensions={0} | all-to-all | bytes 262144 | tf_op jit(solution)/shard_map/all_to_all | solution.py:608
  45.0 7.7 %shard_map.199 = (bf16[704,500]{1,0:T(8,128)(2,1)}, f32[704,512]{1,0:T(8,128)S(1)}, f32[8,512]{1,0:T(8,128)S(1)}) custom-call(f32[8,8,512]{2,1,0:T(8,128)S(1)} %all_to_all.20.stats_ref, f32[704,512]{1,0:T(8,128)S(1)} %get-tuple-element.72.proj_ref, f32[8,512]{1,0:T(8,128)S(1)} %get-tuple-element.73.par_ref), custom_call_target="tpu_custom_call" | custom-call | bytes 8388608 | tf_op jit(solution)/shard_map/pallas_call | solution.py:673
  61.1 11.5 %collective-permute-done.5.far_ref = bf16[704,500]{1,0:T(8,128)(2,1)S(1)} collective-permute-done((bf16[704,500]{1,0:T(8,128)(2,1)}, bf16[704,500]{1,0:T(8,128)(2,1)S(1)}, u32[]{:S(2)}, u32[]{:S(2)}) %collective-permute-start.5) | collective-permute-done | bytes 704032 | tf_op jit(solution)/shard_map/ppermute | solution.py:543
  74.8 3.6 %shard_map.201 = (f32[704,512]{1,0:T(8,128)S(1)}, f32[8,8,512]{2,1,0:T(8,128)S(1)}) custom-call(f32[704,512]{1,0:T(8,128)} %copy-done.12, f32[8,512]{1,0:T(8,128)S(1)} %get-tuple-element.78.means_ref, bf16[704,500]{1,0:T(8,128)(2,1)S(1)} %collective-permute-done.5.far_ref, bf16[704,500]{1,0:T(8,128)(2,1)S(1)} %collective-permute-done.7.cross_ref, ...), custom_call_target="tpu_custom_call" | custom-call | flops 704000000 | bytes 6291456 | tf_op jit(solution)/shard_map/pallas_call | solution.py:619
  78.4 10.0 %all_to_all.21.stats_ref = f32[8,8,512]{2,1,0:T(8,128)S(1)} all-to-all(f32[8,8,512]{2,1,0:T(8,128)S(1)} %get-tuple-element.80), channel_id=1, replica_groups=mesh['seq'=8,'neur'=4] {'seq'}, dimensions={0} | all-to-all | bytes 262144 | tf_op jit(solution)/shard_map/all_to_all | solution.py:608
  88.4 10.2 %shard_map.202 = (bf16[704,500]{1,0:T(8,128)(2,1)}, f32[704,512]{1,0:T(8,128)S(1)}, f32[8,8,512]{2,1,0:T(8,128)S(1)}, f32[8,512]{1,0:T(8,128)S(1)}, f32[2,500]{1,0:T(2,128)}, /*index=5*/f32[2,500]{1,0:T(2,128)}) custom-call(f32[8,8,512]{2,1,0:T(8,128)S(1)} %all_to_all.21.stats_ref, f32[704,512]{1,0:T(8,128)S(1)} %get-tuple-element.81.proj_ref, ...), custom_call_target="tpu_custom_call" | custom-call | bytes 12582912 | tf_op jit(solution)/shard_map/pallas_call | solution.py:681
  98.6 11.1 %all_to_all.22.sums_ref = f32[8,8,512]{2,1,0:T(8,128)S(1)} all-to-all(f32[8,8,512]{2,1,0:T(8,128)S(1)} %get-tuple-element.85), channel_id=1, replica_groups=mesh['seq'=8,'neur'=4] {'seq'}, dimensions={0} | all-to-all | bytes 262144 | tf_op jit(solution)/shard_map/all_to_all | solution.py:608
  111.2 6.7 %shard_map.212 = (bf16[256,512]{1,0:T(8,128)(2,1)S(1)}, bf16[256,512]{1,0:T(8,128)(2,1)S(1)}, bf16[256,512]{1,0:T(8,128)(2,1)S(1)}, bf16[256,512]{1,0:T(8,128)(2...) custom-call(bf16[704,500]{1,0:T(8,128)(2,1)S(1)} %copy-done.20, ...), custom_call_target="tpu_custom_call" | custom-call | flops 1408000000 | bytes 6291456 | tf_op jit(solution)/shard_map/pallas_call | solution.py:638
  123.8 24.9 %collective-permute-done.30 = bf16[256,512]{1,0:T(8,128)(2,1)S(1)} collective-permute-done((bf16[256,512]{1,0:T(8,128)(2,1)S(1)}, bf16[256,512]{1,0:T(8,128)(2,1)S(1)}, u32[]{:S(2)}, u32[]{:S(2)}) %collective-permute-start.30) | collective-permute-done | bytes 262176 | tf_op jit(solution)/shard_map/ppermute | solution.py:543
  152.9 7.1 %collective-permute-done.27 = bf16[256,512]{1,0:T(8,128)(2,1)S(1)} collective-permute-done((bf16[256,512]{1,0:T(8,128)(2,1)S(1)}, bf16[256,512]{1,0:T(8,128)(2,1)S(1)}, u32[]{:S(2)}, u32[]{:S(2)}) %collective-permute-start.27) | collective-permute-done | bytes 262176 | tf_op jit(solution)/shard_map/ppermute | solution.py:543
  160.8 4.8 %collective-permute-done.29 = bf16[256,512]{1,0:T(8,128)(2,1)S(1)} collective-permute-done((bf16[256,512]{1,0:T(8,128)(2,1)S(1)}, bf16[256,512]{1,0:T(8,128)(2,1)S(1)}, u32[]{:S(2)}, u32[]{:S(2)}) %collective-permute-start.29) | collective-permute-done | bytes 262176 | tf_op jit(solution)/shard_map/ppermute | solution.py:543
  165.5 5.6 %collective-permute-done.31 = bf16[256,512]{1,0:T(8,128)(2,1)S(1)} collective-permute-done((bf16[256,512]{1,0:T(8,128)(2,1)S(1)}, bf16[256,512]{1,0:T(8,128)(2,1)S(1)}, u32[]{:S(2)}, u32[]{:S(2)}) %collective-permute-start.31) | collective-permute-done | bytes 262176 | tf_op jit(solution)/shard_map/ppermute | solution.py:543
  175.4 5.2 %shard_map.206 = (f32[704,512]{1,0:T(8,128)S(1)}, f32[8,8,512]{2,1,0:T(8,128)}) custom-call(f32[704,512]{1,0:T(8,128)S(1)} %shard_map.204.keep_ref, bf16[704,512]{1,0:T(8,128)(2,1)S(1)} %collective-permute-done.9.got_ref, f32[704,512]{1,0:T(8,128)} %copy-done, f32[704,512]{1,0:T(8,128)} %copy-done.10, f32[8,512]{1,0:T(8,128)S(1)} %get-tuple-element.83.first_ref.sum_ref, ...), custom_call_target="tpu_custom_call" | custom-call | bytes 10485760 | tf_op jit(solution)/shard_map/pallas_call | solution.py:699
  181.7 3.7 %all-to-all-start.3 = ((f32[8,8,512]{2,1,0:T(8,128)}), f32[8,8,512]{2,1,0:T(8,128)S(1)}, u32[]{:S(2)}, u32[]{:S(2)}) async-start(f32[8,8,512]{2,1,0:T(8,128)} %get-tuple-element.91), calls=%async_computation.3 | async-start | bytes 262144 | tf_op jit(solution)/shard_map/all_to_all | solution.py:608
  188.4 4.2 %all-to-all-done.3.sums_ref = f32[8,8,512]{2,1,0:T(8,128)S(1)} async-done(((f32[8,8,512]{2,1,0:T(8,128)}), f32[8,8,512]{2,1,0:T(8,128)S(1)}, u32[]{:S(2)}, u32[]{:S(2)}) %all-to-all-start.3) | async-done | bytes 131104 | tf_op jit(solution)/shard_map/all_to_all | solution.py:608
  195.5 6.8 %shard_map.210 = (bf16[256,512]{1,0:T(8,128)(2,1)S(1)}, bf16[256,512]{1,0:T(8,128)(2,1)S(1)}, bf16[256,512]{1,0:T(8,128)(2,1)S(1)}, bf16[256,512]{1,0:T(8,128)(2...) custom-call(bf16[704,500]{1,0:T(8,128)(2,1)S(1)} %bitcast.15, ...), custom_call_target="tpu_custom_call" | custom-call | flops 1408000000 | bytes 6291456 | tf_op jit(solution)/shard_map/pallas_call | solution.py:638
  207.6 7.4 %collective-permute-done.16 = bf16[256,512]{1,0:T(8,128)(2,1)S(1)} collective-permute-done((bf16[256,512]{1,0:T(8,128)(2,1)S(1)}, bf16[256,512]{1,0:T(8,128)(2,1)S(1)}, u32[]{:S(2)}, u32[]{:S(2)}) %collective-permute-start.16) | collective-permute-done | bytes 262176 | tf_op jit(solution)/shard_map/ppermute | solution.py:543
  215.2 7.7 %collective-permute-done.34.refs_2_ = bf16[256,512]{1,0:T(8,128)(2,1)S(1)} collective-permute-done((bf16[256,512]{1,0:T(8,128)(2,1)S(1)}, bf16[256,512]{1,0:T(8,128)(2,1)S(1)}, u32[]{:S(2)}, u32[]{:S(2)}) %collective-permute-start.34) | collective-permute-done | bytes 262176 | tf_op jit(solution)/shard_map/ppermute | solution.py:543
  222.9 5.8 %collective-permute-done.35.refs_3_ = bf16[256,512]{1,0:T(8,128)(2,1)S(1)} collective-permute-done((bf16[256,512]{1,0:T(8,128)(2,1)S(1)}, bf16[256,512]{1,0:T(8,128)(2,1)S(1)}, u32[]{:S(2)}, u32[]{:S(2)}) %collective-permute-start.35) | collective-permute-done | bytes 262176 | tf_op jit(solution)/shard_map/ppermute | solution.py:543
  231.7 28.3 %collective-permute-done.15 = bf16[256,512]{1,0:T(8,128)(2,1)S(1)} collective-permute-done((bf16[256,512]{1,0:T(8,128)(2,1)S(1)}, bf16[256,512]{1,0:T(8,128)(2,1)S(1)}, u32[]{:S(2)}, u32[]{:S(2)}) %collective-permute-start.15) | collective-permute-done | bytes 262176 | tf_op jit(solution)/shard_map/ppermute | solution.py:543
  260.0 3.0 collective-permute-start.39
  263.1 8.1 %collective-permute-done.36.refs_4_ = bf16[256,512]{1,0:T(8,128)(2,1)S(1)} collective-permute-done((bf16[256,512]{1,0:T(8,128)(2,1)S(1)}, bf16[256,512]{1,0:T(8,128)(2,1)S(1)}, u32[]{:S(2)}, u32[]{:S(2)}) %collective-permute-start.36) | collective-permute-done | bytes 262176 | tf_op jit(solution)/shard_map/ppermute | solution.py:543
  271.2 11.2 %collective-permute-done.38.refs_6_ = bf16[256,512]{1,0:T(8,128)(2,1)S(1)} collective-permute-done((bf16[256,512]{1,0:T(8,128)(2,1)S(1)}, bf16[256,512]{1,0:T(8,128)(2,1)S(1)}, u32[]{:S(2)}, u32[]{:S(2)}) %collective-permute-start.38) | collective-permute-done | bytes 262176 | tf_op jit(solution)/shard_map/ppermute | solution.py:543
  283.9 4.3 %collective-permute-done.39.refs_7_ = bf16[256,512]{1,0:T(8,128)(2,1)S(1)} collective-permute-done((bf16[256,512]{1,0:T(8,128)(2,1)S(1)}, bf16[256,512]{1,0:T(8,128)(2,1)S(1)}, u32[]{:S(2)}, u32[]{:S(2)}) %collective-permute-start.39) | collective-permute-done | bytes 262176 | tf_op jit(solution)/shard_map/ppermute | solution.py:543
  293.6 5.5 %collective-permute-done.14 = bf16[256,512]{1,0:T(8,128)(2,1)S(1)} collective-permute-done((bf16[256,512]{1,0:T(8,128)(2,1)S(1)}, bf16[256,512]{1,0:T(8,128)(2,1)S(1)}, u32[]{:S(2)}, u32[]{:S(2)}) %collective-permute-start.14) | collective-permute-done | bytes 262176 | tf_op jit(solution)/shard_map/ppermute | solution.py:543
  300.8 6.8 %collective-permute-done.19.refs_1_ = bf16[256,512]{1,0:T(8,128)(2,1)S(1)} collective-permute-done((bf16[256,512]{1,0:T(8,128)(2,1)S(1)}, bf16[256,512]{1,0:T(8,128)(2,1)S(1)}, u32[]{:S(2)}, u32[]{:S(2)}) %collective-permute-start.19) | collective-permute-done | bytes 262176 | tf_op jit(solution)/shard_map/ppermute | solution.py:543
  318.6 24.9 %collective-permute-done.22.refs_4_ = bf16[256,512]{1,0:T(8,128)(2,1)S(1)} collective-permute-done((bf16[256,512]{1,0:T(8,128)(2,1)S(1)}, bf16[256,512]{1,0:T(8,128)(2,1)S(1)}, u32[]{:S(2)}, u32[]{:S(2)}) %collective-permute-start.22) | collective-permute-done | bytes 262176 | tf_op jit(solution)/shard_map/ppermute | solution.py:543
  343.5 11.2 %collective-permute-done.24.refs_6_ = bf16[256,512]{1,0:T(8,128)(2,1)S(1)} collective-permute-done((bf16[256,512]{1,0:T(8,128)(2,1)S(1)}, bf16[256,512]{1,0:T(8,128)(2,1)S(1)}, u32[]{:S(2)}, u32[]{:S(2)}) %collective-permute-start.24) | collective-permute-done | bytes 262176 | tf_op jit(solution)/shard_map/ppermute | solution.py:543
  354.7 4.3 %collective-permute-done.25.refs_7_ = bf16[256,512]{1,0:T(8,128)(2,1)S(1)} collective-permute-done((bf16[256,512]{1,0:T(8,128)(2,1)S(1)}, bf16[256,512]{1,0:T(8,128)(2,1)S(1)}, u32[]{:S(2)}, u32[]{:S(2)}) %collective-permute-start.25) | collective-permute-done | bytes 262176 | tf_op jit(solution)/shard_map/ppermute | solution.py:543
  (155 shorter events, 77.3 us)
Async XLA Ops:
  3.8 22.0 %collective-permute-start.2 = (bf16[2,512,512]{2,1,0:T(8,128)(2,1)S(1)}, bf16[2,512,512]{2,1,0:T(8,128)(2,1)S(1)}, u32[]{:S(2)}, u32[]{:S(2)}) collective-permute-start(bf16[2,512,512]{2,1,0:T(8,128)(2,1)S(1)} %get-tuple-element.66), channel_id=1, source_target_pairs={{0,1},{1,0},{2,3},{3,2},{4,5},{5,4},{6,7},{7,6},{8,9},{9,8},{10,11... | collective-permute-start | bytes 3145736 | tf_op jit(solution)/shard_map/ppermute | solution.py:543
  6.1 19.8 %collective-permute-start.3 = (bf16[2,512,512]{2,1,0:T(8,128)(2,1)S(1)}, bf16[2,512,512]{2,1,0:T(8,128)(2,1)S(1)}, u32[]{:S(2)}, u32[]{:S(2)}) collective-permute-start(bf16[2,512,512]{2,1,0:T(8,128)(2,1)S(1)} %get-tuple-element.67), channel_id=1, source_target_pairs={{0,1},{1,0},{2,3},{3,2},{4,5},{5,4},{6,7},{7,6},{8,9},{9,8},{10,11... | collective-permute-start | bytes 3145736 | tf_op jit(solution)/shard_map/ppermute | solution.py:543
  6.6 19.2 %collective-permute-start = (bf16[704,500]{1,0:T(8,128)(2,1)S(1)}, bf16[704,500]{1,0:T(8,128)(2,1)S(1)}, u32[]{:S(2)}, u32[]{:S(2)}) collective-permute-start(bf16[704,500]{1,0:T(8,128)(2,1)S(1)} %bitcast.13), channel_id=1, source_target_pairs={{0,2},{1,3},{2,0},{3,1},{4,6},{5,7},{6,4},{7,5},{8,10},{9,11},{10,... | collective-permute-start | bytes 2112008 | tf_op jit(solution)/shard_map/ppermute | solution.py:543
  53.8 18.8 %collective-permute-start.5 = (bf16[704,500]{1,0:T(8,128)(2,1)}, bf16[704,500]{1,0:T(8,128)(2,1)S(1)}, u32[]{:S(2)}, u32[]{:S(2)}) collective-permute-start(bf16[704,500]{1,0:T(8,128)(2,1)} %get-tuple-element.74.own_ref), channel_id=1, source_target_pairs={{0,2},{1,3},{2,0},{3,1},{4,6},{5,7},{6,4},{7,5},{8,10},{9,11},{10,... | collective-permute-start | bytes 2112008 | tf_op jit(solution)/shard_map/ppermute | solution.py:543
  110.3 38.5 %collective-permute-start.8 = (bf16[704,512]{1,0:T(8,128)(2,1)S(1)}, bf16[704,512]{1,0:T(8,128)(2,1)S(1)}, u32[]{:S(2)}, u32[]{:S(2)}) collective-permute-start(bf16[704,512]{1,0:T(8,128)(2,1)S(1)} %get-tuple-element.88.g_ref), channel_id=1, source_target_pairs={{0,1},{1,0},{2,3},{3,2},{4,5},{5,4},{6,7},{7,6},{8,9},{9,8},{10,11... | collective-permute-start | bytes 2162696 | tf_op jit(solution)/shard_map/ppermute | solution.py:543
  117.9 30.8 %collective-permute-start.30 = (bf16[256,512]{1,0:T(8,128)(2,1)S(1)}, bf16[256,512]{1,0:T(8,128)(2,1)S(1)}, u32[]{:S(2)}, u32[]{:S(2)}) collective-permute-start(bf16[256,512]{1,0:T(8,128)(2,1)S(1)} %get-tuple-element.113), channel_id=1, source_target_pairs={{0,16},{4,20},{8,24},{12,28},{16,0},{20,4},{24,8},{28,12},{1,17},{... | collective-permute-start | bytes 786440 | tf_op jit(solution)/shard_map/ppermute | solution.py:543
  118.3 67.1 %collective-permute-start.26 = (bf16[256,512]{1,0:T(8,128)(2,1)S(1)}, bf16[256,512]{1,0:T(8,128)(2,1)S(1)}, u32[]{:S(2)}, u32[]{:S(2)}) collective-permute-start(bf16[256,512]{1,0:T(8,128)(2,1)S(1)} %get-tuple-element.107), channel_id=1, source_target_pairs={{0,16},{4,20},{8,24},{12,28},{16,0},{20,4},{24,8},{28,12},{1,17},{... | collective-permute-start | bytes 786440 | tf_op jit(solution)/shard_map/ppermute | solution.py:543
  120.9 39.1 %collective-permute-start.27 = (bf16[256,512]{1,0:T(8,128)(2,1)S(1)}, bf16[256,512]{1,0:T(8,128)(2,1)S(1)}, u32[]{:S(2)}, u32[]{:S(2)}) collective-permute-start(bf16[256,512]{1,0:T(8,128)(2,1)S(1)} %get-tuple-element.109), channel_id=1, source_target_pairs={{0,16},{4,20},{8,24},{12,28},{16,0},{20,4},{24,8},{28,12},{1,17},{... | collective-permute-start | bytes 786440 | tf_op jit(solution)/shard_map/ppermute | solution.py:543
  121.3 44.2 %collective-permute-start.29 = (bf16[256,512]{1,0:T(8,128)(2,1)S(1)}, bf16[256,512]{1,0:T(8,128)(2,1)S(1)}, u32[]{:S(2)}, u32[]{:S(2)}) collective-permute-start(bf16[256,512]{1,0:T(8,128)(2,1)S(1)} %get-tuple-element.111), channel_id=1, source_target_pairs={{0,16},{4,20},{8,24},{12,28},{16,0},{20,4},{24,8},{28,12},{1,17},{... | collective-permute-start | bytes 786440 | tf_op jit(solution)/shard_map/ppermute | solution.py:543
  148.7 22.4 %collective-permute-start.31 = (bf16[256,512]{1,0:T(8,128)(2,1)S(1)}, bf16[256,512]{1,0:T(8,128)(2,1)S(1)}, u32[]{:S(2)}, u32[]{:S(2)}) collective-permute-start(bf16[256,512]{1,0:T(8,128)(2,1)S(1)} %add_convert_fusion.2), channel_id=1, source_target_pairs={{0,8},{4,12},{8,0},{12,4},{16,24},{20,28},{24,16},{28,20},{1,9},{5... | collective-permute-start | bytes 786440 | tf_op jit(solution)/shard_map/ppermute | solution.py:543
  152.5 22.9 %collective-permute-start.9 = (bf16[704,512]{1,0:T(8,128)(2,1)S(1)}, bf16[704,512]{1,0:T(8,128)(2,1)S(1)}, u32[]{:S(2)}, u32[]{:S(2)}) collective-permute-start(bf16[704,512]{1,0:T(8,128)(2,1)S(1)} %shard_map.205), channel_id=1, source_target_pairs={{0,2},{1,3},{2,0},{3,1},{4,6},{5,7},{6,4},{7,5},{8,10},{9,11},{10,... | collective-permute-start | bytes 2162696 | tf_op jit(solution)/shard_map/ppermute | solution.py:543
  160.8 24.7 %collective-permute-start.28 = (bf16[256,512]{1,0:T(8,128)(2,1)}, bf16[256,512]{1,0:T(8,128)(2,1)}, u32[]{:S(2)}, u32[]{:S(2)}) collective-permute-start(bf16[256,512]{1,0:T(8,128)(2,1)} %add_convert_fusion.5), channel_id=1, source_target_pairs={{0,8},{4,12},{8,0},{12,4},{16,24},{20,28},{24,16},{28,20},{1,9},{5... | collective-permute-start | bytes 786440 | tf_op jit(solution)/shard_map/ppermute | solution.py:543
  171.9 13.6 %collective-permute-start.32 = (bf16[256,512]{1,0:T(8,128)(2,1)}, bf16[256,512]{1,0:T(8,128)(2,1)}, u32[]{:S(2)}, u32[]{:S(2)}) collective-permute-start(bf16[256,512]{1,0:T(8,128)(2,1)} %add_convert_fusion.1), channel_id=1, source_target_pairs={{0,4},{4,0},{8,12},{12,8},{16,20},{20,16},{24,28},{28,24},{1,5},{5... | collective-permute-start | bytes 786440 | tf_op jit(solution)/shard_map/ppermute | solution.py:543
  186.7 16.9 %collective-permute-start.33 = (bf16[256,512]{1,0:T(8,128)(2,1)S(1)}, bf16[256,512]{1,0:T(8,128)(2,1)S(1)}, u32[]{:S(2)}, u32[]{:S(2)}) collective-permute-start(bf16[256,512]{1,0:T(8,128)(2,1)S(1)} %add_convert_fusion.refs_0_), channel_id=1, source_target_pairs={{0,4},{4,0},{8,12},{12,8},{16,20},{20,16},{24,28},{28,24},{1,5},{5... | collective-permute-start | bytes 786440 | tf_op jit(solution)/shard_map/ppermute | solution.py:543
  202.6 20.3 %collective-permute-start.34 = (bf16[256,512]{1,0:T(8,128)(2,1)S(1)}, bf16[256,512]{1,0:T(8,128)(2,1)S(1)}, u32[]{:S(2)}, u32[]{:S(2)}) collective-permute-start(bf16[256,512]{1,0:T(8,128)(2,1)S(1)} %add_convert_fusion.refs_0_), channel_id=1, source_target_pairs={{0,8},{4,12},{8,0},{12,4},{16,24},{20,28},{24,16},{28,20},{1,9},{5... | collective-permute-start | bytes 786440 | tf_op jit(solution)/shard_map/ppermute | solution.py:543
  203.5 25.2 %collective-permute-start.35 = (bf16[256,512]{1,0:T(8,128)(2,1)S(1)}, bf16[256,512]{1,0:T(8,128)(2,1)S(1)}, u32[]{:S(2)}, u32[]{:S(2)}) collective-permute-start(bf16[256,512]{1,0:T(8,128)(2,1)S(1)} %collective-permute-done.33.refs_1_), channel_id=1, source_target_pairs={{0,8},{4,12},{8,0},{12,4},{16,24},{20,28},{24,16},{28,20},{1,9},{5... | collective-permute-start | bytes 786440 | tf_op jit(solution)/shard_map/ppermute | solution.py:543
  204.7 24.6 %collective-permute-start.13 = (bf16[256,512]{1,0:T(8,128)(2,1)S(1)}, bf16[256,512]{1,0:T(8,128)(2,1)S(1)}, u32[]{:S(2)}, u32[]{:S(2)}) collective-permute-start(bf16[256,512]{1,0:T(8,128)(2,1)S(1)} %get-tuple-element.100), channel_id=1, source_target_pairs={{0,16},{4,20},{8,24},{12,28},{16,0},{20,4},{24,8},{28,12},{1,17},{... | collective-permute-start | bytes 786440 | tf_op jit(solution)/shard_map/ppermute | solution.py:543
  207.3 52.6 %collective-permute-start.15 = (bf16[256,512]{1,0:T(8,128)(2,1)S(1)}, bf16[256,512]{1,0:T(8,128)(2,1)S(1)}, u32[]{:S(2)}, u32[]{:S(2)}) collective-permute-start(bf16[256,512]{1,0:T(8,128)(2,1)S(1)} %get-tuple-element.102), channel_id=1, source_target_pairs={{0,16},{4,20},{8,24},{12,28},{16,0},{20,4},{24,8},{28,12},{1,17},{... | collective-permute-start | bytes 786440 | tf_op jit(solution)/shard_map/ppermute | solution.py:543
  215.1 44.9 %collective-permute-start.17 = (bf16[256,512]{1,0:T(8,128)(2,1)S(1)}, bf16[256,512]{1,0:T(8,128)(2,1)S(1)}, u32[]{:S(2)}, u32[]{:S(2)}) collective-permute-start(bf16[256,512]{1,0:T(8,128)(2,1)S(1)} %add_convert_fusion.9), channel_id=1, source_target_pairs={{0,8},{4,12},{8,0},{12,4},{16,24},{20,28},{24,16},{28,20},{1,9},{5... | collective-permute-start | bytes 786440 | tf_op jit(solution)/shard_map/ppermute | solution.py:543
  222.9 67.6 %collective-permute-start.10 = (bf16[704,512]{1,0:T(8,128)(2,1)S(1)}, bf16[704,512]{1,0:T(8,128)(2,1)S(1)}, u32[]{:S(2)}, u32[]{:S(2)}) collective-permute-start(bf16[704,512]{1,0:T(8,128)(2,1)S(1)} %copy-done.3), channel_id=1, source_target_pairs={{0,1},{1,0},{2,3},{3,2},{4,5},{5,4},{6,7},{7,6},{8,9},{9,8},{10,11... | collective-permute-start | bytes 2162696 | tf_op jit(solution)/shard_map/ppermute | solution.py:543
  228.7 42.4 %collective-permute-start.36 = (bf16[256,512]{1,0:T(8,128)(2,1)S(1)}, bf16[256,512]{1,0:T(8,128)(2,1)S(1)}, u32[]{:S(2)}, u32[]{:S(2)}) collective-permute-start(bf16[256,512]{1,0:T(8,128)(2,1)S(1)} %add_convert_fusion.refs_0_), channel_id=1, source_target_pairs={{0,16},{4,20},{8,24},{12,28},{16,0},{20,4},{24,8},{28,12},{1,17},{... | collective-permute-start | bytes 786440 | tf_op jit(solution)/shard_map/ppermute | solution.py:543
  229.3 53.1 %collective-permute-start.37 = (bf16[256,512]{1,0:T(8,128)(2,1)S(1)}, bf16[256,512]{1,0:T(8,128)(2,1)S(1)}, u32[]{:S(2)}, u32[]{:S(2)}) collective-permute-start(bf16[256,512]{1,0:T(8,128)(2,1)S(1)} %collective-permute-done.33.refs_1_), channel_id=1, source_target_pairs={{0,16},{4,20},{8,24},{12,28},{16,0},{20,4},{24,8},{28,12},{1,17},{... | collective-permute-start | bytes 786440 | tf_op jit(solution)/shard_map/ppermute | solution.py:543
  259.9 22.5 %collective-permute-start.38 = (bf16[256,512]{1,0:T(8,128)(2,1)S(1)}, bf16[256,512]{1,0:T(8,128)(2,1)S(1)}, u32[]{:S(2)}, u32[]{:S(2)}) collective-permute-start(bf16[256,512]{1,0:T(8,128)(2,1)S(1)} %collective-permute-done.34.refs_2_), channel_id=1, source_target_pairs={{0,16},{4,20},{8,24},{12,28},{16,0},{20,4},{24,8},{28,12},{1,17},{... | collective-permute-start | bytes 786440 | tf_op jit(solution)/shard_map/ppermute | solution.py:543
  260.0 28.1 %collective-permute-start.39 = (bf16[256,512]{1,0:T(8,128)(2,1)S(1)}, bf16[256,512]{1,0:T(8,128)(2,1)S(1)}, u32[]{:S(2)}, u32[]{:S(2)}) collective-permute-start(bf16[256,512]{1,0:T(8,128)(2,1)S(1)} %collective-permute-done.35.refs_3_), channel_id=1, source_target_pairs={{0,16},{4,20},{8,24},{12,28},{16,0},{20,4},{24,8},{28,12},{1,17},{... | collective-permute-start | bytes 786440 | tf_op jit(solution)/shard_map/ppermute | solution.py:543
  271.2 22.5 %collective-permute-start.12 = (bf16[256,512]{1,0:T(8,128)(2,1)S(1)}, bf16[256,512]{1,0:T(8,128)(2,1)S(1)}, u32[]{:S(2)}, u32[]{:S(2)}) collective-permute-start(bf16[256,512]{1,0:T(8,128)(2,1)S(1)} %get-tuple-element.98), channel_id=1, source_target_pairs={{0,16},{4,20},{8,24},{12,28},{16,0},{20,4},{24,8},{28,12},{1,17},{... | collective-permute-start | bytes 786440 | tf_op jit(solution)/shard_map/ppermute | solution.py:543
  282.4 16.7 %collective-permute-start.14 = (bf16[256,512]{1,0:T(8,128)(2,1)S(1)}, bf16[256,512]{1,0:T(8,128)(2,1)S(1)}, u32[]{:S(2)}, u32[]{:S(2)}) collective-permute-start(bf16[256,512]{1,0:T(8,128)(2,1)S(1)} %add_convert_fusion.12), channel_id=1, source_target_pairs={{0,8},{4,12},{8,0},{12,4},{16,24},{20,28},{24,16},{28,20},{1,9},{5... | collective-permute-start | bytes 786440 | tf_op jit(solution)/shard_map/ppermute | solution.py:543
  282.4 16.7 %collective-permute-start.18 = (bf16[256,512]{1,0:T(8,128)(2,1)S(1)}, bf16[256,512]{1,0:T(8,128)(2,1)S(1)}, u32[]{:S(2)}, u32[]{:S(2)}) collective-permute-start(bf16[256,512]{1,0:T(8,128)(2,1)S(1)} %add_convert_fusion.8), channel_id=1, source_target_pairs={{0,4},{4,0},{8,12},{12,8},{16,20},{20,16},{24,28},{28,24},{1,5},{5... | collective-permute-start | bytes 786440 | tf_op jit(solution)/shard_map/ppermute | solution.py:543
  293.1 24.1 %collective-permute-start.11 = (bf16[704,512]{1,0:T(8,128)(2,1)S(1)}, bf16[704,512]{1,0:T(8,128)(2,1)S(1)}, u32[]{:S(2)}, u32[]{:S(2)}) collective-permute-start(bf16[704,512]{1,0:T(8,128)(2,1)S(1)} %shard_map.209), channel_id=1, source_target_pairs={{0,2},{1,3},{2,0},{3,1},{4,6},{5,7},{6,4},{7,5},{8,10},{9,11},{10,... | collective-permute-start | bytes 2162696 | tf_op jit(solution)/shard_map/ppermute | solution.py:543
  311.3 32.2 %collective-permute-start.22 = (bf16[256,512]{1,0:T(8,128)(2,1)S(1)}, bf16[256,512]{1,0:T(8,128)(2,1)S(1)}, u32[]{:S(2)}, u32[]{:S(2)}) collective-permute-start(bf16[256,512]{1,0:T(8,128)(2,1)S(1)} %add_convert_fusion.7.refs_0_), channel_id=1, source_target_pairs={{0,16},{4,20},{8,24},{12,28},{16,0},{20,4},{24,8},{28,12},{1,17},{... | collective-permute-start | bytes 786440 | tf_op jit(solution)/shard_map/ppermute | solution.py:543
  313.9 40.8 %collective-permute-start.23 = (bf16[256,512]{1,0:T(8,128)(2,1)S(1)}, bf16[256,512]{1,0:T(8,128)(2,1)S(1)}, u32[]{:S(2)}, u32[]{:S(2)}) collective-permute-start(bf16[256,512]{1,0:T(8,128)(2,1)S(1)} %collective-permute-done.19.refs_1_), channel_id=1, source_target_pairs={{0,16},{4,20},{8,24},{12,28},{16,0},{20,4},{24,8},{28,12},{1,17},{... | collective-permute-start | bytes 786440 | tf_op jit(solution)/shard_map/ppermute | solution.py:543
  314.3 40.4 %collective-permute-start.24 = (bf16[256,512]{1,0:T(8,128)(2,1)S(1)}, bf16[256,512]{1,0:T(8,128)(2,1)S(1)}, u32[]{:S(2)}, u32[]{:S(2)}) collective-permute-start(bf16[256,512]{1,0:T(8,128)(2,1)S(1)} %collective-permute-done.20.refs_2_), channel_id=1, source_target_pairs={{0,16},{4,20},{8,24},{12,28},{16,0},{20,4},{24,8},{28,12},{1,17},{... | collective-permute-start | bytes 786440 | tf_op jit(solution)/shard_map/ppermute | solution.py:543
  316.8 42.2 %collective-permute-start.25 = (bf16[256,512]{1,0:T(8,128)(2,1)S(1)}, bf16[256,512]{1,0:T(8,128)(2,1)S(1)}, u32[]{:S(2)}, u32[]{:S(2)}) collective-permute-start(bf16[256,512]{1,0:T(8,128)(2,1)S(1)} %collective-permute-done.21.refs_3_), channel_id=1, source_target_pairs={{0,16},{4,20},{8,24},{12,28},{16,0},{20,4},{24,8},{28,12},{1,17},{... | collective-permute-start | bytes 786440 | tf_op jit(solution)/shard_map/ppermute | solution.py:543
  (43 other events, 294.5 us)
where the time goes:
time: 362 us; the launch traced here: 361 us
  waiting for transfers between devices  201 us (56%)
  Pallas kernels  68.8 us (19%)
  starting transfers between devices  38.1 us (11%)
  blocking collectives  34.3 us (9%)
  local copies, waits for them, and re-layouts  11.5 us (3%)
  other arithmetic  6.31 us (2%)
    ppermute x40, waiting for transfers between devices, swap(): return lax.ppermute(x, axis, [(i, i ^ bit) for i in range(n)])  197 us
    ppermute x40, starting transfers between devices, swap(): return lax.ppermute(x, axis, [(i, i ^ bit) for i in range(n)])  34.4 us
    all_to_all x3, blocking collectives, share(): return lax.all_to_all(stats, 'seq', 0, 0, tiled=True)  34.3 us
    pallas_call x2, Pallas kernels, weights(): call(weight_kernel, [shape(half, width, dtype=BF16)] * 8, [pltpu.VMEM((8,...  13.5 us
    unnamed x68, local copies, waits for them, and re-layouts  11.5 us
    pallas_call x1, Pallas kernels, per_device(): call(turn_kernel, [shape(length, real, dtype=BF16), shape(length, width),...  10.2 us
    pallas_call x1, Pallas kernels, per_device(): call(forward_kernel, [shape(length, real, dtype=BF16), shape(length, widt...  7.71 us
  transfers between devices with their start and end apart: 41, of which 25 were waited for; matrix products, arithmetic and copies ran while one was open for 2% of the time, Pallas kernels for 11%

commit v1 on v0

--- a/solution.py
+++ b/solution.py
@@ -27,7 +27,7 @@
         out_shape=outs,
         scratch_shapes=list(scratch),
         compiler_params=pltpu.CompilerParams(vmem_limit_bytes=VMEM_BYTES),
-        cost_estimate=pl.CostEstimate(flops=flops, bytes_accessed=nbytes, transcendentals=0),
+        cost_estimate=pl.CostEstimate(flops=1, bytes_accessed=1, transcendentals=0),
     )
 
 
@@ -501,7 +501,7 @@
 
 def weight_kernel(own_ref, mate_ref, far_ref, cross_ref, g_ref, sum_ref, total_ref, *refs):
     outs, hold = refs[:-1], refs[-1]
-    place = lax.axis_index("seq") & 7
+    place = seat()
     half, width = outs[0].shape
     alone = lax.broadcasted_iota(jnp.int32, (8, width), 0) == 0
     summed = jnp.where(alone, total_ref[7:8, :], 0.0)
@@ -521,7 +521,7 @@
 
 def spread_kernel(*refs):
     shares, out_ref, hold = refs[:-2], refs[-2], refs[-1]
-    place, here = lax.axis_index("seq") & 7, lax.axis_index("neur")
+    place, here = seat(), lax.axis_index("neur")
     for r, share in enumerate(shares):
         hold[r] = share[...]
     half = shares[0].shape[0]
@@ -543,24 +543,32 @@
     return lax.ppermute(x, axis, [(i, i ^ bit) for i in range(n)])
 
 
+LEVEL = {4: 1, 2: 2, 1: 4}
+
+
+def seat():
+    place = lax.axis_index("seq")
+    return ((place & 1) << 2) | (place & 2) | ((place >> 2) & 1)
+
+
 def reduce_shares(shares):
     part = {(r >> 2 & 1, r >> 1 & 1, r & 1): v for r, v in enumerate(shares)}
-    got = {q: swap(part[(1,) + q], 4) for q in ((1, 1), (1, 0), (0, 1), (0, 0))}
+    got = {q: swap(part[(1,) + q], LEVEL[4]) for q in ((1, 1), (1, 0), (0, 1), (0, 0))}
     mine = {q: half_sum(part[(0,) + q], v) for q, v in got.items()}
-    first = half_sum(mine[(0, 1)], swap(mine[(1, 1)], 2))
-    last = half_sum(mine[(0, 0)], swap(mine[(1, 0)], 2))
-    return half_sum(last, swap(first, 1))
+    first = half_sum(mine[(0, 1)], swap(mine[(1, 1)], LEVEL[2]))
+    last = half_sum(mine[(0, 0)], swap(mine[(1, 0)], LEVEL[2]))
+    return half_sum(last, swap(first, LEVEL[1]))
 
 
 def gather_shares(v):
     out = {0: v}
-    out[1] = swap(v, 1)
-    out[2] = swap(v, 2)
-    out[4] = swap(v, 4)
-    out[3] = swap(out[1], 2)
-    out[6] = swap(out[2], 4)
-    out[5] = swap(out[1], 4)
-    out[7] = swap(out[3], 4)
+    out[1] = swap(v, LEVEL[1])
+    out[2] = swap(v, LEVEL[2])
+    out[4] = swap(v, LEVEL[4])
+    out[3] = swap(out[1], LEVEL[2])
+    out[6] = swap(out[2], LEVEL[4])
+    out[5] = swap(out[1], LEVEL[4])
+    out[7] = swap(out[3], LEVEL[4])
     return [out[r] for r in range(8)]
 
 

time: 362 us -> 240 us (0.66)
  waiting for transfers between devices: 201 us -> 86.5 us
  starting transfers between devices: 38.1 us -> 26.5 us
  blocking collectives: 34.3 us -> 44.3 us
    ppermute x40, waiting for transfers between devices: 197 us -> 86.5 us  [swap(): return lax.ppermute(x, axis, [(i, i ^ bit) for i in range(n)])]
    all_to_all x3 -> x4, blocking collectives: 34.3 us -> 44.3 us  [share(): return lax.all_to_all(stats, 'seq', 0, 0, tiled=True)]
    ppermute x40, starting transfers between devices: 34.4 us -> 26.5 us  [swap(): return lax.ppermute(x, axis, [(i, i ^ bit) for i in range(n)])]
    all_to_all x1 -> x0, waiting for transfers between devices: 4.21 us -> none  [share(): return lax.all_to_all(stats, 'seq', 0, 0, tiled=True)]
    all_to_all x1 -> x0, starting transfers between devices: 3.72 us -> none  [share(): return lax.all_to_all(stats, 'seq', 0, 0, tiled=True)]
    unnamed x68 -> x54, local copies, waits for them, and re-layouts: 11.5 us -> 8.99 us
  transfers between devices with their start and end apart: 41 -> 40, of which waited for: 25 -> 22; matrix products, arithmetic and copies ran while one was open for 2% -> 2% of each run, Pallas kernels for 11% -> 16%
where the time goes in v1:
time: 240 us; the launch traced here: 239 us
  waiting for transfers between devices  86.5 us (36%)
  Pallas kernels  67.9 us (28%)
  blocking collectives  44.3 us (18%)
  starting transfers between devices  26.5 us (11%)
  local copies, waits for them, and re-layouts  9 us (4%)
  other arithmetic  3.89 us (2%)
    ppermute x40, waiting for transfers between devices, swap(): return lax.ppermute(x, axis, [(i, i ^ bit) for i in range(n)])  86.5 us
    all_to_all x4, blocking collectives, share(): return lax.all_to_all(stats, 'seq', 0, 0, tiled=True)  44.3 us
    ppermute x40, starting transfers between devices, swap(): return lax.ppermute(x, axis, [(i, i ^ bit) for i in range(n)])  26.5 us
    pallas_call x2, Pallas kernels, weights(): call(weight_kernel, [shape(half, width, dtype=BF16)] * 8, [pltpu.VMEM((8,...  13.4 us
    pallas_call x1, Pallas kernels, per_device(): call(turn_kernel, [shape(length, real, dtype=BF16), shape(length, width),...  10.2 us
    unnamed x54, local copies, waits for them, and re-layouts  8.99 us
    pallas_call x1, Pallas kernels, per_device(): call(forward_kernel, [shape(length, real, dtype=BF16), shape(length, widt...  7.71 us
    pallas_call x2, Pallas kernels, project(): call(project_late, [shape(length, width), shape(peers, 8, width)], flops=...  7.21 us
  transfers between devices with their start and end apart: 40, of which 22 were waited for; matrix products, arithmetic and copies ran while one was open for 2% of the time, Pallas kernels for 16%

profile of v1, /device:TPU:0, one launch (start us, length us, event | category | flops | bytes accessed | tf_op | source)
XLA Modules:
  0.0 239.2 jit_solution(6057284605792081739)
XLA Ops:
  6.6 2.9 %collective-permute-start = (bf16[704,500]{1,0:T(8,128)(2,1)S(1)}, bf16[704,500]{1,0:T(8,128)(2,1)S(1)}, u32[]{:S(2)}, u32[]{:S(2)}) collective-permute-start(bf16[704,500]{1,0:T(8,128)(2,1)S(1)} %bitcast.13), channel_id=1, source_target_pairs={{0,2},{1,3},{2,0},{3,1},{4,6},{5,7},{6,4},{7,5},{8,10},{9,11},{10,... | collective-permute-start | bytes 2112008 | tf_op jit(solution)/shard_map/ppermute | solution.py:543
  9.9 2.7 %shard_map.196 = (f32[704,512]{1,0:T(8,128)S(1)}, f32[8,512]{1,0:T(8,128)S(1)}) custom-call(bf16[704,500]{1,0:T(8,128)(2,1)S(1)} %bitcast.14, bf16[704,500]{1,0:T(8,128)(2,1)S(1)} %collective-permute-done.1.mate_ref, bf16[4,512,512]{2,1,0:T(8,128)(2,1)} %get-tuple-element.94.w_ref), custom_call_target="tpu_custom_call" | custom-call | flops 1 | bytes 1 | tf_op jit(solution)/shard_map/pallas_call | solution.py:622
  13.7 12.2 %collective-permute-done.far_ref = bf16[704,500]{1,0:T(8,128)(2,1)S(1)} collective-permute-done((bf16[704,500]{1,0:T(8,128)(2,1)S(1)}, bf16[704,500]{1,0:T(8,128)(2,1)S(1)}, u32[]{:S(2)}, u32[]{:S(2)}) %collective-permute-start) | collective-permute-done | bytes 704032 | tf_op jit(solution)/shard_map/ppermute | solution.py:543
  28.1 3.6 %shard_map.198 = (f32[704,512]{1,0:T(8,128)S(1)}, f32[8,8,512]{2,1,0:T(8,128)S(1)}) custom-call(f32[704,512]{1,0:T(8,128)} %copy-done.16, f32[8,512]{1,0:T(8,128)S(1)} %get-tuple-element.69.means_ref, bf16[704,500]{1,0:T(8,128)(2,1)S(1)} %collective-permute-done.far_ref, bf16[704,500]{1,0:T(8,128)(2,1)S(1)} %collective-permute-done.4.cross_ref, ...), custom_call_target="tpu_custom_call" | custom-call | flops 1 | bytes 1 | tf_op jit(solution)/shard_map/pallas_call | solution.py:627
  31.8 13.2 %all_to_all.20.stats_ref = f32[8,8,512]{2,1,0:T(8,128)S(1)} all-to-all(f32[8,8,512]{2,1,0:T(8,128)S(1)} %get-tuple-element.71), channel_id=1, replica_groups=mesh['seq'=8,'neur'=4] {'seq'}, dimensions={0} | all-to-all | bytes 262144 | tf_op jit(solution)/shard_map/all_to_all | solution.py:616
  45.0 7.7 %shard_map.199 = (bf16[704,500]{1,0:T(8,128)(2,1)}, f32[704,512]{1,0:T(8,128)S(1)}, f32[8,512]{1,0:T(8,128)S(1)}) custom-call(f32[8,8,512]{2,1,0:T(8,128)S(1)} %all_to_all.20.stats_ref, f32[704,512]{1,0:T(8,128)S(1)} %get-tuple-element.72.proj_ref, f32[8,512]{1,0:T(8,128)S(1)} %get-tuple-element.73.par_ref), custom_call_target="tpu_custom_call" | custom-call | flops 1 | bytes 1 | tf_op jit(solution)/shard_map/pallas_call | solution.py:681
  57.3 2.7 %shard_map.200 = (f32[704,512]{1,0:T(8,128)S(1)}, f32[8,512]{1,0:T(8,128)S(1)}) custom-call(bf16[704,500]{1,0:T(8,128)(2,1)S(1)} %copy-done.11, bf16[704,500]{1,0:T(8,128)(2,1)S(1)} %collective-permute-done.6.mate_ref, bf16[4,512,512]{2,1,0:T(8,128)(2,1)} %get-tuple-element.75.w_ref), custom_call_target="tpu_custom_call" | custom-call | flops 1 | bytes 1 | tf_op jit(solution)/shard_map/pallas_call | solution.py:622
  61.1 11.5 %collective-permute-done.5.far_ref = bf16[704,500]{1,0:T(8,128)(2,1)S(1)} collective-permute-done((bf16[704,500]{1,0:T(8,128)(2,1)}, bf16[704,500]{1,0:T(8,128)(2,1)S(1)}, u32[]{:S(2)}, u32[]{:S(2)}) %collective-permute-start.5) | collective-permute-done | bytes 704032 | tf_op jit(solution)/shard_map/ppermute | solution.py:543
  74.8 3.6 %shard_map.201 = (f32[704,512]{1,0:T(8,128)S(1)}, f32[8,8,512]{2,1,0:T(8,128)S(1)}) custom-call(f32[704,512]{1,0:T(8,128)} %copy-done.17, f32[8,512]{1,0:T(8,128)S(1)} %get-tuple-element.78.means_ref, bf16[704,500]{1,0:T(8,128)(2,1)S(1)} %collective-permute-done.5.far_ref, bf16[704,500]{1,0:T(8,128)(2,1)S(1)} %collective-permute-done.7.cross_ref, ...), custom_call_target="tpu_custom_call" | custom-call | flops 1 | bytes 1 | tf_op jit(solution)/shard_map/pallas_call | solution.py:627
  78.4 10.2 %all_to_all.21.stats_ref = f32[8,8,512]{2,1,0:T(8,128)S(1)} all-to-all(f32[8,8,512]{2,1,0:T(8,128)S(1)} %get-tuple-element.80), channel_id=1, replica_groups=mesh['seq'=8,'neur'=4] {'seq'}, dimensions={0} | all-to-all | bytes 262144 | tf_op jit(solution)/shard_map/all_to_all | solution.py:616
  88.6 10.2 %shard_map.202 = (bf16[704,500]{1,0:T(8,128)(2,1)}, f32[704,512]{1,0:T(8,128)S(1)}, f32[8,8,512]{2,1,0:T(8,128)S(1)}, f32[8,512]{1,0:T(8,128)S(1)}, f32[2,500]{1,0:T(2,128)}, /*index=5*/f32[2,500]{1,0:T(2,128)}) custom-call(f32[8,8,512]{2,1,0:T(8,128)S(1)} %all_to_all.21.stats_ref, f32[704,512]{1,0:T(8,128)S(1)} %get-tuple-element.81.proj_ref, ...), custom_call_target="tpu_custom_call" | custom-call | flops 1 | bytes 1 | tf_op jit(solution)/shard_map/pallas_call | solution.py:689
  98.8 9.8 %all_to_all.22.sums_ref = f32[8,8,512]{2,1,0:T(8,128)S(1)} all-to-all(f32[8,8,512]{2,1,0:T(8,128)S(1)} %get-tuple-element.85), channel_id=1, replica_groups=mesh['seq'=8,'neur'=4] {'seq'}, dimensions={0} | all-to-all | bytes 262144 | tf_op jit(solution)/shard_map/all_to_all | solution.py:616
  110.0 6.7 %shard_map.212 = (bf16[256,512]{1,0:T(8,128)(2,1)S(1)}, bf16[256,512]{1,0:T(8,128)(2,1)S(1)}, bf16[256,512]{1,0:T(8,128)(2,1)S(1)}, bf16[256,512]{1,0:T(8,128)(2...) custom-call(bf16[704,500]{1,0:T(8,128)(2,1)S(1)} %copy-done.12, ...), custom_call_target="tpu_custom_call" | custom-call | flops 1 | bytes 1 | tf_op jit(solution)/shard_map/pallas_call | solution.py:646
  120.2 2.5 %shard_map.205 = bf16[704,512]{1,0:T(8,128)(2,1)S(1)} custom-call(bf16[704,512]{1,0:T(8,128)(2,1)S(1)} %copy-done.5, bf16[704,512]{1,0:T(8,128)(2,1)S(1)} %collective-permute-done.8.mate_ref, bf16[4,512,512]{2,1,0:T(8,128)(2,1)} %get-tuple-element.75.w_ref, bf16[2,512,512]{2,1,0:T(8,128)(2,1)S(1)} %collective-permute-done.3.wmate_ref), custom_call_target="tpu_custom_call" | custom-call | flops 1 | bytes 1 | tf_op jit(solution)/shard_map/pallas_call | solution.py:637
  127.5 4.2 %collective-permute-done.27 = bf16[256,512]{1,0:T(8,128)(2,1)S(1)} collective-permute-done((bf16[256,512]{1,0:T(8,128)(2,1)S(1)}, bf16[256,512]{1,0:T(8,128)(2,1)S(1)}, u32[]{:S(2)}, u32[]{:S(2)}) %collective-permute-start.27) | collective-permute-done | bytes 262176 | tf_op jit(solution)/shard_map/ppermute | solution.py:543
  131.8 5.5 %collective-permute-done.29 = bf16[256,512]{1,0:T(8,128)(2,1)S(1)} collective-permute-done((bf16[256,512]{1,0:T(8,128)(2,1)S(1)}, bf16[256,512]{1,0:T(8,128)(2,1)S(1)}, u32[]{:S(2)}, u32[]{:S(2)}) %collective-permute-start.29) | collective-permute-done | bytes 262176 | tf_op jit(solution)/shard_map/ppermute | solution.py:543
  137.8 2.5 %shard_map.204.keep_ref = f32[704,512]{1,0:T(8,128)S(1)} custom-call(bf16[704,512]{1,0:T(8,128)(2,1)S(1)} %copy-done.5, bf16[704,512]{1,0:T(8,128)(2,1)S(1)} %collective-permute-done.8.mate_ref, bf16[4,512,512]{2,1,0:T(8,128)(2,1)} %get-tuple-element.75.w_ref, bf16[2,512,512]{2,1,0:T(8,128)(2,1)S(1)} %collective-permute-done.3.wmate_ref), custom_call_target="tpu_custom_call" | custom-call | flops 1 | bytes 1 | tf_op jit(solution)/shard_map/pallas_call | solution.py:641
  140.4 4.7 %shard_map.206 = (f32[704,512]{1,0:T(8,128)S(1)}, f32[8,8,512]{2,1,0:T(8,128)S(1)}) custom-call(f32[704,512]{1,0:T(8,128)S(1)} %shard_map.204.keep_ref, bf16[704,512]{1,0:T(8,128)(2,1)S(1)} %collective-permute-done.9.got_ref, f32[704,512]{1,0:T(8,128)} %copy-done, f32[704,512]{1,0:T(8,128)} %copy-done.15, f32[8,512]{1,0:T(8,128)S(1)} %get-tuple-element.83.first_ref.sum_ref, ...), custom_call_target="tpu_custom_call" | custom-call | flops 1 | bytes 1 | tf_op jit(solution)/shard_map/pallas_call | solution.py:707
  145.1 11.1 %all_to_all.23.sums_ref = f32[8,8,512]{2,1,0:T(8,128)S(1)} all-to-all(f32[8,8,512]{2,1,0:T(8,128)S(1)} %get-tuple-element.91), channel_id=1, replica_groups=mesh['seq'=8,'neur'=4] {'seq'}, dimensions={0} | all-to-all | bytes 262144 | tf_op jit(solution)/shard_map/all_to_all | solution.py:616
  157.7 6.7 %shard_map.210 = (bf16[256,512]{1,0:T(8,128)(2,1)S(1)}, bf16[256,512]{1,0:T(8,128)(2,1)S(1)}, bf16[256,512]{1,0:T(8,128)(2,1)S(1)}, bf16[256,512]{1,0:T(8,128)(2...) custom-call(bf16[704,500]{1,0:T(8,128)(2,1)S(1)} %bitcast.15, ...), custom_call_target="tpu_custom_call" | custom-call | flops 1 | bytes 1 | tf_op jit(solution)/shard_map/pallas_call | solution.py:646
  167.3 6.4 %collective-permute-done.16 = bf16[256,512]{1,0:T(8,128)(2,1)S(1)} collective-permute-done((bf16[256,512]{1,0:T(8,128)(2,1)S(1)}, bf16[256,512]{1,0:T(8,128)(2,1)S(1)}, u32[]{:S(2)}, u32[]{:S(2)}) %collective-permute-start.16) | collective-permute-done | bytes 262176 | tf_op jit(solution)/shard_map/ppermute | solution.py:543
  177.0 2.7 %collective-permute-done.15 = bf16[256,512]{1,0:T(8,128)(2,1)S(1)} collective-permute-done((bf16[256,512]{1,0:T(8,128)(2,1)S(1)}, bf16[256,512]{1,0:T(8,128)(2,1)S(1)}, u32[]{:S(2)}, u32[]{:S(2)}) %collective-permute-start.15) | collective-permute-done | bytes 262176 | tf_op jit(solution)/shard_map/ppermute | solution.py:543
  180.1 5.8 %collective-permute-done.17 = bf16[256,512]{1,0:T(8,128)(2,1)S(1)} collective-permute-done((bf16[256,512]{1,0:T(8,128)(2,1)S(1)}, bf16[256,512]{1,0:T(8,128)(2,1)S(1)}, u32[]{:S(2)}, u32[]{:S(2)}) %collective-permute-start.17) | collective-permute-done | bytes 262176 | tf_op jit(solution)/shard_map/ppermute | solution.py:543
  186.0 5.5 %collective-permute-done.34.refs_2_ = bf16[256,512]{1,0:T(8,128)(2,1)S(1)} collective-permute-done((bf16[256,512]{1,0:T(8,128)(2,1)S(1)}, bf16[256,512]{1,0:T(8,128)(2,1)S(1)}, u32[]{:S(2)}, u32[]{:S(2)}) %collective-permute-start.34) | collective-permute-done | bytes 262176 | tf_op jit(solution)/shard_map/ppermute | solution.py:543
  191.7 2.5 %shard_map.209 = bf16[704,512]{1,0:T(8,128)(2,1)S(1)} custom-call(bf16[704,512]{1,0:T(8,128)(2,1)S(1)} %copy-done.3, bf16[704,512]{1,0:T(8,128)(2,1)S(1)} %collective-permute-done.10.mate_ref, bf16[4,512,512]{2,1,0:T(8,128)(2,1)} %get-tuple-element.94.w_ref, bf16[2,512,512]{2,1,0:T(8,128)(2,1)S(1)} %collective-permute-done.2.wmate_ref), custom_call_target="tpu_custom_call" | custom-call | flops 1 | bytes 1 | tf_op jit(solution)/shard_map/pallas_call | solution.py:637
  199.4 7.5 %collective-permute-done.18 = bf16[256,512]{1,0:T(8,128)(2,1)S(1)} collective-permute-done((bf16[256,512]{1,0:T(8,128)(2,1)S(1)}, bf16[256,512]{1,0:T(8,128)(2,1)S(1)}, u32[]{:S(2)}, u32[]{:S(2)}) %collective-permute-start.18) | collective-permute-done | bytes 262176 | tf_op jit(solution)/shard_map/ppermute | solution.py:543
  209.6 2.5 %shard_map.213 = f32[2000,500]{1,0:T(8,128)} custom-call(bf16[256,512]{1,0:T(8,128)(2,1)S(1)} %add_convert_fusion.refs_0_, bf16[256,512]{1,0:T(8,128)(2,1)S(1)} %collective-permute-done.33.refs_1_, bf16[256,512]{1,0:T(8,128)(2,1)S(1)} %collective-permute-done.34.refs_2_, bf16[256,512]{1,0:T(8,128)(2,1)S(1)} %collective-permute-done.35.refs_3_, ...), custom_call_target="tpu_custom_call" | custom-call | flops 1 | bytes 1 | tf_op jit(solution)/shard_map/pallas_call | solution.py:660
  212.1 5.0 %collective-permute-done.19.refs_1_ = bf16[256,512]{1,0:T(8,128)(2,1)S(1)} collective-permute-done((bf16[256,512]{1,0:T(8,128)(2,1)S(1)}, bf16[256,512]{1,0:T(8,128)(2,1)S(1)}, u32[]{:S(2)}, u32[]{:S(2)}) %collective-permute-start.19) | collective-permute-done | bytes 262176 | tf_op jit(solution)/shard_map/ppermute | solution.py:543
  218.9 2.5 %shard_map.208 = f32[704,512]{1,0:T(8,128)S(1)} custom-call(bf16[704,512]{1,0:T(8,128)(2,1)S(1)} %copy-done.3, bf16[704,512]{1,0:T(8,128)(2,1)S(1)} %collective-permute-done.10.mate_ref, bf16[4,512,512]{2,1,0:T(8,128)(2,1)} %get-tuple-element.94.w_ref, bf16[2,512,512]{2,1,0:T(8,128)(2,1)S(1)} %collective-permute-done.2.wmate_ref), custom_call_target="tpu_custom_call" | custom-call | flops 1 | bytes 1 | tf_op jit(solution)/shard_map/pallas_call | solution.py:641
  228.3 5.6 %collective-permute-done.24.refs_6_ = bf16[256,512]{1,0:T(8,128)(2,1)S(1)} collective-permute-done((bf16[256,512]{1,0:T(8,128)(2,1)S(1)}, bf16[256,512]{1,0:T(8,128)(2,1)S(1)}, u32[]{:S(2)}, u32[]{:S(2)}) %collective-permute-start.24) | collective-permute-done | bytes 262176 | tf_op jit(solution)/shard_map/ppermute | solution.py:543
  233.9 2.8 %collective-permute-done.25.refs_7_ = bf16[256,512]{1,0:T(8,128)(2,1)S(1)} collective-permute-done((bf16[256,512]{1,0:T(8,128)(2,1)S(1)}, bf16[256,512]{1,0:T(8,128)(2,1)S(1)}, u32[]{:S(2)}, u32[]{:S(2)}) %collective-permute-start.25) | collective-permute-done | bytes 262176 | tf_op jit(solution)/shard_map/ppermute | solution.py:543
  236.7 2.5 %shard_map.211 = f32[2000,500]{1,0:T(8,128)} custom-call(bf16[256,512]{1,0:T(8,128)(2,1)S(1)} %add_convert_fusion.7.refs_0_, bf16[256,512]{1,0:T(8,128)(2,1)S(1)} %collective-permute-done.19.refs_1_, bf16[256,512]{1,0:T(8,128)(2,1)S(1)} %collective-permute-done.20.refs_2_, bf16[256,512]{1,0:T(8,128)(2,1)S(1)} %collective-permute-done.21.refs_3_, ...), custom_call_target="tpu_custom_call" | custom-call | flops 1 | bytes 1 | tf_op jit(solution)/shard_map/pallas_call | solution.py:660
  (140 shorter events, 52.7 us)
Async XLA Ops:
  3.8 22.0 %collective-permute-start.2 = (bf16[2,512,512]{2,1,0:T(8,128)(2,1)S(1)}, bf16[2,512,512]{2,1,0:T(8,128)(2,1)S(1)}, u32[]{:S(2)}, u32[]{:S(2)}) collective-permute-start(bf16[2,512,512]{2,1,0:T(8,128)(2,1)S(1)} %get-tuple-element.66), channel_id=1, source_target_pairs={{0,1},{1,0},{2,3},{3,2},{4,5},{5,4},{6,7},{7,6},{8,9},{9,8},{10,11... | collective-permute-start | bytes 3145736 | tf_op jit(solution)/shard_map/ppermute | solution.py:543
  6.1 19.8 %collective-permute-start.3 = (bf16[2,512,512]{2,1,0:T(8,128)(2,1)S(1)}, bf16[2,512,512]{2,1,0:T(8,128)(2,1)S(1)}, u32[]{:S(2)}, u32[]{:S(2)}) collective-permute-start(bf16[2,512,512]{2,1,0:T(8,128)(2,1)S(1)} %get-tuple-element.67), channel_id=1, source_target_pairs={{0,1},{1,0},{2,3},{3,2},{4,5},{5,4},{6,7},{7,6},{8,9},{9,8},{10,11... | collective-permute-start | bytes 3145736 | tf_op jit(solution)/shard_map/ppermute | solution.py:543
  6.6 19.2 %collective-permute-start = (bf16[704,500]{1,0:T(8,128)(2,1)S(1)}, bf16[704,500]{1,0:T(8,128)(2,1)S(1)}, u32[]{:S(2)}, u32[]{:S(2)}) collective-permute-start(bf16[704,500]{1,0:T(8,128)(2,1)S(1)} %bitcast.13), channel_id=1, source_target_pairs={{0,2},{1,3},{2,0},{3,1},{4,6},{5,7},{6,4},{7,5},{8,10},{9,11},{10,... | collective-permute-start | bytes 2112008 | tf_op jit(solution)/shard_map/ppermute | solution.py:543
  53.8 18.8 %collective-permute-start.5 = (bf16[704,500]{1,0:T(8,128)(2,1)}, bf16[704,500]{1,0:T(8,128)(2,1)S(1)}, u32[]{:S(2)}, u32[]{:S(2)}) collective-permute-start(bf16[704,500]{1,0:T(8,128)(2,1)} %get-tuple-element.74.own_ref), channel_id=1, source_target_pairs={{0,2},{1,3},{2,0},{3,1},{4,6},{5,7},{6,4},{7,5},{8,10},{9,11},{10,... | collective-permute-start | bytes 2112008 | tf_op jit(solution)/shard_map/ppermute | solution.py:543
  109.2 9.9 %collective-permute-start.8 = (bf16[704,512]{1,0:T(8,128)(2,1)S(1)}, bf16[704,512]{1,0:T(8,128)(2,1)S(1)}, u32[]{:S(2)}, u32[]{:S(2)}) collective-permute-start(bf16[704,512]{1,0:T(8,128)(2,1)S(1)} %get-tuple-element.88.g_ref), channel_id=1, source_target_pairs={{0,1},{1,0},{2,3},{3,2},{4,5},{5,4},{6,7},{7,6},{8,9},{9,8},{10,11... | collective-permute-start | bytes 2162696 | tf_op jit(solution)/shard_map/ppermute | solution.py:543
  117.0 14.6 %collective-permute-start.27 = (bf16[256,512]{1,0:T(8,128)(2,1)S(1)}, bf16[256,512]{1,0:T(8,128)(2,1)S(1)}, u32[]{:S(2)}, u32[]{:S(2)}) collective-permute-start(bf16[256,512]{1,0:T(8,128)(2,1)S(1)} %get-tuple-element.109), channel_id=1, source_target_pairs={{0,4},{4,0},{8,12},{12,8},{16,20},{20,16},{24,28},{28,24},{1,5},{5... | collective-permute-start | bytes 786440 | tf_op jit(solution)/shard_map/ppermute | solution.py:543
  118.9 18.4 %collective-permute-start.29 = (bf16[256,512]{1,0:T(8,128)(2,1)S(1)}, bf16[256,512]{1,0:T(8,128)(2,1)S(1)}, u32[]{:S(2)}, u32[]{:S(2)}) collective-permute-start(bf16[256,512]{1,0:T(8,128)(2,1)S(1)} %get-tuple-element.111), channel_id=1, source_target_pairs={{0,4},{4,0},{8,12},{12,8},{16,20},{20,16},{24,28},{28,24},{1,5},{5... | collective-permute-start | bytes 786440 | tf_op jit(solution)/shard_map/ppermute | solution.py:543
  122.7 17.7 %collective-permute-start.9 = (bf16[704,512]{1,0:T(8,128)(2,1)S(1)}, bf16[704,512]{1,0:T(8,128)(2,1)S(1)}, u32[]{:S(2)}, u32[]{:S(2)}) collective-permute-start(bf16[704,512]{1,0:T(8,128)(2,1)S(1)} %shard_map.205), channel_id=1, source_target_pairs={{0,2},{1,3},{2,0},{3,1},{4,6},{5,7},{6,4},{7,5},{8,10},{9,11},{10,... | collective-permute-start | bytes 2162696 | tf_op jit(solution)/shard_map/ppermute | solution.py:543
  126.1 11.2 %collective-permute-start.31 = (bf16[256,512]{1,0:T(8,128)(2,1)S(1)}, bf16[256,512]{1,0:T(8,128)(2,1)S(1)}, u32[]{:S(2)}, u32[]{:S(2)}) collective-permute-start(bf16[256,512]{1,0:T(8,128)(2,1)S(1)} %add_convert_fusion.2), channel_id=1, source_target_pairs={{0,8},{4,12},{8,0},{12,4},{16,24},{20,28},{24,16},{28,20},{1,9},{5... | collective-permute-start | bytes 786440 | tf_op jit(solution)/shard_map/ppermute | solution.py:543
  126.2 38.5 %collective-permute-start.26 = (bf16[256,512]{1,0:T(8,128)(2,1)S(1)}, bf16[256,512]{1,0:T(8,128)(2,1)S(1)}, u32[]{:S(2)}, u32[]{:S(2)}) collective-permute-start(bf16[256,512]{1,0:T(8,128)(2,1)S(1)} %get-tuple-element.107), channel_id=1, source_target_pairs={{0,4},{4,0},{8,12},{12,8},{16,20},{20,16},{24,28},{28,24},{1,5},{5... | collective-permute-start | bytes 786440 | tf_op jit(solution)/shard_map/ppermute | solution.py:543
  131.7 33.0 %collective-permute-start.28 = (bf16[256,512]{1,0:T(8,128)(2,1)S(1)}, bf16[256,512]{1,0:T(8,128)(2,1)S(1)}, u32[]{:S(2)}, u32[]{:S(2)}) collective-permute-start(bf16[256,512]{1,0:T(8,128)(2,1)S(1)} %add_convert_fusion.5), channel_id=1, source_target_pairs={{0,8},{4,12},{8,0},{12,4},{16,24},{20,28},{24,16},{28,20},{1,9},{5... | collective-permute-start | bytes 786440 | tf_op jit(solution)/shard_map/ppermute | solution.py:543
  137.4 27.3 %collective-permute-start.32 = (bf16[256,512]{1,0:T(8,128)(2,1)S(1)}, bf16[256,512]{1,0:T(8,128)(2,1)S(1)}, u32[]{:S(2)}, u32[]{:S(2)}) collective-permute-start(bf16[256,512]{1,0:T(8,128)(2,1)S(1)} %add_convert_fusion.1), channel_id=1, source_target_pairs={{0,16},{4,20},{8,24},{12,28},{16,0},{20,4},{24,8},{28,12},{1,17},{... | collective-permute-start | bytes 786440 | tf_op jit(solution)/shard_map/ppermute | solution.py:543
  164.4 9.3 %collective-permute-start.16 = (bf16[256,512]{1,0:T(8,128)(2,1)S(1)}, bf16[256,512]{1,0:T(8,128)(2,1)S(1)}, u32[]{:S(2)}, u32[]{:S(2)}) collective-permute-start(bf16[256,512]{1,0:T(8,128)(2,1)S(1)} %get-tuple-element.104), channel_id=1, source_target_pairs={{0,4},{4,0},{8,12},{12,8},{16,20},{20,16},{24,28},{28,24},{1,5},{5... | collective-permute-start | bytes 786440 | tf_op jit(solution)/shard_map/ppermute | solution.py:543
  164.8 11.0 %collective-permute-start.33 = (bf16[256,512]{1,0:T(8,128)(2,1)S(1)}, bf16[256,512]{1,0:T(8,128)(2,1)S(1)}, u32[]{:S(2)}, u32[]{:S(2)}) collective-permute-start(bf16[256,512]{1,0:T(8,128)(2,1)S(1)} %add_convert_fusion.refs_0_), channel_id=1, source_target_pairs={{0,16},{4,20},{8,24},{12,28},{16,0},{20,4},{24,8},{28,12},{1,17},{... | collective-permute-start | bytes 786440 | tf_op jit(solution)/shard_map/ppermute | solution.py:543
  165.3 11.7 %collective-permute-start.13 = (bf16[256,512]{1,0:T(8,128)(2,1)S(1)}, bf16[256,512]{1,0:T(8,128)(2,1)S(1)}, u32[]{:S(2)}, u32[]{:S(2)}) collective-permute-start(bf16[256,512]{1,0:T(8,128)(2,1)S(1)} %get-tuple-element.100), channel_id=1, source_target_pairs={{0,4},{4,0},{8,12},{12,8},{16,20},{20,16},{24,28},{28,24},{1,5},{5... | collective-permute-start | bytes 786440 | tf_op jit(solution)/shard_map/ppermute | solution.py:543
  167.1 12.7 %collective-permute-start.15 = (bf16[256,512]{1,0:T(8,128)(2,1)S(1)}, bf16[256,512]{1,0:T(8,128)(2,1)S(1)}, u32[]{:S(2)}, u32[]{:S(2)}) collective-permute-start(bf16[256,512]{1,0:T(8,128)(2,1)S(1)} %get-tuple-element.102), channel_id=1, source_target_pairs={{0,4},{4,0},{8,12},{12,8},{16,20},{20,16},{24,28},{28,24},{1,5},{5... | collective-permute-start | bytes 786440 | tf_op jit(solution)/shard_map/ppermute | solution.py:543
  173.8 12.1 %collective-permute-start.17 = (bf16[256,512]{1,0:T(8,128)(2,1)S(1)}, bf16[256,512]{1,0:T(8,128)(2,1)S(1)}, u32[]{:S(2)}, u32[]{:S(2)}) collective-permute-start(bf16[256,512]{1,0:T(8,128)(2,1)S(1)} %add_convert_fusion.9), channel_id=1, source_target_pairs={{0,8},{4,12},{8,0},{12,4},{16,24},{20,28},{24,16},{28,20},{1,9},{5... | collective-permute-start | bytes 786440 | tf_op jit(solution)/shard_map/ppermute | solution.py:543
  173.8 17.7 %collective-permute-start.34 = (bf16[256,512]{1,0:T(8,128)(2,1)S(1)}, bf16[256,512]{1,0:T(8,128)(2,1)S(1)}, u32[]{:S(2)}, u32[]{:S(2)}) collective-permute-start(bf16[256,512]{1,0:T(8,128)(2,1)S(1)} %add_convert_fusion.refs_0_), channel_id=1, source_target_pairs={{0,8},{4,12},{8,0},{12,4},{16,24},{20,28},{24,16},{28,20},{1,9},{5... | collective-permute-start | bytes 786440 | tf_op jit(solution)/shard_map/ppermute | solution.py:543
  175.9 19.1 %collective-permute-start.35 = (bf16[256,512]{1,0:T(8,128)(2,1)S(1)}, bf16[256,512]{1,0:T(8,128)(2,1)S(1)}, u32[]{:S(2)}, u32[]{:S(2)}) collective-permute-start(bf16[256,512]{1,0:T(8,128)(2,1)S(1)} %collective-permute-done.33.refs_1_), channel_id=1, source_target_pairs={{0,8},{4,12},{8,0},{12,4},{16,24},{20,28},{24,16},{28,20},{1,9},{5... | collective-permute-start | bytes 786440 | tf_op jit(solution)/shard_map/ppermute | solution.py:543
  177.0 14.5 %collective-permute-start.10 = (bf16[704,512]{1,0:T(8,128)(2,1)S(1)}, bf16[704,512]{1,0:T(8,128)(2,1)S(1)}, u32[]{:S(2)}, u32[]{:S(2)}) collective-permute-start(bf16[704,512]{1,0:T(8,128)(2,1)S(1)} %copy-done.3), channel_id=1, source_target_pairs={{0,1},{1,0},{2,3},{3,2},{4,5},{5,4},{6,7},{7,6},{8,9},{9,8},{10,11... | collective-permute-start | bytes 2162696 | tf_op jit(solution)/shard_map/ppermute | solution.py:543
  179.8 16.4 %collective-permute-start.12 = (bf16[256,512]{1,0:T(8,128)(2,1)S(1)}, bf16[256,512]{1,0:T(8,128)(2,1)S(1)}, u32[]{:S(2)}, u32[]{:S(2)}) collective-permute-start(bf16[256,512]{1,0:T(8,128)(2,1)S(1)} %get-tuple-element.98), channel_id=1, source_target_pairs={{0,4},{4,0},{8,12},{12,8},{16,20},{20,16},{24,28},{28,24},{1,5},{5... | collective-permute-start | bytes 786440 | tf_op jit(solution)/shard_map/ppermute | solution.py:543
  185.9 12.2 %collective-permute-start.14 = (bf16[256,512]{1,0:T(8,128)(2,1)S(1)}, bf16[256,512]{1,0:T(8,128)(2,1)S(1)}, u32[]{:S(2)}, u32[]{:S(2)}) collective-permute-start(bf16[256,512]{1,0:T(8,128)(2,1)S(1)} %add_convert_fusion.12), channel_id=1, source_target_pairs={{0,8},{4,12},{8,0},{12,4},{16,24},{20,28},{24,16},{28,20},{1,9},{5... | collective-permute-start | bytes 786440 | tf_op jit(solution)/shard_map/ppermute | solution.py:543
  191.5 15.4 %collective-permute-start.18 = (bf16[256,512]{1,0:T(8,128)(2,1)S(1)}, bf16[256,512]{1,0:T(8,128)(2,1)S(1)}, u32[]{:S(2)}, u32[]{:S(2)}) collective-permute-start(bf16[256,512]{1,0:T(8,128)(2,1)S(1)} %add_convert_fusion.8), channel_id=1, source_target_pairs={{0,16},{4,20},{8,24},{12,28},{16,0},{20,4},{24,8},{28,12},{1,17},{... | collective-permute-start | bytes 786440 | tf_op jit(solution)/shard_map/ppermute | solution.py:543
  191.5 17.3 %collective-permute-start.36 = (bf16[256,512]{1,0:T(8,128)(2,1)S(1)}, bf16[256,512]{1,0:T(8,128)(2,1)S(1)}, u32[]{:S(2)}, u32[]{:S(2)}) collective-permute-start(bf16[256,512]{1,0:T(8,128)(2,1)S(1)} %add_convert_fusion.refs_0_), channel_id=1, source_target_pairs={{0,4},{4,0},{8,12},{12,8},{16,20},{20,16},{24,28},{28,24},{1,5},{5... | collective-permute-start | bytes 786440 | tf_op jit(solution)/shard_map/ppermute | solution.py:543
  195.0 13.9 %collective-permute-start.37 = (bf16[256,512]{1,0:T(8,128)(2,1)S(1)}, bf16[256,512]{1,0:T(8,128)(2,1)S(1)}, u32[]{:S(2)}, u32[]{:S(2)}) collective-permute-start(bf16[256,512]{1,0:T(8,128)(2,1)S(1)} %collective-permute-done.33.refs_1_), channel_id=1, source_target_pairs={{0,4},{4,0},{8,12},{12,8},{16,20},{20,16},{24,28},{28,24},{1,5},{5... | collective-permute-start | bytes 786440 | tf_op jit(solution)/shard_map/ppermute | solution.py:543
  196.2 12.7 %collective-permute-start.38 = (bf16[256,512]{1,0:T(8,128)(2,1)S(1)}, bf16[256,512]{1,0:T(8,128)(2,1)S(1)}, u32[]{:S(2)}, u32[]{:S(2)}) collective-permute-start(bf16[256,512]{1,0:T(8,128)(2,1)S(1)} %collective-permute-done.34.refs_2_), channel_id=1, source_target_pairs={{0,4},{4,0},{8,12},{12,8},{16,20},{20,16},{24,28},{28,24},{1,5},{5... | collective-permute-start | bytes 786440 | tf_op jit(solution)/shard_map/ppermute | solution.py:543
  198.1 11.5 %collective-permute-start.39 = (bf16[256,512]{1,0:T(8,128)(2,1)S(1)}, bf16[256,512]{1,0:T(8,128)(2,1)S(1)}, u32[]{:S(2)}, u32[]{:S(2)}) collective-permute-start(bf16[256,512]{1,0:T(8,128)(2,1)S(1)} %collective-permute-done.35.refs_3_), channel_id=1, source_target_pairs={{0,4},{4,0},{8,12},{12,8},{16,20},{20,16},{24,28},{28,24},{1,5},{5... | collective-permute-start | bytes 786440 | tf_op jit(solution)/shard_map/ppermute | solution.py:543
  206.9 18.6 %collective-permute-start.11 = (bf16[704,512]{1,0:T(8,128)(2,1)S(1)}, bf16[704,512]{1,0:T(8,128)(2,1)S(1)}, u32[]{:S(2)}, u32[]{:S(2)}) collective-permute-start(bf16[704,512]{1,0:T(8,128)(2,1)S(1)} %shard_map.209), channel_id=1, source_target_pairs={{0,2},{1,3},{2,0},{3,1},{4,6},{5,7},{6,4},{7,5},{8,10},{9,11},{10,... | collective-permute-start | bytes 2162696 | tf_op jit(solution)/shard_map/ppermute | solution.py:543
  212.1 11.4 %collective-permute-start.20 = (bf16[256,512]{1,0:T(8,128)(2,1)S(1)}, bf16[256,512]{1,0:T(8,128)(2,1)S(1)}, u32[]{:S(2)}, u32[]{:S(2)}) collective-permute-start(bf16[256,512]{1,0:T(8,128)(2,1)S(1)} %add_convert_fusion.7.refs_0_), channel_id=1, source_target_pairs={{0,8},{4,12},{8,0},{12,4},{16,24},{20,28},{24,16},{28,20},{1,9},{5... | collective-permute-start | bytes 786440 | tf_op jit(solution)/shard_map/ppermute | solution.py:543
  222.0 11.9 %collective-permute-start.23 = (bf16[256,512]{1,0:T(8,128)(2,1)S(1)}, bf16[256,512]{1,0:T(8,128)(2,1)S(1)}, u32[]{:S(2)}, u32[]{:S(2)}) collective-permute-start(bf16[256,512]{1,0:T(8,128)(2,1)S(1)} %collective-permute-done.19.refs_1_), channel_id=1, source_target_pairs={{0,4},{4,0},{8,12},{12,8},{16,20},{20,16},{24,28},{28,24},{1,5},{5... | collective-permute-start | bytes 786440 | tf_op jit(solution)/shard_map/ppermute | solution.py:543
  223.5 10.4 %collective-permute-start.24 = (bf16[256,512]{1,0:T(8,128)(2,1)S(1)}, bf16[256,512]{1,0:T(8,128)(2,1)S(1)}, u32[]{:S(2)}, u32[]{:S(2)}) collective-permute-start(bf16[256,512]{1,0:T(8,128)(2,1)S(1)} %collective-permute-done.20.refs_2_), channel_id=1, source_target_pairs={{0,4},{4,0},{8,12},{12,8},{16,20},{20,16},{24,28},{28,24},{1,5},{5... | collective-permute-start | bytes 786440 | tf_op jit(solution)/shard_map/ppermute | solution.py:543
  224.0 12.7 %collective-permute-start.25 = (bf16[256,512]{1,0:T(8,128)(2,1)S(1)}, bf16[256,512]{1,0:T(8,128)(2,1)S(1)}, u32[]{:S(2)}, u32[]{:S(2)}) collective-permute-start(bf16[256,512]{1,0:T(8,128)(2,1)S(1)} %collective-permute-done.21.refs_3_), channel_id=1, source_target_pairs={{0,4},{4,0},{8,12},{12,8},{16,20},{20,16},{24,28},{28,24},{1,5},{5... | collective-permute-start | bytes 786440 | tf_op jit(solution)/shard_map/ppermute | solution.py:543
  (35 other events, 208.8 us)

commit v2 on v1

v2 whole, which is shorter than its diff:
```python
import functools
import math

import jax
import jax.numpy as jnp
from jax import lax
from jax.experimental import pallas as pl
from jax.experimental.pallas import tpu as pltpu
from jax.sharding import PartitionSpec as P

EPSILON = 1e-05
MOMENTUM = 0.1
LANE = 128
CHUNKS = 32
GROUPS = CHUNKS // 8
TOLERANCE = 1e-5
LOG2E = math.log2(math.e)
LN2 = math.log(2.0)
F32 = jnp.float32
BF16 = jnp.bfloat16
VMEM_BYTES = 16 * 1024 * 1024


def call(kernel, outs, scratch=(), **specs):
    return pl.pallas_call(
        kernel,
        **specs,
        out_shape=outs,
        scratch_shapes=list(scratch),
        compiler_params=pltpu.CompilerParams(vmem_limit_bytes=VMEM_BYTES),
    )


def shape(*dims, dtype=F32):
    return jax.ShapeDtypeStruct(dims, dtype)


def tiles_of(width):
    return [(j, j * LANE, min(LANE, width - j * LANE)) for j in range(-(-width // LANE))]


def dot(a, b):
    return jnp.dot(a, b, preferred_element_type=F32)


def dot_nt(a, b):
    return lax.dot_general(a, b, (((1,), (1,)), ((), ())), preferred_element_type=F32)


def block_kernel(w_ref, gain_ref, shift_ref, decay_ref, out_ref, mate_ref, par_ref):
    here = lax.axis_index("neur")
    blocks, width, _ = out_ref.shape
    real = w_ref.shape[0] // blocks
    out_ref[...] = jnp.zeros(out_ref.shape, BF16)
    for b in range(blocks):
        out_ref[b, :real, : w_ref.shape[1]] = w_ref[b * real : (b + 1) * real, :]
    for i, k in enumerate((1, 3)):
        mate_ref[i] = out_ref[here ^ k]
    par_ref[...] = jnp.zeros(par_ref.shape, F32)
    for i, row_ref in enumerate((gain_ref, shift_ref, decay_ref)):
        par_ref[i : i + 1, : row_ref.shape[1]] = row_ref[...]


def means_of(x_ref):
    length = x_ref.shape[0]
    return dot(jnp.ones((16, length), BF16), x_ref[...])[:1] * (1.0 / length)


def project_early(own_ref, mate_ref, w_ref, part_ref, means_ref):
    here = lax.axis_index("neur")
    k = own_ref.shape[1]
    means_ref[...] = jnp.zeros(means_ref.shape, F32)
    means_ref[0:1, :k] = means_of(own_ref)
    means_ref[1:2, :k] = means_of(mate_ref)
    for c in range(0, part_ref.shape[1], 256):
        part_ref[:, c : c + 256] = dot(own_ref[...], w_ref[here, :k, c : c + 256]) + dot(
            mate_ref[...], w_ref[here ^ 1, :k, c : c + 256]
        )


def project_late(part_ref, means_ref, far_ref, cross_ref, w_ref, proj_ref, stats_ref):
    here = lax.axis_index("neur")
    k = far_ref.shape[1]
    peers, _, width = stats_ref.shape
    far, cross = means_of(far_ref), means_of(cross_ref)
    for p in range(peers):
        stats_ref[p, 2:4, :] = means_ref[0:2, :]
        stats_ref[p, 4:8, :] = jnp.zeros((4, width), F32)
        stats_ref[p, 4:5, :k] = far
        stats_ref[p, 5:6, :k] = cross
    length = proj_ref.shape[0]
    for c in range(0, part_ref.shape[1], 256):
        y = (
            part_ref[:, c : c + 256]
            + dot(far_ref[...], w_ref[here ^ 2, :k, c : c + 256])
            + dot(cross_ref[...], w_ref[here ^ 3, :k, c : c + 256])
        )
        proj_ref[:, c : c + 256] = y
        mean = jnp.sum(y, axis=0, keepdims=True) * (1.0 / length)
        off = y - mean
        spread = jnp.sum(off * off, axis=0, keepdims=True)
        for p in range(stats_ref.shape[0]):
            stats_ref[p, 0:1, c : c + 256] = mean
            stats_ref[p, 1:2, c : c + 256] = spread


def merged(stats_ref, length, sum_ref):
    peers = stats_ref.shape[0]
    means = [stats_ref[p, 0:1, :] for p in range(peers)]
    mean = sum(means[1:], means[0]) * (1.0 / peers)
    total = None
    for p in range(peers):
        off = means[p] - mean
        term = stats_ref[p, 1:2, :] + off * off * float(length)
        total = term if total is None else total + term
    var = total * (1.0 / (peers * length))
    inverse = lax.rsqrt(var + EPSILON)
    features = stats_ref[0, 2:6, :]
    for p in range(1, peers):
        features = features + stats_ref[p, 2:6, :]
    sum_ref[0:1, :] = mean
    sum_ref[1:2, :] = var
    sum_ref[2:3, :] = inverse
    sum_ref[3:4, :] = stats_ref[lax.axis_index("seq"), 0:1, :]
    sum_ref[4:8, :] = features * (1.0 / peers)
    return mean, var, inverse


def spread_rows(row, tiles):
    return [jnp.broadcast_to(row[:, c : c + LANE], (8, LANE)) for _, c, _ in tiles]


def load_step(ref, step, tiles, lead=0):
    steps = (ref.shape[1] - lead) // CHUNKS
    return [
        ref[j, pl.ds(lead + step + g * 8 * steps, 8, stride=steps), :]
        for j, _, _ in tiles
        for g in range(GROUPS)
    ]


def store_step(ref, step, tiles, values, lead=0):
    steps = (ref.shape[1] - lead) // CHUNKS
    i = 0
    for j, _, _ in tiles:
        for g in range(GROUPS):
            ref[j, pl.ds(lead + step + g * 8 * steps, 8, stride=steps), :] = values[i]
            i += 1


def rows_before(x, k, fill):
    at = lax.broadcasted_iota(jnp.int32, x.shape, 0)
    return jnp.where(at >= k, pltpu.roll(x, k, axis=0), fill)


def rows_after(x, k, fill):
    at = lax.broadcasted_iota(jnp.int32, x.shape, 0)
    return jnp.where(at < 8 - k, pltpu.roll(x, 8 - k, axis=0), fill)


def whole_row(x, i):
    return jnp.broadcast_to(x[i : i + 1, :], x.shape)


def chain(base, slope, floor=None, back=False):
    shifted, last, first = (rows_after, 0, 7) if back else (rows_before, 7, 0)
    starts = [None] * GROUPS
    carry = jnp.zeros((8, LANE), F32)
    for g in reversed(range(GROUPS)) if back else range(GROUPS):
        b, q, f = base[g], slope[g], None if floor is None else floor[g]
        for k in (1, 2, 4):
            early = shifted(b, k, 0.0)
            if f is not None:
                f = jnp.maximum(f, b + q * shifted(f, k, 0.0))
            b = b + q * early
            q = q * shifted(q, k, 1.0)
        ends = b + q * carry
        if f is not None:
            ends = jnp.maximum(ends, f)
        starts[g] = jnp.where(
            lax.broadcasted_iota(jnp.int32, ends.shape, 0) == first, carry, shifted(ends, 1, 0.0)
        )
        carry = whole_row(ends, last)
    return starts


def by_tile(tiles, run, *lists):
    out = []
    for n in range(len(tiles)):
        out += run(*(x[n * GROUPS : (n + 1) * GROUPS] for x in lists))
    return out


def handed_on(ends):
    out, carry = [], jnp.zeros((8, LANE), F32)
    for x in ends:
        out.append(jnp.where(lax.broadcasted_iota(jnp.int32, x.shape, 0) == 0, carry, rows_before(x, 1, 0.0)))
        carry = whole_row(x, 7)
    return out


def power(x, n):
    out = None
    while n:
        if n & 1:
            out = x if out is None else out * x
        x = x * x
        n >>= 1
    return out


def softplus2(before):
    return [jnp.where(b > 25.0, b * LN2, jnp.log(1.0 + jnp.exp2(b))) for b in before]


def run_bounds(drive_ref, decay, tiles, steps):
    u = [d for d in decay for _ in range(GROUPS)]
    u2 = [d * LOG2E for d in u]

    def body(step, carry):
        state, line = carry
        drive = load_step(drive_ref, step, tiles)
        line = [d + a * v for d, a, v in zip(drive, u, line)]
        state = softplus2([d + a * v for d, a, v in zip(drive, u2, state)])
        return state, line

    zero = [jnp.zeros((8, LANE), F32) for _ in u]
    state, line = lax.fori_loop(0, steps, body, (zero, zero), unroll=11)
    return state, [a * LN2 for a in line]


def run_chunks(drive_ref, state_ref, start, decay, tiles, steps):
    u2 = [d * LOG2E for d in decay for _ in range(GROUPS)]

    def body(step, carry):
        state, slope = carry
        drive = load_step(drive_ref, step, tiles)
        before = [d + u * s for d, u, s in zip(drive, u2, state)]
        state = softplus2(before)
        slope = [a + (b - s * LOG2E) for a, b, s in zip(slope, before, state)]
        store_step(state_ref, step, tiles, state, lead=8)
        return state, slope

    zero = [jnp.zeros((8, LANE), F32) for _ in start]
    state, slope = lax.fori_loop(0, steps, body, (start, zero), unroll=True)
    top = [power(d, steps) for d in decay for _ in range(GROUPS)]
    return state, [t * jnp.exp2(a) for t, a in zip(top, slope)]


def solve(drive_ref, state_ref, decay_row, tiles):
    steps = drive_ref.shape[1] // CHUNKS
    decay = spread_rows(decay_row, tiles)
    top = [power(d, steps) for d in decay for _ in range(GROUPS)]
    low, line = run_bounds(drive_ref, decay, tiles, steps)
    start = by_tile(tiles, lambda f, b, q: chain(b, q, f), low, line, top)

    def again(carry):
        count, worst, _ = carry
        return jnp.logical_and(worst > 0.0, count < CHUNKS + 1)

    def newton(carry):
        count, _, start = carry
        end, slope = run_chunks(drive_ref, state_ref, start, decay, tiles, steps)
        miss = [e - s for e, s in zip(by_tile(tiles, handed_on, end), start)]
        worst = None
        for m, s in zip(miss, start):
            over = jnp.abs(m) - TOLERANCE * jnp.maximum(s, 1.0)
            worst = over if worst is None else jnp.maximum(worst, over)

        def step(miss, slope, start):
            after = [
                jnp.where(
                    lax.broadcasted_iota(jnp.int32, m.shape, 0) == 7,
                    whole_row(miss[g + 1], 0) if g + 1 < GROUPS else 0.0,
                    rows_after(m, 1, 0.0),
                )
                for g, m in enumerate(miss)
            ]
            return [s + c for s, c in zip(start, chain(after, slope))]

        return count + 1, jnp.max(worst), by_tile(tiles, step, miss, slope, start)

    lax.while_loop(again, newton, (jnp.int32(0), jnp.float32(1.0), start))


def run_back(grad_ref, sigma_ref, start, decay, tiles, steps, store):
    u = [d for d in decay for _ in range(GROUPS)]

    def body(i, carry):
        z, prod = carry
        step = steps - 1 - i
        gs = load_step(grad_ref, step, tiles)
        sig = load_step(sigma_ref, step, tiles)
        z = [s * (g + a * v) for s, g, a, v in zip(sig, gs, u, z)]
        if store:
            store_step(grad_ref, step, tiles, z)
            return z, prod
        return z, [p * (s * a) for p, s, a in zip(prod, sig, u)]

    ones = [] if store else [jnp.ones((8, LANE), F32) for _ in start]
    return lax.fori_loop(0, steps, body, (start, ones), unroll=11)


def solve_back(grad_ref, sigma_ref, decay_row, tiles):
    steps = grad_ref.shape[1] // CHUNKS
    decay = spread_rows(decay_row, tiles)
    zero = [jnp.zeros((8, LANE), F32)] * (len(tiles) * GROUPS)
    end, slope = run_back(grad_ref, sigma_ref, zero, decay, tiles, steps, False)
    start = by_tile(tiles, lambda b, q: chain(b, q, back=True), end, slope)
    run_back(grad_ref, sigma_ref, start, decay, tiles, steps, True)


BLOCK = 88


def row_blocks(length, body):
    @pl.loop(0, length // BLOCK)
    def _(i):
        body(pl.ds(pl.multiple_of(i * BLOCK, 8), BLOCK))


def fill_drive(proj_ref, drive_ref, mean, inverse, gain, shift, tiles):
    scale = inverse * gain * LOG2E
    offset = shift * LOG2E

    def body(rows):
        for j, c, _ in tiles:
            at = slice(c, c + LANE)
            drive_ref[j, rows, :] = (proj_ref[rows, at] - mean[:, at]) * scale[:, at] + offset[:, at]

    row_blocks(proj_ref.shape[0], body)


def fill_sigma(drive_ref, prev_ref, decay_row, tiles, length):
    u2 = decay_row * LOG2E

    def body(i, _):
        for j, c, _w in tiles:
            rows = pl.ds(pl.multiple_of(i * BLOCK, 8), BLOCK)
            before = drive_ref[j, rows, :] + u2[:, c : c + LANE] * prev_ref[j, pl.ds(i * BLOCK + 7, BLOCK), :]
            drive_ref[j, rows, :] = 1.0 / (1.0 + jnp.exp2(-before))
        return 0

    lax.fori_loop(0, length // BLOCK, body, 0)


def finish_back(grad_ref, state_ref, proj_ref, mean, inverse, tiles, gb_ref, sums_ref):
    length, width = proj_ref.shape
    zero = tuple(jnp.zeros((1, LANE), F32) for _ in tiles)

    def body(i, carry):
        shift, gain, decay = (list(x) for x in carry)
        rows = pl.ds(pl.multiple_of(i * BLOCK, 8), BLOCK)
        for j, c, _w in tiles:
            at = slice(c, c + LANE)
            gb = grad_ref[j, rows, :]
            gb_ref[rows, at] = gb
            shift[j] = shift[j] + jnp.sum(gb, axis=0, keepdims=True)
            gain[j] = gain[j] + jnp.sum(gb * (proj_ref[rows, at] - mean[:, at]), axis=0, keepdims=True)
            decay[j] = decay[j] + jnp.sum(
                gb * state_ref[j, pl.ds(i * BLOCK + 7, BLOCK), :], axis=0, keepdims=True
            )
        return tuple(shift), tuple(gain), tuple(decay)

    shift, gain, decay = lax.fori_loop(0, length // BLOCK, body, (zero, zero, zero))
    for j, c, _ in tiles:
        at = slice(c, c + LANE)
        scaled = gain[j] * inverse[:, at]
        for p in range(sums_ref.shape[0]):
            sums_ref[p, 0:1, at] = shift[j]
            sums_ref[p, 1:2, at] = scaled
            sums_ref[p, 2:3, at] = decay[j]


def clear(state_ref, tiles):
    for j, _, _ in tiles:
        state_ref[j, 0:8, :] = jnp.zeros((8, LANE), F32)


def put_states(state_ref, out_ref, tiles, wide_ref=None):
    def body(i, _):
        rows = pl.ds(pl.multiple_of(i * 16, 16), 16)
        for j, c, w in tiles:
            s = state_ref[j, pl.ds(pl.multiple_of(8 + i * 16, 8), 16), :]
            out_ref[rows, c : c + w] = s[:, :w].astype(BF16)
            if wide_ref is not None:
                wide_ref[rows, c : c + LANE] = s
        return 0

    lax.fori_loop(0, out_ref.shape[0] // 16, body, 0, unroll=4)


def forward_kernel(stats_ref, proj_ref, par_ref, out_ref, wide_ref, sum_ref, drive, state):
    length, width = proj_ref.shape
    tiles = tiles_of(width)
    outs = tiles_of(out_ref.shape[1])
    mean, var, inverse = merged(stats_ref, length, sum_ref)
    gain, shift, decay = par_ref[0:1, :], par_ref[1:2, :], par_ref[2:3, :]
    fill_drive(proj_ref, drive, mean, inverse, gain, shift, tiles)
    clear(state, tiles)
    solve(drive, state, decay, tiles)
    put_states(state, out_ref, outs, wide_ref)


def turn_kernel(
    stats_ref,
    proj_ref,
    par_ref,
    first_ref,
    cot_hbm,
    rmean_hbm,
    rvar_hbm,
    out_ref,
    gb_ref,
    sums_ref,
    sum_ref,
    nmean_ref,
    nvar_ref,
    drive,
    state,
    grad,
    cot_ref,
    rmean_ref,
    rvar_ref,
    arrived,
):
    copies = [
        pltpu.make_async_copy(a, b, arrived.at[i])
        for i, (a, b) in enumerate(
            ((cot_hbm, cot_ref), (rmean_hbm, rmean_ref), (rvar_hbm, rvar_ref))
        )
    ]
    for copy in copies:
        copy.start()
    length, width = proj_ref.shape
    tiles = tiles_of(width)
    outs = tiles_of(out_ref.shape[1])
    mean, var, inverse = merged(stats_ref, length, sum_ref)
    gain, shift, decay = par_ref[0:1, :], par_ref[1:2, :], par_ref[2:3, :]
    real = out_ref.shape[1]
    count = float(stats_ref.shape[0] * length)
    fill_drive(proj_ref, drive, mean, inverse, gain, shift, tiles)
    clear(state, tiles)
    solve(drive, state, decay, tiles)
    put_states(state, out_ref, outs)
    fill_sigma(drive, state, decay, tiles, length)
    for copy in copies:
        copy.wait()
    for row, m, v in ((0, first_ref[0:1, :], first_ref[1:2, :]), (1, mean, var)):
        nmean_ref[row : row + 1, :] = (1.0 - MOMENTUM) * rmean_ref[row : row + 1, :] + MOMENTUM * m[:, :real]
        nvar_ref[row : row + 1, :] = (1.0 - MOMENTUM) * rvar_ref[row : row + 1, :] + (
            MOMENTUM * v[:, :real]
        ) * (count / (count - 1.0))
    for j, _, w in outs:
        if w < LANE:
            grad[j] = jnp.zeros(grad.shape[1:], F32)

    def load_cot(i, _):
        rows = pl.ds(pl.multiple_of(i * 16, 16), 16)
        for j, c, w in outs:
            grad[j, rows, :w] = cot_ref[rows, c : c + w].astype(F32)
        return 0

    lax.fori_loop(0, length // 16, load_cot, 0, unroll=4)
    solve_back(grad, drive, decay, tiles)
    finish_back(grad, state, proj_ref, mean, inverse, tiles, gb_ref, sums_ref)


def back_kernel(
    keep_ref, got_ref, proj_ref, wide_ref, sum_ref, par_ref, gb_ref, sums_ref, drive, state, grad
):
    length, width = proj_ref.shape
    tiles = tiles_of(width)
    mean, inverse = sum_ref[0:1, :], sum_ref[2:3, :]
    gain, shift, decay = par_ref[0:1, :], par_ref[1:2, :], par_ref[2:3, :]
    fill_drive(proj_ref, drive, mean, inverse, gain, shift, tiles)
    clear(state, tiles)

    def load(i, _):
        rows = pl.ds(pl.multiple_of(i * 16, 16), 16)
        for j, c, _w in tiles:
            at = slice(c, c + LANE)
            grad[j, rows, :] = keep_ref[rows, at] + got_ref[rows, at].astype(F32)
            state[j, pl.ds(pl.multiple_of(8 + i * 16, 8), 16), :] = wide_ref[rows, at]
        return 0

    lax.fori_loop(0, length // 16, load, 0, unroll=4)
    fill_sigma(drive, state, decay, tiles, length)
    solve_back(grad, drive, decay, tiles)
    finish_back(grad, state, proj_ref, mean, inverse, tiles, gb_ref, sums_ref)


def total_of(sums_ref):
    peers = sums_ref.shape[0]
    out = sums_ref[0]
    for p in range(1, peers):
        out = out + sums_ref[p]
    return out


def grad_kernel(sums_ref, gb_ref, proj_ref, sum_ref, par_ref, g_ref, total_ref):
    length, _ = proj_ref.shape
    total = total_of(sums_ref)
    total_ref[...] = total
    count = float(sums_ref.shape[0] * length)
    mean, inverse = sum_ref[0:1, :], sum_ref[2:3, :]
    scale = par_ref[0:1, :] * inverse
    base = total[0:1, :] * (1.0 / count)
    lean = total[1:2, :] * (1.0 / count) * inverse

    total_ref[7:8, :] = scale * (
        sums_ref[lax.axis_index("seq"), 0:1, :]
        - length * base
        - length * (sum_ref[3:4, :] - mean) * lean
    )

    def body(i, _):
        rows = pl.ds(pl.multiple_of(i * 16, 16), 16)
        g_ref[rows, :] = (
            scale * (gb_ref[rows, :] - base - (proj_ref[rows, :] - mean) * lean)
        ).astype(BF16)
        return 0

    lax.fori_loop(0, length // 16, body, 0, unroll=4)


def send_kernel(g_ref, mate_ref, w_ref, wmate_ref, out_ref):
    here = lax.axis_index("neur")
    for c in range(0, out_ref.shape[1], 256):
        at = slice(c, c + 256)
        out_ref[:, at] = (
            dot_nt(g_ref[...], w_ref[here ^ 2, at, :]) + dot_nt(mate_ref[...], wmate_ref[1, at, :])
        ).astype(BF16)


def keep_kernel(g_ref, mate_ref, w_ref, wmate_ref, out_ref):
    here = lax.axis_index("neur")
    for c in range(0, out_ref.shape[1], 256):
        at = slice(c, c + 256)
        out_ref[:, at] = dot_nt(g_ref[...], w_ref[here, at, :]) + dot_nt(
            mate_ref[...], wmate_ref[0, at, :]
        )


def split(row):
    high = row.astype(BF16)
    return high, (row - high.astype(F32)).astype(BF16)


def dot_tn(a, b):
    return lax.dot_general(a, b, (((0,), (0,)), ((), ())), preferred_element_type=F32)


def outer(a, b):
    (a_high, a_low), (b_high, b_low) = split(a), split(b)
    return dot_tn(
        jnp.concatenate([a_high, a_high, a_low, a_low]), jnp.concatenate([b_high, b_low, b_high, b_low])
    )


def weight_kernel(parted, own_ref, mate_ref, far_ref, cross_ref, g_ref, sum_ref, total_ref, *refs):
    outs, hold = (refs[:-1], refs[-1]) if parted else ((), refs[0])
    place = seat() if parted else 0
    _, half, width = hold.shape
    for k, x_ref in enumerate((own_ref, mate_ref, far_ref, cross_ref)):
        real = x_ref.shape[1]
        mean = sum_ref[4 + k : 5 + k, :real]
        part = (dot_tn(x_ref[...], g_ref[...]) - outer(mean, total_ref[7:8, :])).astype(BF16)
        hold[(2 * k) ^ place] = part[:half]
        rest = part[half:]
        hold[(2 * k + 1) ^ place, : rest.shape[0], :] = rest
        if not parted:
            hold[2 * k + 1, rest.shape[0] :, :] = jnp.zeros((half - rest.shape[0], width), BF16)
    count = hold.shape[0] // len(outs) if outs else 0
    for r, out in enumerate(outs):
        out[...] = hold[r] if count == 1 else hold[r * count : (r + 1) * count]


def halve_kernel(keep_ref, got_ref, mine_ref, give_ref):
    count = mine_ref.shape[0]
    for i in range(2 * count):
        value = wide_sum(keep_ref[i], got_ref[i])
        if i < count:
            mine_ref[i] = value
        else:
            give_ref[i - count] = value.astype(BF16)


def spread_kernel(parted, *refs):
    if parted:
        shares, out_ref, hold = refs[:-2], refs[-2], refs[-1]
        for r, share in enumerate(shares):
            hold[r] = share[...]
    else:
        hold, out_ref = refs
    place, here = seat() if parted else 0, lax.axis_index("neur")
    half = hold.shape[1]
    block = out_ref.shape[0] // 4
    width = out_ref.shape[1]
    for b in range(4):
        for h in range(2):
            low, high = b * block + h * half, min(b * block + h * half + half, (b + 1) * block)
            which = (((here ^ b) * 2) + h) ^ place
            out_ref[low:high, :] = hold[which, : high - low, :width].astype(F32)


def wide_sum(a, b):
    return a.astype(F32) + b.astype(F32)


def half_sum(a, b):
    return wide_sum(a, b).astype(BF16)


def swap(x, bit, axis="seq"):
    n = lax.axis_size(axis)
    return lax.ppermute(x, axis, [(i, i ^ bit) for i in range(n)])


LEVEL = {4: 1, 2: 2, 1: 4}


def seat():
    place = lax.axis_index("seq")
    return ((place & 1) << 2) | (place & 2) | ((place >> 2) & 1)


def send_shares(shares):
    part = {(r >> 2 & 1, r >> 1 & 1, r & 1): v for r, v in enumerate(shares)}
    return part, {q: swap(part[(1,) + q], LEVEL[4]) for q in ((1, 1), (1, 0), (0, 1), (0, 0))}


def halve_shares(part, got):
    mine = {q: wide_sum(part[(0,) + q], v) for q, v in got.items()}
    away, near = (swap(mine[(1, i)].astype(BF16), LEVEL[2]) for i in (1, 0))
    return {i: mine[(0, i)] for i in (0, 1)}, away, near


def quarter_shares(mine, away, near):
    return wide_sum(mine[0], near), swap(half_sum(mine[1], away), LEVEL[1])


def gather_shares(v):
    out = {0: v}
    out[4] = swap(v, LEVEL[4])
    out[2] = swap(v, LEVEL[2])
    out[1] = swap(v, LEVEL[1])
    out[2], out[4] = lax.optimization_barrier((out[2], out[4]))
    out[6] = swap(out[2], LEVEL[4])
    out[5] = swap(out[1], LEVEL[4])
    out[3] = swap(out[1], LEVEL[2])
    out[3], out[6] = lax.optimization_barrier((out[3], out[6]))
    out[7] = swap(out[3], LEVEL[4])
    return [out[r] for r in range(8)]


def per_device(devices_seq, *args):
    (
        tokens,
        w_first,
        gain_first,
        shift_first,
        decay_first,
        w_second,
        gain_second,
        shift_second,
        decay_second,
        cotangent,
        running_mean,
        running_var,
    ) = args
    _, length, real = tokens.shape
    width = -(-real // LANE) * LANE
    tiles = len(tiles_of(width))
    peers = devices_seq
    here = lax.axis_index("neur")
    tokens, cotangent = tokens[0], cotangent[0]

    scans = [
        pltpu.VMEM((tiles, length, LANE), F32),
        pltpu.VMEM((tiles, length + 8, LANE), F32),
    ]
    grads = [pltpu.VMEM((tiles, length, LANE), F32)]

    def share(stats):
        return lax.all_to_all(stats, "seq", 0, 0, tiled=True)

    def project(own, w, rows, *gives):
        far = swap(own, 2, "neur")
        mate = swap(own, 1, "neur")
        w = lax.optimization_barrier((w, own))[0]
        w4, give, par = call(
            block_kernel,
            [shape(4, width, width, dtype=BF16), shape(2, width, width, dtype=BF16), shape(8, width)],
        )(w, *(row[None] for row in rows))
        part, means = call(project_early, [shape(length, width), shape(8, width)])(own, mate, w4)
        gives = [swap(lax.optimization_barrier((g, own))[0], 1, "neur") for g in gives + (give,)] if gives else give
        far, part, par, gives = lax.optimization_barrier((far, part, par, gives))
        cross = swap(far, 1, "neur")
        proj, stats = call(project_late, [shape(length, width), shape(peers, 8, width)])(
            part, means, far, cross, w4
        )
        return (own, mate, far, cross), proj, share(stats), w4, gives, par

    def gradient(sums, gb, proj, summary, par):
        return call(grad_kernel, [shape(length, width, dtype=BF16), shape(8, width)])(
            sums, gb, proj, summary, par
        )

    def send(g, mate, w4, wm):
        out = call(send_kernel, shape(length, width, dtype=BF16))(g, mate, w4, wm)
        out, g, mate = lax.optimization_barrier((out, g, mate))
        got = swap(out, 2, "neur")
        keep = call(keep_kernel, shape(length, width))(g, mate, w4, wm)
        return out, keep, got

    half = width // 2

    def parts_shape(*lead):
        return shape(*lead, half, width, dtype=BF16)

    def weight_parts(fine, *operands):
        if peers != 8:
            return call(functools.partial(weight_kernel, False), parts_shape(8))(*operands)
        return call(
            functools.partial(weight_kernel, True),
            [parts_shape()] * 8 if fine else [parts_shape(4)] * 2,
            [pltpu.VMEM((8, half, width), BF16)],
        )(*operands)

    def weights(shares):
        if peers != 8:
            return call(functools.partial(spread_kernel, False), shape(4 * real, real))(shares)
        return call(
            functools.partial(spread_kernel, True),
            shape(4 * real, real),
            [pltpu.VMEM((8, half, width), BF16)],
        )(*gather_shares(shares))

    def together(*values):
        return lax.optimization_barrier(values)

    first_x, first_proj, first_stats, first_w, give, first_par = project(
        tokens, w_first, (gain_first, shift_first, decay_first)
    )
    first_out, first_wide, first_sum = call(
        forward_kernel,
        [shape(length, real, dtype=BF16), shape(length, width), shape(8, width)],
        scans)(first_stats, first_proj, first_par)

    second_x, second_proj, second_stats, second_w, (first_mate, second_mate), second_par = project(
        first_out, w_second, (gain_second, shift_second, decay_second), give
    )
    second_out, second_gb, second_sums, second_sum, new_mean, new_var = call(
        turn_kernel,
        [
            shape(length, real, dtype=BF16),
            shape(length, width),
            shape(peers, 8, width),
            shape(8, width),
            shape(2, real),
            shape(2, real),
        ],
        scans
        + grads
        + [
            pltpu.VMEM((length, real), BF16),
            pltpu.VMEM((2, real), F32),
            pltpu.VMEM((2, real), F32),
            pltpu.SemaphoreType.DMA((3,)),
        ],
        in_specs=[pl.BlockSpec(memory_space=pltpu.VMEM)] * 4 + [pl.BlockSpec(memory_space=pl.ANY)] * 3,
    )(second_stats, second_proj, second_par, first_sum, cotangent, running_mean, running_var)

    def after(x, *earlier):
        return lax.optimization_barrier((x, earlier))[0]

    second_sums = share(second_sums)
    second_g, second_total = gradient(second_sums, second_gb, second_proj, second_sum, second_par)
    mate = swap(second_g, 1, "neur")
    second_parts = weight_parts(False, *second_x, second_g, second_sum, second_total)
    mate, second_parts = together(mate, second_parts)
    out, keep, got = send(second_g, mate, second_w, second_mate)
    if peers == 8:
        parcel = swap(second_parts[1], LEVEL[4])
    first_gb, first_sums = call(
        back_kernel, [shape(length, width), shape(peers, 8, width)], scans + grads
    )(keep, got, first_proj, first_wide, first_sum, first_par)
    if peers == 8:
        mine, give = call(halve_kernel, [shape(2, half, width), parts_shape(2)])(
            second_parts[0], after(parcel, first_gb)
        )
        parcel = swap(give, LEVEL[2])
    first_sums = share(first_sums)
    first_g, first_total = gradient(first_sums, first_gb, first_proj, first_sum, first_par)
    mate = swap(first_g, 1, "neur")
    first_parts = weight_parts(True, *first_x, first_g, first_sum, first_total)
    mate, first_parts = together(mate, first_parts)
    out, keep, got = send(first_g, mate, first_w, first_mate)
    if peers == 8:
        part, parcels = send_shares(first_parts)
        mine, give = call(halve_kernel, [shape(1, half, width), parts_shape(1)])(
            mine, after(parcel, first_parts)
        )
        second_share = half_sum(*after((mine[0], swap(give[0], LEVEL[1])), keep))
        first_share = half_sum(*quarter_shares(*halve_shares(part, parcels)))
    else:
        second_share, first_share = lax.psum((second_parts, first_parts), "seq")
    grad_w_first = weights(first_share)
    grad_w_second = weights(second_share)
    input_grad = (keep + got.astype(F32))[:, :real]

    def pair(row):
        return jnp.stack([first_total[row, :real], second_total[row, :real]])

    return (
        first_out[None],
        second_out[None],
        input_grad[None],
        grad_w_first,
        grad_w_second,
        pair(1),
        pair(0),
        pair(2),
        new_mean,
        new_var,
    )


def solution(mesh):
    rows, line, flat = P("seq", None, "neur"), P("neur"), P(None, "neur")
    return jax.shard_map(
        functools.partial(per_device, mesh.shape["seq"]),
        mesh=mesh,
        in_specs=(rows, flat, line, line, line, flat, line, line, line, rows, flat, flat),
        out_specs=(rows, rows, rows) + (flat,) * 7,
        check_vma=False,
    )
```

time: 240 us -> 220 us (0.917)
  Pallas kernels: 67.9 us -> 35.1 us
  waiting for transfers between devices: 86.5 us -> 104 us
  local copies, waits for them, and re-layouts: 9 us -> 3.86 us
  starting transfers between devices: 26.5 us -> 29.6 us
    pallas_call x16 -> x18, Pallas kernels: 45.4 us -> 20.2 us  [the longest x2 5.04 us: weight_parts(): call(functools.partial(weight_kernel, True), [parts_shape()] * 8 if fine...]
    ppermute x40 -> x36, waiting for transfers between devices: 86.5 us -> 104 us  [swap(): return lax.ppermute(x, axis, [(i, i ^ bit) for i in range(n)])]
    unnamed x54 -> x26, local copies, waits for them, and re-layouts: 8.99 us -> 3.85 us
    ppermute x40 -> x36, starting transfers between devices: 26.5 us -> 29.6 us  [swap(): return lax.ppermute(x, axis, [(i, i ^ bit) for i in range(n)])]
    pallas_call x1, Pallas kernels: 10.2 us -> 7.4 us  [per_device(): call(turn_kernel, [shape(length, real, dtype=BF16), shape(length, width),...]
    pallas_call x1, Pallas kernels: 7.71 us -> 5.1 us  [per_device(): call(forward_kernel, [shape(length, real, dtype=BF16), shape(length, widt...]
  transfers between devices with their start and end apart: 40 -> 36, of which waited for: 22 -> 24; matrix products, arithmetic and copies ran while one was open for 2% -> 1% of each run, Pallas kernels for 16% -> 7%
where the time goes in v2:
time: 220 us; the launch traced here: 219 us
  waiting for transfers between devices  104 us (47%)
  blocking collectives  42.9 us (20%)
  Pallas kernels  35.1 us (16%)
  starting transfers between devices  29.6 us (13%)
  local copies, waits for them, and re-layouts  3.86 us (2%)
  other arithmetic  2.97 us (1%)
    ppermute x36, waiting for transfers between devices, swap(): return lax.ppermute(x, axis, [(i, i ^ bit) for i in range(n)])  104 us
    all_to_all x4, blocking collectives, share(): return lax.all_to_all(stats, 'seq', 0, 0, tiled=True)  42.9 us
    ppermute x36, starting transfers between devices, swap(): return lax.ppermute(x, axis, [(i, i ^ bit) for i in range(n)])  29.6 us
    pallas_call x1, Pallas kernels, per_device(): call(turn_kernel, [shape(length, real, dtype=BF16), shape(length, width),...  7.4 us
    pallas_call x1, Pallas kernels, per_device(): call(forward_kernel, [shape(length, real, dtype=BF16), shape(length, widt...  5.1 us
    pallas_call x2, Pallas kernels, weight_parts(): call(functools.partial(weight_kernel, True), [parts_shape()] * 8 if fine...  5.04 us
    pallas_call x2, Pallas kernels, weights(): call(functools.partial(spread_kernel, True), shape(4 * real, real), [pltp...  4.93 us
  transfers between devices with their start and end apart: 36, of which 24 were waited for; matrix products, arithmetic and copies ran while one was open for 1% of the time, Pallas kernels for 7%

profile of v2, /device:TPU:0, one launch (start us, length us, event | category | flops | bytes accessed | tf_op | source)
XLA Modules:
  0.0 219.2 jit_solution(6394127098362227347)
XLA Ops:
  1.2 2.6 %collective-permute-start = (bf16[704,500]{1,0:T(8,128)(2,1)}, bf16[704,500]{1,0:T(8,128)(2,1)S(1)}, u32[]{:S(2)}, u32[]{:S(2)}) collective-permute-start(bf16[704,500]{1,0:T(8,128)(2,1)} %bitcast.15), channel_id=1, source_target_pairs={{0,2},{1,3},{2,0},{3,1},{4,6},{5,7},{6,4},{7,5},{8,10},{9,11},{10,... | collective-permute-start | bytes 2112008 | tf_op jit(solution)/shard_map/ppermute | solution.py:617
  8.8 11.9 %collective-permute-done.far_ref = bf16[704,500]{1,0:T(8,128)(2,1)S(1)} collective-permute-done((bf16[704,500]{1,0:T(8,128)(2,1)}, bf16[704,500]{1,0:T(8,128)(2,1)S(1)}, u32[]{:S(2)}, u32[]{:S(2)}) %collective-permute-start) | collective-permute-done | bytes 704032 | tf_op jit(solution)/shard_map/ppermute | solution.py:617
  20.7 2.2 collective-permute-done.2.cross_ref
  24.2 13.4 %all_to_all.20.stats_ref = f32[8,8,512]{2,1,0:T(8,128)S(1)} all-to-all(f32[8,8,512]{2,1,0:T(8,128)S(1)} %get-tuple-element.104), channel_id=1, replica_groups=mesh['seq'=8,'neur'=4] {'seq'}, dimensions={0} | all-to-all | bytes 262144 | tf_op jit(solution)/shard_map/all_to_all | solution.py:686
  37.6 5.1 %shard_map.198 = (bf16[704,500]{1,0:T(8,128)(2,1)}, f32[704,512]{1,0:T(8,128)S(1)}, f32[8,512]{1,0:T(8,128)S(1)}) custom-call(f32[8,8,512]{2,1,0:T(8,128)S(1)} %all_to_all.20.stats_ref, f32[704,512]{1,0:T(8,128)S(1)} %get-tuple-element.105.proj_ref, f32[8,512]{1,0:T(8,128)S(1)} %get-tuple-element.106.par_ref), custom_call_target="tpu_custom_call" | custom-call | tf_op jit(solution)/shard_map/pallas_call | solution.py:746
  45.3 2.6 %collective-permute-done.4.mate_ref = bf16[704,500]{1,0:T(8,128)(2,1)S(1)} collective-permute-done((bf16[704,500]{1,0:T(8,128)(2,1)S(1)}, bf16[704,500]{1,0:T(8,128)(2,1)S(1)}, u32[]{:S(2)}, u32[]{:S(2)}) %collective-permute-start.4) | collective-permute-done | bytes 704032 | tf_op jit(solution)/shard_map/ppermute | solution.py:617
  49.0 13.4 %collective-permute-done.3.far_ref = bf16[704,500]{1,0:T(8,128)(2,1)S(1)} collective-permute-done((bf16[704,500]{1,0:T(8,128)(2,1)S(1)}, bf16[704,500]{1,0:T(8,128)(2,1)S(1)}, u32[]{:S(2)}, u32[]{:S(2)}) %collective-permute-start.3) | collective-permute-done | bytes 704032 | tf_op jit(solution)/shard_map/ppermute | solution.py:617
  62.4 2.2 collective-permute-done.7.cross_ref
  65.9 10.0 %all_to_all.21.stats_ref = f32[8,8,512]{2,1,0:T(8,128)S(1)} all-to-all(f32[8,8,512]{2,1,0:T(8,128)S(1)} %get-tuple-element.119), channel_id=1, replica_groups=mesh['seq'=8,'neur'=4] {'seq'}, dimensions={0} | all-to-all | bytes 262144 | tf_op jit(solution)/shard_map/all_to_all | solution.py:686
  75.8 7.4 %shard_map.202 = (bf16[704,500]{1,0:T(8,128)(2,1)}, f32[704,512]{1,0:T(8,128)S(1)}, f32[8,8,512]{2,1,0:T(8,128)S(1)}, f32[8,512]{1,0:T(8,128)S(1)}, f32[2,500]{1,0:T(2,128)}, /*index=5*/f32[2,500]{1,0:T(2,128)}) custom-call(f32[8,8,512]{2,1,0:T(8,128)S(1)} %all_to_all.21.stats_ref, f32[704,512]{1,0:T(8,128)S(1)} %get-tuple-element.120.proj_ref, ...), custom_call_target="tpu_custom_call" | custom-call | tf_op jit(solution)/shard_map/pallas_call | solution.py:754
  83.2 9.8 %all_to_all.22.sums_ref = f32[8,8,512]{2,1,0:T(8,128)S(1)} all-to-all(f32[8,8,512]{2,1,0:T(8,128)S(1)} %get-tuple-element.124), channel_id=1, replica_groups=mesh['seq'=8,'neur'=4] {'seq'}, dimensions={0} | all-to-all | bytes 262144 | tf_op jit(solution)/shard_map/all_to_all | solution.py:686
  93.5 2.5 %shard_map.204 = (bf16[4,256,512]{2,1,0:T(8,128)(2,1)S(1)}, bf16[4,256,512]{2,1,0:T(8,128)(2,1)S(1)}) custom-call(bf16[704,500]{1,0:T(8,128)(2,1)S(1)} %copy-done.1, bf16[704,500]{1,0:T(8,128)(2,1)S(1)} %collective-permute-done.4.mate_ref, bf16[704,500]{1,0:T(8,128)(2,1)S(1)} %collective-permute-done.3.far_ref, ...), custom_call_target="tpu_custom_call" | custom-call | tf_op jit(solution)/shard_map/pallas_call | solution.py:725
  99.7 15.9 %collective-permute-done.9.got_ref = bf16[704,512]{1,0:T(8,128)(2,1)S(1)} collective-permute-done((bf16[704,512]{1,0:T(8,128)(2,1)S(1)}, bf16[704,512]{1,0:T(8,128)(2,1)S(1)}, u32[]{:S(2)}, u32[]{:S(2)}) %collective-permute-start.9) | collective-permute-done | bytes 720928 | tf_op jit(solution)/shard_map/ppermute | solution.py:617
  115.6 2.4 %shard_map.207 = (f32[704,512]{1,0:T(8,128)S(1)}, f32[8,8,512]{2,1,0:T(8,128)S(1)}) custom-call(f32[704,512]{1,0:T(8,128)S(1)} %shard_map.206.keep_ref, bf16[704,512]{1,0:T(8,128)(2,1)S(1)} %collective-permute-done.9.got_ref, f32[704,512]{1,0:T(8,128)S(1)} %get-tuple-element.105.proj_ref, f32[704,512]{1,0:T(8,128)S(1)} %get-tuple-element.136.wide_ref, ...), custom_call_target="tpu_custom_call" | custom-call | tf_op jit(solution)/shard_map/pallas_call | solution.py:786
  118.0 9.7 %all_to_all.23.sums_ref = f32[8,8,512]{2,1,0:T(8,128)S(1)} all-to-all(f32[8,8,512]{2,1,0:T(8,128)S(1)} %get-tuple-element.137), channel_id=1, replica_groups=mesh['seq'=8,'neur'=4] {'seq'}, dimensions={0} | all-to-all | bytes 262144 | tf_op jit(solution)/shard_map/all_to_all | solution.py:686
  128.5 2.5 %shard_map.209 = (bf16[256,512]{1,0:T(8,128)(2,1)S(1)}, bf16[256,512]{1,0:T(8,128)(2,1)S(1)}, bf16[256,512]{1,0:T(8,128)(2,1)S(1)}, bf16[256,512]{1,0:T(8,128)(2...) custom-call(bf16[704,500]{1,0:T(8,128)(2,1)S(1)} %bitcast.17, ...), custom_call_target="tpu_custom_call" | custom-call | tf_op jit(solution)/shard_map/pallas_call | solution.py:725
  134.5 5.8 %collective-permute-done.16 = bf16[256,512]{1,0:T(8,128)(2,1)S(1)} collective-permute-done((bf16[256,512]{1,0:T(8,128)(2,1)S(1)}, bf16[256,512]{1,0:T(8,128)(2,1)S(1)}, u32[]{:S(2)}, u32[]{:S(2)}) %collective-permute-start.16) | collective-permute-done | bytes 262176 | tf_op jit(solution)/shard_map/ppermute | solution.py:617
  143.6 2.2 %collective-permute-done.13 = bf16[256,512]{1,0:T(8,128)(2,1)S(1)} collective-permute-done((bf16[256,512]{1,0:T(8,128)(2,1)S(1)}, bf16[256,512]{1,0:T(8,128)(2,1)S(1)}, u32[]{:S(2)}, u32[]{:S(2)}) %collective-permute-start.13) | collective-permute-done | bytes 262176 | tf_op jit(solution)/shard_map/ppermute | solution.py:617
  145.9 2.1 collective-permute-start.14
  148.0 3.4 %collective-permute-done.15 = bf16[256,512]{1,0:T(8,128)(2,1)S(1)} collective-permute-done((bf16[256,512]{1,0:T(8,128)(2,1)S(1)}, bf16[256,512]{1,0:T(8,128)(2,1)S(1)}, u32[]{:S(2)}, u32[]{:S(2)}) %collective-permute-start.15) | collective-permute-done | bytes 262176 | tf_op jit(solution)/shard_map/ppermute | solution.py:617
  155.8 3.4 %collective-permute-done.28 = bf16[256,512]{1,0:T(8,128)(2,1)S(1)} collective-permute-done((bf16[256,512]{1,0:T(8,128)(2,1)S(1)}, bf16[256,512]{1,0:T(8,128)(2,1)S(1)}, u32[]{:S(2)}, u32[]{:S(2)}) %collective-permute-start.28) | collective-permute-done | bytes 262176 | tf_op jit(solution)/shard_map/ppermute | solution.py:617
  165.0 5.5 %collective-permute-done.18 = bf16[256,512]{1,0:T(8,128)(2,1)S(1)} collective-permute-done((bf16[256,512]{1,0:T(8,128)(2,1)S(1)}, bf16[256,512]{1,0:T(8,128)(2,1)S(1)}, u32[]{:S(2)}, u32[]{:S(2)}) %collective-permute-start.18) | collective-permute-done | bytes 262176 | tf_op jit(solution)/shard_map/ppermute | solution.py:617
  172.0 2.2 %collective-permute-done.30.refs_2_ = bf16[256,512]{1,0:T(8,128)(2,1)S(1)} collective-permute-done((bf16[256,512]{1,0:T(8,128)(2,1)S(1)}, bf16[256,512]{1,0:T(8,128)(2,1)S(1)}, u32[]{:S(2)}, u32[]{:S(2)}) %collective-permute-start.30) | collective-permute-done | bytes 262176 | tf_op jit(solution)/shard_map/ppermute | solution.py:617
  176.2 5.6 %collective-permute-done.29.refs_1_ = bf16[256,512]{1,0:T(8,128)(2,1)S(1)} collective-permute-done((bf16[256,512]{1,0:T(8,128)(2,1)S(1)}, bf16[256,512]{1,0:T(8,128)(2,1)S(1)}, u32[]{:S(2)}, u32[]{:S(2)}) %collective-permute-start.29) | collective-permute-done | bytes 262176 | tf_op jit(solution)/shard_map/ppermute | solution.py:617
  183.0 2.5 %collective-permute-done.20.refs_2_ = bf16[256,512]{1,0:T(8,128)(2,1)S(1)} collective-permute-done((bf16[256,512]{1,0:T(8,128)(2,1)S(1)}, bf16[256,512]{1,0:T(8,128)(2,1)S(1)}, u32[]{:S(2)}, u32[]{:S(2)}) %collective-permute-start.20) | collective-permute-done | bytes 262176 | tf_op jit(solution)/shard_map/ppermute | solution.py:617
  185.8 5.6 %collective-permute-done.19.refs_1_ = bf16[256,512]{1,0:T(8,128)(2,1)S(1)} collective-permute-done((bf16[256,512]{1,0:T(8,128)(2,1)S(1)}, bf16[256,512]{1,0:T(8,128)(2,1)S(1)}, u32[]{:S(2)}, u32[]{:S(2)}) %collective-permute-start.19) | collective-permute-done | bytes 262176 | tf_op jit(solution)/shard_map/ppermute | solution.py:617
  195.7 3.3 %collective-permute-done.22.refs_3_ = bf16[256,512]{1,0:T(8,128)(2,1)S(1)} collective-permute-done((bf16[256,512]{1,0:T(8,128)(2,1)S(1)}, bf16[256,512]{1,0:T(8,128)(2,1)S(1)}, u32[]{:S(2)}, u32[]{:S(2)}) %collective-permute-start.22) | collective-permute-done | bytes 262176 | tf_op jit(solution)/shard_map/ppermute | solution.py:617
  201.8 5.6 %collective-permute-done.35.refs_7_ = bf16[256,512]{1,0:T(8,128)(2,1)S(1)} collective-permute-done((bf16[256,512]{1,0:T(8,128)(2,1)S(1)}, bf16[256,512]{1,0:T(8,128)(2,1)S(1)}, u32[]{:S(2)}, u32[]{:S(2)}) %collective-permute-start.35) | collective-permute-done | bytes 262176 | tf_op jit(solution)/shard_map/ppermute | solution.py:617
  207.5 2.5 %shard_map.215 = f32[2000,500]{1,0:T(8,128)} custom-call(bf16[256,512]{1,0:T(8,128)(2,1)S(1)} %add_convert_fusion.refs_0_, bf16[256,512]{1,0:T(8,128)(2,1)S(1)} %collective-permute-done.29.refs_1_, bf16[256,512]{1,0:T(8,128)(2,1)S(1)} %collective-permute-done.30.refs_2_, bf16[256,512]{1,0:T(8,128)(2,1)S(1)} %collective-permute-done.32.refs_3_, ...), custom_call_target="tpu_custom_call" | custom-call | tf_op jit(solution)/shard_map/pallas_call | solution.py:734
  209.9 3.2 %collective-permute-done.24.refs_5_ = bf16[256,512]{1,0:T(8,128)(2,1)S(1)} collective-permute-done((bf16[256,512]{1,0:T(8,128)(2,1)S(1)}, bf16[256,512]{1,0:T(8,128)(2,1)S(1)}, u32[]{:S(2)}, u32[]{:S(2)}) %collective-permute-start.24) | collective-permute-done | bytes 262176 | tf_op jit(solution)/shard_map/ppermute | solution.py:617
  213.1 3.7 %collective-permute-done.25.refs_7_ = bf16[256,512]{1,0:T(8,128)(2,1)S(1)} collective-permute-done((bf16[256,512]{1,0:T(8,128)(2,1)S(1)}, bf16[256,512]{1,0:T(8,128)(2,1)S(1)}, u32[]{:S(2)}, u32[]{:S(2)}) %collective-permute-start.25) | collective-permute-done | bytes 262176 | tf_op jit(solution)/shard_map/ppermute | solution.py:617
  216.8 2.5 %shard_map.212 = f32[2000,500]{1,0:T(8,128)} custom-call(bf16[256,512]{1,0:T(8,128)(2,1)S(1)} %add_convert_fusion.1.refs_0_, bf16[256,512]{1,0:T(8,128)(2,1)S(1)} %collective-permute-done.19.refs_1_, bf16[256,512]{1,0:T(8,128)(2,1)S(1)} %collective-permute-done.20.refs_2_, bf16[256,512]{1,0:T(8,128)(2,1)S(1)} %collective-permute-done.22.refs_3_, ...), custom_call_target="tpu_custom_call" | custom-call | tf_op jit(solution)/shard_map/pallas_call | solution.py:734
  (101 shorter events, 45.6 us)
Async XLA Ops:
  0.7 7.0 %collective-permute-start.1 = (bf16[704,500]{1,0:T(8,128)(2,1)}, bf16[704,500]{1,0:T(8,128)(2,1)S(1)}, u32[]{:S(2)}, u32[]{:S(2)}) collective-permute-start(bf16[704,500]{1,0:T(8,128)(2,1)} %bitcast.14), channel_id=1, source_target_pairs={{0,1},{1,0},{2,3},{3,2},{4,5},{5,4},{6,7},{7,6},{8,9},{9,8},{10,11... | collective-permute-start | bytes 2112008 | tf_op jit(solution)/shard_map/ppermute | solution.py:617
  1.2 19.5 %collective-permute-start = (bf16[704,500]{1,0:T(8,128)(2,1)}, bf16[704,500]{1,0:T(8,128)(2,1)S(1)}, u32[]{:S(2)}, u32[]{:S(2)}) collective-permute-start(bf16[704,500]{1,0:T(8,128)(2,1)} %bitcast.15), channel_id=1, source_target_pairs={{0,2},{1,3},{2,0},{3,1},{4,6},{5,7},{6,4},{7,5},{8,10},{9,11},{10,... | collective-permute-start | bytes 2112008 | tf_op jit(solution)/shard_map/ppermute | solution.py:617
  42.7 19.7 %collective-permute-start.5 = (bf16[2,512,512]{2,1,0:T(8,128)(2,1)S(1)}, bf16[2,512,512]{2,1,0:T(8,128)(2,1)S(1)}, u32[]{:S(2)}, u32[]{:S(2)}) collective-permute-start(bf16[2,512,512]{2,1,0:T(8,128)(2,1)S(1)} %get-tuple-element.113), channel_id=1, source_target_pairs={{0,1},{1,0},{2,3},{3,2},{4,5},{5,4},{6,7},{7,6},{8,9},{9,8},{10,11... | collective-permute-start | bytes 3145736 | tf_op jit(solution)/shard_map/ppermute | solution.py:617
  43.1 19.3 %collective-permute-start.6 = (bf16[2,512,512]{2,1,0:T(8,128)(2,1)S(1)}, bf16[2,512,512]{2,1,0:T(8,128)(2,1)S(1)}, u32[]{:S(2)}, u32[]{:S(2)}) collective-permute-start(bf16[2,512,512]{2,1,0:T(8,128)(2,1)S(1)} %get-tuple-element.115), channel_id=1, source_target_pairs={{0,1},{1,0},{2,3},{3,2},{4,5},{5,4},{6,7},{7,6},{8,9},{9,8},{10,11... | collective-permute-start | bytes 3145736 | tf_op jit(solution)/shard_map/ppermute | solution.py:617
  43.8 4.1 %collective-permute-start.4 = (bf16[704,500]{1,0:T(8,128)(2,1)S(1)}, bf16[704,500]{1,0:T(8,128)(2,1)S(1)}, u32[]{:S(2)}, u32[]{:S(2)}) collective-permute-start(bf16[704,500]{1,0:T(8,128)(2,1)S(1)} %copy-done.1), channel_id=1, source_target_pairs={{0,1},{1,0},{2,3},{3,2},{4,5},{5,4},{6,7},{7,6},{8,9},{9,8},{10,11... | collective-permute-start | bytes 2112008 | tf_op jit(solution)/shard_map/ppermute | solution.py:617
  43.8 18.5 %collective-permute-start.3 = (bf16[704,500]{1,0:T(8,128)(2,1)S(1)}, bf16[704,500]{1,0:T(8,128)(2,1)S(1)}, u32[]{:S(2)}, u32[]{:S(2)}) collective-permute-start(bf16[704,500]{1,0:T(8,128)(2,1)S(1)} %copy-done.1), channel_id=1, source_target_pairs={{0,2},{1,3},{2,0},{3,1},{4,6},{5,7},{6,4},{7,5},{8,10},{9,11},{10,... | collective-permute-start | bytes 2112008 | tf_op jit(solution)/shard_map/ppermute | solution.py:617
  97.0 18.6 %collective-permute-start.9 = (bf16[704,512]{1,0:T(8,128)(2,1)S(1)}, bf16[704,512]{1,0:T(8,128)(2,1)S(1)}, u32[]{:S(2)}, u32[]{:S(2)}) collective-permute-start(bf16[704,512]{1,0:T(8,128)(2,1)S(1)} %shard_map.205), channel_id=1, source_target_pairs={{0,2},{1,3},{2,0},{3,1},{4,6},{5,7},{6,4},{7,5},{8,10},{9,11},{10,... | collective-permute-start | bytes 2162696 | tf_op jit(solution)/shard_map/ppermute | solution.py:617
  98.6 29.7 %collective-permute-start.26 = (bf16[4,256,512]{2,1,0:T(8,128)(2,1)S(1)}, bf16[4,256,512]{2,1,0:T(8,128)(2,1)S(1)}, u32[]{:S(2)}, u32[]{:S(2)}) collective-permute-start(bf16[4,256,512]{2,1,0:T(8,128)(2,1)S(1)} %get-tuple-element.167), channel_id=1, source_target_pairs={{0,4},{4,0},{8,12},{12,8},{16,20},{20,16},{24,28},{28,24},{1,5},{5... | collective-permute-start | bytes 3145736 | tf_op jit(solution)/shard_map/ppermute | solution.py:617
  128.5 14.8 %collective-permute-start.27 = (bf16[2,256,512]{2,1,0:T(8,128)(2,1)S(1)}, bf16[2,256,512]{2,1,0:T(8,128)(2,1)S(1)}, u32[]{:S(2)}, u32[]{:S(2)}) collective-permute-start(bf16[2,256,512]{2,1,0:T(8,128)(2,1)S(1)} %get-tuple-element.170), channel_id=1, source_target_pairs={{0,8},{4,12},{8,0},{12,4},{16,24},{20,28},{24,16},{28,20},{1,9},{5... | collective-permute-start | bytes 1572872 | tf_op jit(solution)/shard_map/ppermute | solution.py:617
  131.1 9.2 %collective-permute-start.16 = (bf16[256,512]{1,0:T(8,128)(2,1)S(1)}, bf16[256,512]{1,0:T(8,128)(2,1)S(1)}, u32[]{:S(2)}, u32[]{:S(2)}) collective-permute-start(bf16[256,512]{1,0:T(8,128)(2,1)S(1)} %get-tuple-element.161), channel_id=1, source_target_pairs={{0,4},{4,0},{8,12},{12,8},{16,20},{20,16},{24,28},{28,24},{1,5},{5... | collective-permute-start | bytes 786440 | tf_op jit(solution)/shard_map/ppermute | solution.py:617
  132.4 13.4 %collective-permute-start.13 = (bf16[256,512]{1,0:T(8,128)(2,1)S(1)}, bf16[256,512]{1,0:T(8,128)(2,1)S(1)}, u32[]{:S(2)}, u32[]{:S(2)}) collective-permute-start(bf16[256,512]{1,0:T(8,128)(2,1)S(1)} %get-tuple-element.157), channel_id=1, source_target_pairs={{0,4},{4,0},{8,12},{12,8},{16,20},{20,16},{24,28},{28,24},{1,5},{5... | collective-permute-start | bytes 786440 | tf_op jit(solution)/shard_map/ppermute | solution.py:617
  133.2 18.3 %collective-permute-start.15 = (bf16[256,512]{1,0:T(8,128)(2,1)S(1)}, bf16[256,512]{1,0:T(8,128)(2,1)S(1)}, u32[]{:S(2)}, u32[]{:S(2)}) collective-permute-start(bf16[256,512]{1,0:T(8,128)(2,1)S(1)} %get-tuple-element.159), channel_id=1, source_target_pairs={{0,4},{4,0},{8,12},{12,8},{16,20},{20,16},{24,28},{28,24},{1,5},{5... | collective-permute-start | bytes 786440 | tf_op jit(solution)/shard_map/ppermute | solution.py:617
  140.3 11.5 %collective-permute-start.17 = (bf16[256,512]{1,0:T(8,128)(2,1)S(1)}, bf16[256,512]{1,0:T(8,128)(2,1)S(1)}, u32[]{:S(2)}, u32[]{:S(2)}) collective-permute-start(bf16[256,512]{1,0:T(8,128)(2,1)S(1)} %add_convert_fusion.3), channel_id=1, source_target_pairs={{0,8},{4,12},{8,0},{12,4},{16,24},{20,28},{24,16},{28,20},{1,9},{5... | collective-permute-start | bytes 786440 | tf_op jit(solution)/shard_map/ppermute | solution.py:617
  142.4 18.2 %collective-permute-start.12 = (bf16[256,512]{1,0:T(8,128)(2,1)S(1)}, bf16[256,512]{1,0:T(8,128)(2,1)S(1)}, u32[]{:S(2)}, u32[]{:S(2)}) collective-permute-start(bf16[256,512]{1,0:T(8,128)(2,1)S(1)} %get-tuple-element.155), channel_id=1, source_target_pairs={{0,4},{4,0},{8,12},{12,8},{16,20},{20,16},{24,28},{28,24},{1,5},{5... | collective-permute-start | bytes 786440 | tf_op jit(solution)/shard_map/ppermute | solution.py:617
  143.3 15.9 %collective-permute-start.28 = (bf16[256,512]{1,0:T(8,128)(2,1)S(1)}, bf16[256,512]{1,0:T(8,128)(2,1)S(1)}, u32[]{:S(2)}, u32[]{:S(2)}) collective-permute-start(bf16[256,512]{1,0:T(8,128)(2,1)S(1)} %bitcast.27), channel_id=1, source_target_pairs={{0,16},{4,20},{8,24},{12,28},{16,0},{20,4},{24,8},{28,12},{1,17},{... | collective-permute-start | bytes 786440 | tf_op jit(solution)/shard_map/ppermute | solution.py:617
  145.9 17.1 %collective-permute-start.14 = (bf16[256,512]{1,0:T(8,128)(2,1)S(1)}, bf16[256,512]{1,0:T(8,128)(2,1)S(1)}, u32[]{:S(2)}, u32[]{:S(2)}) collective-permute-start(bf16[256,512]{1,0:T(8,128)(2,1)S(1)} %add_convert_fusion.4), channel_id=1, source_target_pairs={{0,8},{4,12},{8,0},{12,4},{16,24},{20,28},{24,16},{28,20},{1,9},{5... | collective-permute-start | bytes 786440 | tf_op jit(solution)/shard_map/ppermute | solution.py:617
  151.9 18.6 %collective-permute-start.18 = (bf16[256,512]{1,0:T(8,128)(2,1)S(1)}, bf16[256,512]{1,0:T(8,128)(2,1)S(1)}, u32[]{:S(2)}, u32[]{:S(2)}) collective-permute-start(bf16[256,512]{1,0:T(8,128)(2,1)S(1)} %add_convert_fusion.2), channel_id=1, source_target_pairs={{0,16},{4,20},{8,24},{12,28},{16,0},{20,4},{24,8},{28,12},{1,17},{... | collective-permute-start | bytes 786440 | tf_op jit(solution)/shard_map/ppermute | solution.py:617
  159.3 12.6 %collective-permute-start.31 = (bf16[256,512]{1,0:T(8,128)(2,1)S(1)}, bf16[256,512]{1,0:T(8,128)(2,1)S(1)}, u32[]{:S(2)}, u32[]{:S(2)}) collective-permute-start(bf16[256,512]{1,0:T(8,128)(2,1)S(1)} %add_convert_fusion.refs_0_), channel_id=1, source_target_pairs={{0,4},{4,0},{8,12},{12,8},{16,20},{20,16},{24,28},{28,24},{1,5},{5... | collective-permute-start | bytes 786440 | tf_op jit(solution)/shard_map/ppermute | solution.py:617
  160.6 13.6 %collective-permute-start.30 = (bf16[256,512]{1,0:T(8,128)(2,1)S(1)}, bf16[256,512]{1,0:T(8,128)(2,1)S(1)}, u32[]{:S(2)}, u32[]{:S(2)}) collective-permute-start(bf16[256,512]{1,0:T(8,128)(2,1)S(1)} %add_convert_fusion.refs_0_), channel_id=1, source_target_pairs={{0,8},{4,12},{8,0},{12,4},{16,24},{20,28},{24,16},{28,20},{1,9},{5... | collective-permute-start | bytes 786440 | tf_op jit(solution)/shard_map/ppermute | solution.py:617
  160.6 38.8 %collective-permute-start.11 = (bf16[704,512]{1,0:T(8,128)(2,1)S(1)}, bf16[704,512]{1,0:T(8,128)(2,1)S(1)}, u32[]{:S(2)}, u32[]{:S(2)}) collective-permute-start(bf16[704,512]{1,0:T(8,128)(2,1)S(1)} %shard_map.210), channel_id=1, source_target_pairs={{0,2},{1,3},{2,0},{3,1},{4,6},{5,7},{6,4},{7,5},{8,10},{9,11},{10,... | collective-permute-start | bytes 2162696 | tf_op jit(solution)/shard_map/ppermute | solution.py:617
  163.1 18.8 %collective-permute-start.29 = (bf16[256,512]{1,0:T(8,128)(2,1)S(1)}, bf16[256,512]{1,0:T(8,128)(2,1)S(1)}, u32[]{:S(2)}, u32[]{:S(2)}) collective-permute-start(bf16[256,512]{1,0:T(8,128)(2,1)S(1)} %add_convert_fusion.refs_0_), channel_id=1, source_target_pairs={{0,16},{4,20},{8,24},{12,28},{16,0},{20,4},{24,8},{28,12},{1,17},{... | collective-permute-start | bytes 786440 | tf_op jit(solution)/shard_map/ppermute | solution.py:617
  170.7 12.4 %collective-permute-start.21 = (bf16[256,512]{1,0:T(8,128)(2,1)S(1)}, bf16[256,512]{1,0:T(8,128)(2,1)S(1)}, u32[]{:S(2)}, u32[]{:S(2)}) collective-permute-start(bf16[256,512]{1,0:T(8,128)(2,1)S(1)} %add_convert_fusion.1.refs_0_), channel_id=1, source_target_pairs={{0,4},{4,0},{8,12},{12,8},{16,20},{20,16},{24,28},{28,24},{1,5},{5... | collective-permute-start | bytes 786440 | tf_op jit(solution)/shard_map/ppermute | solution.py:617
  172.0 13.6 %collective-permute-start.20 = (bf16[256,512]{1,0:T(8,128)(2,1)S(1)}, bf16[256,512]{1,0:T(8,128)(2,1)S(1)}, u32[]{:S(2)}, u32[]{:S(2)}) collective-permute-start(bf16[256,512]{1,0:T(8,128)(2,1)S(1)} %add_convert_fusion.1.refs_0_), channel_id=1, source_target_pairs={{0,8},{4,12},{8,0},{12,4},{16,24},{20,28},{24,16},{28,20},{1,9},{5... | collective-permute-start | bytes 786440 | tf_op jit(solution)/shard_map/ppermute | solution.py:617
  174.2 17.2 %collective-permute-start.19 = (bf16[256,512]{1,0:T(8,128)(2,1)S(1)}, bf16[256,512]{1,0:T(8,128)(2,1)S(1)}, u32[]{:S(2)}, u32[]{:S(2)}) collective-permute-start(bf16[256,512]{1,0:T(8,128)(2,1)S(1)} %add_convert_fusion.1.refs_0_), channel_id=1, source_target_pairs={{0,16},{4,20},{8,24},{12,28},{16,0},{20,4},{24,8},{28,12},{1,17},{... | collective-permute-start | bytes 786440 | tf_op jit(solution)/shard_map/ppermute | solution.py:617
  181.8 10.8 %collective-permute-start.33 = (bf16[256,512]{1,0:T(8,128)(2,1)S(1)}, bf16[256,512]{1,0:T(8,128)(2,1)S(1)}, u32[]{:S(2)}, u32[]{:S(2)}) collective-permute-start(bf16[256,512]{1,0:T(8,128)(2,1)S(1)} %collective-permute-done.30.refs_2_), channel_id=1, source_target_pairs={{0,4},{4,0},{8,12},{12,8},{16,20},{20,16},{24,28},{28,24},{1,5},{5... | collective-permute-start | bytes 786440 | tf_op jit(solution)/shard_map/ppermute | solution.py:617
  183.0 10.6 %collective-permute-start.32 = (bf16[256,512]{1,0:T(8,128)(2,1)S(1)}, bf16[256,512]{1,0:T(8,128)(2,1)S(1)}, u32[]{:S(2)}, u32[]{:S(2)}) collective-permute-start(bf16[256,512]{1,0:T(8,128)(2,1)S(1)} %collective-permute-done.29.refs_1_), channel_id=1, source_target_pairs={{0,8},{4,12},{8,0},{12,4},{16,24},{20,28},{24,16},{28,20},{1,9},{5... | collective-permute-start | bytes 786440 | tf_op jit(solution)/shard_map/ppermute | solution.py:617
  185.5 9.7 %collective-permute-start.23 = (bf16[256,512]{1,0:T(8,128)(2,1)S(1)}, bf16[256,512]{1,0:T(8,128)(2,1)S(1)}, u32[]{:S(2)}, u32[]{:S(2)}) collective-permute-start(bf16[256,512]{1,0:T(8,128)(2,1)S(1)} %collective-permute-done.20.refs_2_), channel_id=1, source_target_pairs={{0,4},{4,0},{8,12},{12,8},{16,20},{20,16},{24,28},{28,24},{1,5},{5... | collective-permute-start | bytes 786440 | tf_op jit(solution)/shard_map/ppermute | solution.py:617
  191.4 7.6 %collective-permute-start.22 = (bf16[256,512]{1,0:T(8,128)(2,1)S(1)}, bf16[256,512]{1,0:T(8,128)(2,1)S(1)}, u32[]{:S(2)}, u32[]{:S(2)}) collective-permute-start(bf16[256,512]{1,0:T(8,128)(2,1)S(1)} %collective-permute-done.19.refs_1_), channel_id=1, source_target_pairs={{0,8},{4,12},{8,0},{12,4},{16,24},{20,28},{24,16},{28,20},{1,9},{5... | collective-permute-start | bytes 786440 | tf_op jit(solution)/shard_map/ppermute | solution.py:617
  192.6 9.2 %collective-permute-start.34 = (bf16[256,512]{1,0:T(8,128)(2,1)S(1)}, bf16[256,512]{1,0:T(8,128)(2,1)S(1)}, u32[]{:S(2)}, u32[]{:S(2)}) collective-permute-start(bf16[256,512]{1,0:T(8,128)(2,1)S(1)} %collective-permute-done.29.refs_1_), channel_id=1, source_target_pairs={{0,4},{4,0},{8,12},{12,8},{16,20},{20,16},{24,28},{28,24},{1,5},{5... | collective-permute-start | bytes 786440 | tf_op jit(solution)/shard_map/ppermute | solution.py:617
  193.7 13.8 %collective-permute-start.35 = (bf16[256,512]{1,0:T(8,128)(2,1)S(1)}, bf16[256,512]{1,0:T(8,128)(2,1)S(1)}, u32[]{:S(2)}, u32[]{:S(2)}) collective-permute-start(bf16[256,512]{1,0:T(8,128)(2,1)S(1)} %collective-permute-done.32.refs_3_), channel_id=1, source_target_pairs={{0,4},{4,0},{8,12},{12,8},{16,20},{20,16},{24,28},{28,24},{1,5},{5... | collective-permute-start | bytes 786440 | tf_op jit(solution)/shard_map/ppermute | solution.py:617
  195.2 17.9 %collective-permute-start.24 = (bf16[256,512]{1,0:T(8,128)(2,1)S(1)}, bf16[256,512]{1,0:T(8,128)(2,1)S(1)}, u32[]{:S(2)}, u32[]{:S(2)}) collective-permute-start(bf16[256,512]{1,0:T(8,128)(2,1)S(1)} %collective-permute-done.19.refs_1_), channel_id=1, source_target_pairs={{0,4},{4,0},{8,12},{12,8},{16,20},{20,16},{24,28},{28,24},{1,5},{5... | collective-permute-start | bytes 786440 | tf_op jit(solution)/shard_map/ppermute | solution.py:617
  199.0 17.7 %collective-permute-start.25 = (bf16[256,512]{1,0:T(8,128)(2,1)S(1)}, bf16[256,512]{1,0:T(8,128)(2,1)S(1)}, u32[]{:S(2)}, u32[]{:S(2)}) collective-permute-start(bf16[256,512]{1,0:T(8,128)(2,1)S(1)} %collective-permute-done.22.refs_3_), channel_id=1, source_target_pairs={{0,4},{4,0},{8,12},{12,8},{16,20},{20,16},{24,28},{28,24},{1,5},{5... | collective-permute-start | bytes 786440 | tf_op jit(solution)/shard_map/ppermute | solution.py:617
  (17 other events, 130.9 us)

commit v3 on v2

--- a/solution.py
+++ b/solution.py
@@ -390,7 +390,7 @@
     lax.fori_loop(0, out_ref.shape[0] // 16, body, 0, unroll=4)
 
 
-def forward_kernel(stats_ref, proj_ref, par_ref, out_ref, wide_ref, sum_ref, drive, state):
+def forward_kernel(stats_ref, proj_ref, par_ref, out_ref, wide_ref, sum_ref, norm_ref, total_ref, drive, state):
     length, width = proj_ref.shape
     tiles = tiles_of(width)
     outs = tiles_of(out_ref.shape[1])
@@ -400,6 +400,15 @@
     clear(state, tiles)
     solve(drive, state, decay, tiles)
     put_states(state, out_ref, outs, wide_ref)
+    total_ref[...] = jnp.zeros(total_ref.shape, F32)
+    total_ref[7:8, :] = length * (sum_ref[3:4, :] - mean) * inverse
+
+    def put_norm(i, _):
+        rows = pl.ds(pl.multiple_of(i * 16, 16), 16)
+        norm_ref[rows, :] = ((proj_ref[rows, :] - mean) * inverse).astype(BF16)
+        return 0
+
+    lax.fori_loop(0, length // 16, put_norm, 0, unroll=4)
 
 
 def turn_kernel(
@@ -467,7 +476,7 @@
 
 
 def back_kernel(
-    keep_ref, got_ref, proj_ref, wide_ref, sum_ref, par_ref, gb_ref, sums_ref, drive, state, grad
+    keep_ref, got_ref, proj_ref, wide_ref, sum_ref, par_ref, gb_ref, sums_ref, own_ref, drive, state, grad
 ):
     length, width = proj_ref.shape
     tiles = tiles_of(width)
@@ -488,6 +497,15 @@
     fill_sigma(drive, state, decay, tiles, length)
     solve_back(grad, drive, decay, tiles)
     finish_back(grad, state, proj_ref, mean, inverse, tiles, gb_ref, sums_ref)
+    scale = gain * inverse
+    average = sums_ref[0, 0:1, :] * (1.0 / length)
+
+    def put_own(i, _):
+        rows = pl.ds(pl.multiple_of(i * 16, 16), 16)
+        own_ref[rows, :] = (scale * (gb_ref[rows, :] - average)).astype(BF16)
+        return 0
+
+    lax.fori_loop(0, length // 16, put_own, 0, unroll=4)
 
 
 def total_of(sums_ref):
@@ -571,19 +589,75 @@
         hold[(2 * k + 1) ^ place, : rest.shape[0], :] = rest
         if not parted:
             hold[2 * k + 1, rest.shape[0] :, :] = jnp.zeros((half - rest.shape[0], width), BF16)
-    count = hold.shape[0] // len(outs) if outs else 0
-    for r, out in enumerate(outs):
-        out[...] = hold[r] if count == 1 else hold[r * count : (r + 1) * count]
-
-
-def halve_kernel(keep_ref, got_ref, mine_ref, give_ref):
-    count = mine_ref.shape[0]
-    for i in range(2 * count):
-        value = wide_sum(keep_ref[i], got_ref[i])
-        if i < count:
-            mine_ref[i] = value
-        else:
-            give_ref[i - count] = value.astype(BF16)
+    if parted:
+        left, right = slice(0, half), slice(half, width)
+        for out, shares, at in zip(
+            outs, ((0, 1, 2, 3), (4, 5, 6, 7), (0, 1, 4, 5), (2, 3, 6, 7)), (left, left, right, right)
+        ):
+            for i, r in enumerate(shares):
+                out[i] = hold[r, :, at]
+
+
+def halve_kernel(left_ref, got_left_ref, right_ref, got_right_ref, *outs):
+    for n, (keep, got) in enumerate(((left_ref, got_left_ref), (right_ref, got_right_ref))):
+        mine, give = outs[2 * n : 2 * n + 2]
+        for i in range(2):
+            mine[i] = wide_sum(keep[i], got[i])
+            give[i] = half_sum(keep[i + 2], got[i + 2])
+
+
+def settle_kernel(
+    length,
+    left_ref,
+    got_left_ref,
+    right_ref,
+    got_right_ref,
+    lean_left_ref,
+    lean_got_left_ref,
+    lean_right_ref,
+    lean_got_right_ref,
+    sums_ref,
+    stats_ref,
+    sum_ref,
+    par_ref,
+    *outs,
+):
+    peers = sums_ref.shape[0]
+    total = total_of(sums_ref)
+    base = total[0:1, :] * (1.0 / (peers * length))
+    scale = par_ref[0:1, :] * sum_ref[2:3, :]
+    lean = scale * total[1:2, :] * (1.0 / (peers * length))
+    place, here = lax.axis_index("seq"), seat()
+    half = left_ref.shape[1]
+    for n, (keep, got, lean_keep, lean_got, other, shares, at) in enumerate((
+        (left_ref, got_left_ref, lean_left_ref, lean_got_left_ref, place ^ LEVEL[4], (0, 1, 2, 3), slice(0, half)),
+        (right_ref, got_right_ref, lean_right_ref, lean_got_right_ref, place ^ LEVEL[2], (0, 1, 4, 5), slice(half, 2 * half)),
+    )):
+        mine, give = outs[2 * n : 2 * n + 2]
+        columns = [
+            (scale * (sums_ref[p, 0:1, :] * (1.0 / length) - base) * length)[:, at] for p in (place, other)
+        ]
+        for i, r in enumerate(shares):
+            share = here ^ r
+            row, low = share >> 1, pl.multiple_of((share & 1) * half, 128)
+            middle = sum_ref[pl.ds(4 + row, 1), pl.ds(low, half)]
+            value = wide_sum(keep[i], got[i]) - lean[:, at] * wide_sum(lean_keep[i], lean_got[i])
+            for p, column in zip((place, other), columns):
+                value = value + outer(stats_ref[p, pl.ds(2 + row, 1), pl.ds(low, half)] - middle, column)
+            if i < 2:
+                mine[i] = value
+            else:
+                give[i - 2] = value.astype(BF16)
+
+
+def quarter_kernel(left_ref, got_left_ref, right_ref, got_right_ref, mine_ref, give_ref):
+    edge = left_ref.shape[2]
+    for keep, got, at in (
+        (left_ref, got_left_ref, slice(0, edge)),
+        (right_ref, got_right_ref, slice(edge, 2 * edge)),
+    ):
+        mine_ref[:, at] = wide_sum(keep[0], got[0])
+        give_ref[:, at] = half_sum(keep[1], got[1])
 
 
 def spread_kernel(parted, *refs):
@@ -625,26 +699,12 @@
     return ((place & 1) << 2) | (place & 2) | ((place >> 2) & 1)
 
 
-def send_shares(shares):
-    part = {(r >> 2 & 1, r >> 1 & 1, r & 1): v for r, v in enumerate(shares)}
-    return part, {q: swap(part[(1,) + q], LEVEL[4]) for q in ((1, 1), (1, 0), (0, 1), (0, 0))}
-
-
-def halve_shares(part, got):
-    mine = {q: wide_sum(part[(0,) + q], v) for q, v in got.items()}
-    away, near = (swap(mine[(1, i)].astype(BF16), LEVEL[2]) for i in (1, 0))
-    return {i: mine[(0, i)] for i in (0, 1)}, away, near
-
-
-def quarter_shares(mine, away, near):
-    return wide_sum(mine[0], near), swap(half_sum(mine[1], away), LEVEL[1])
-
-
-def gather_shares(v):
-    out = {0: v}
-    out[4] = swap(v, LEVEL[4])
-    out[2] = swap(v, LEVEL[2])
-    out[1] = swap(v, LEVEL[1])
+def gather_first(v):
+    return {0: v, 4: swap(v, LEVEL[4]), 2: swap(v, LEVEL[2]), 1: swap(v, LEVEL[1])}
+
+
+def gather_rest(out):
+    out = dict(out)
     out[2], out[4] = lax.optimization_barrier((out[2], out[4]))
     out[6] = swap(out[2], LEVEL[4])
     out[5] = swap(out[1], LEVEL[4])
@@ -685,7 +745,7 @@
     def share(stats):
         return lax.all_to_all(stats, "seq", 0, 0, tiled=True)
 
-    def project(own, w, rows, *gives):
+    def project(own, w, rows, *gives, aside=None):
         far = swap(own, 2, "neur")
         mate = swap(own, 1, "neur")
         w = lax.optimization_barrier((w, own))[0]
@@ -695,12 +755,13 @@
         )(w, *(row[None] for row in rows))
         part, means = call(project_early, [shape(length, width), shape(8, width)])(own, mate, w4)
         gives = [swap(lax.optimization_barrier((g, own))[0], 1, "neur") for g in gives + (give,)] if gives else give
-        far, part, par, gives = lax.optimization_barrier((far, part, par, gives))
+        extra = aside(mate) if aside else ()
+        far, part, par, gives, extra = lax.optimization_barrier((far, part, par, gives, extra))
         cross = swap(far, 1, "neur")
         proj, stats = call(project_late, [shape(length, width), shape(peers, 8, width)])(
             part, means, far, cross, w4
         )
-        return (own, mate, far, cross), proj, share(stats), w4, gives, par
+        return (own, mate, far, cross), proj, share(stats), w4, gives, par, extra
 
     def gradient(sums, gb, proj, summary, par):
         return call(grad_kernel, [shape(length, width, dtype=BF16), shape(8, width)])(
@@ -712,19 +773,19 @@
         out, g, mate = lax.optimization_barrier((out, g, mate))
         got = swap(out, 2, "neur")
         keep = call(keep_kernel, shape(length, width))(g, mate, w4, wm)
-        return out, keep, got
+        return keep, got
 
     half = width // 2
 
     def parts_shape(*lead):
         return shape(*lead, half, width, dtype=BF16)
 
-    def weight_parts(fine, *operands):
+    def weight_parts(*operands):
         if peers != 8:
             return call(functools.partial(weight_kernel, False), parts_shape(8))(*operands)
         return call(
             functools.partial(weight_kernel, True),
-            [parts_shape()] * 8 if fine else [parts_shape(4)] * 2,
+            [shape(4, half, half, dtype=BF16)] * 4,
             [pltpu.VMEM((8, half, width), BF16)],
         )(*operands)
 
@@ -735,21 +796,38 @@
             functools.partial(spread_kernel, True),
             shape(4 * real, real),
             [pltpu.VMEM((8, half, width), BF16)],
-        )(*gather_shares(shares))
+        )(*shares)
 
     def together(*values):
         return lax.optimization_barrier(values)
 
-    first_x, first_proj, first_stats, first_w, give, first_par = project(
+    first_x, first_proj, first_stats, first_w, give, first_par, _ = project(
         tokens, w_first, (gain_first, shift_first, decay_first)
     )
-    first_out, first_wide, first_sum = call(
+    first_out, first_wide, first_sum, first_norm, norm_total = call(
         forward_kernel,
-        [shape(length, real, dtype=BF16), shape(length, width), shape(8, width)],
-        scans)(first_stats, first_proj, first_par)
-
-    second_x, second_proj, second_stats, second_w, (first_mate, second_mate), second_par = project(
-        first_out, w_second, (gain_second, shift_second, decay_second), give
+        [
+            shape(length, real, dtype=BF16),
+            shape(length, width),
+            shape(8, width),
+            shape(length, width, dtype=BF16),
+            shape(8, width),
+        ],
+        scans,
+    )(first_stats, first_proj, first_par)
+
+    def after(x, *earlier):
+        return lax.optimization_barrier((x, earlier))[0]
+
+    def leaning(mate):
+        if peers != 8:
+            return ()
+        norm = after(first_norm, mate)
+        left, give_left, right, give_right = weight_parts(*first_x, norm, first_sum, norm_total)
+        return left, swap(give_left, LEVEL[4]), right, swap(give_right, LEVEL[2])
+
+    second_x, second_proj, second_stats, second_w, (first_mate, second_mate), second_par, lean = project(
+        first_out, w_second, (gain_second, shift_second, decay_second), give, aside=leaning
     )
     second_out, second_gb, second_sums, second_sum, new_mean, new_var = call(
         turn_kernel,
@@ -772,39 +850,52 @@
         in_specs=[pl.BlockSpec(memory_space=pltpu.VMEM)] * 4 + [pl.BlockSpec(memory_space=pl.ANY)] * 3,
     )(second_stats, second_proj, second_par, first_sum, cotangent, running_mean, running_var)
 
-    def after(x, *earlier):
-        return lax.optimization_barrier((x, earlier))[0]
-
     second_sums = share(second_sums)
     second_g, second_total = gradient(second_sums, second_gb, second_proj, second_sum, second_par)
     mate = swap(second_g, 1, "neur")
-    second_parts = weight_parts(False, *second_x, second_g, second_sum, second_total)
+    pairs = [shape(2, half, half), shape(2, half, half, dtype=BF16)] * 2
+    rest = [shape(half, width), parts_shape()]
+    second_parts = weight_parts(*second_x, second_g, second_sum, second_total)
     mate, second_parts = together(mate, second_parts)
-    out, keep, got = send(second_g, mate, second_w, second_mate)
+    keep, got = send(second_g, mate, second_w, second_mate)
     if peers == 8:
-        parcel = swap(second_parts[1], LEVEL[4])
-    first_gb, first_sums = call(
-        back_kernel, [shape(length, width), shape(peers, 8, width)], scans + grads
+        left, give_left, right, give_right = second_parts
+        parcel = after((swap(give_left, LEVEL[4]), swap(give_right, LEVEL[2])), keep)
+        left, give_left, right, give_right = call(halve_kernel, pairs)(left, parcel[0], right, parcel[1])
+        keep, got, left = together(keep, got, left)
+        parcel = swap(give_left, LEVEL[2]), swap(give_right, LEVEL[4])
+    first_gb, first_sums, first_own = call(
+        back_kernel,
+        [shape(length, width), shape(peers, 8, width), shape(length, width, dtype=BF16)],
+        scans + grads,
     )(keep, got, first_proj, first_wide, first_sum, first_par)
     if peers == 8:
-        mine, give = call(halve_kernel, [shape(2, half, width), parts_shape(2)])(
-            second_parts[0], after(parcel, first_gb)
+        second_mine, give = call(quarter_kernel, rest)(left, parcel[0], right, parcel[1])
+        first_sums, second_mine, give = together(first_sums, second_mine, give)
+        left, give_left, right, give_right = weight_parts(
+            *first_x, first_own, first_sum, jnp.zeros((8, width), F32)
         )
-        parcel = swap(give, LEVEL[2])
+        parcel = swap(give_left, LEVEL[4]), swap(give_right, LEVEL[2])
     first_sums = share(first_sums)
+    if peers == 8:
+        first_sums, last, parcel = together(first_sums, swap(give, LEVEL[1]), parcel)
     first_g, first_total = gradient(first_sums, first_gb, first_proj, first_sum, first_par)
     mate = swap(first_g, 1, "neur")
-    first_parts = weight_parts(True, *first_x, first_g, first_sum, first_total)
-    mate, first_parts = together(mate, first_parts)
-    out, keep, got = send(first_g, mate, first_w, first_mate)
     if peers == 8:
-        part, parcels = send_shares(first_parts)
-        mine, give = call(halve_kernel, [shape(1, half, width), parts_shape(1)])(
-            mine, after(parcel, first_parts)
+        left, give_left, right, give_right = call(functools.partial(settle_kernel, length), pairs)(
+            left, parcel[0], right, parcel[1], *lean, first_sums, first_stats, first_sum, first_par
         )
-        second_share = half_sum(*after((mine[0], swap(give[0], LEVEL[1])), keep))
-        first_share = half_sum(*quarter_shares(*halve_shares(part, parcels)))
+        parcel = swap(give_left, LEVEL[2]), swap(give_right, LEVEL[4])
+        mate, left = together(mate, left)
+        keep, got = send(first_g, mate, first_w, first_mate)
+        second_share = gather_first(half_sum(second_mine, last))
+        mine, give = call(quarter_kernel, rest)(left, parcel[0], right, parcel[1])
+        keep, first_share = together(keep, half_sum(mine, swap(give, LEVEL[1])))
+        second_share = gather_rest(second_share)
+        first_share = gather_rest(gather_first(first_share))
     else:
+        first_parts = weight_parts(*first_x, first_g, first_sum, first_total)
+        keep, got = send(first_g, mate, first_w, first_mate)
         second_share, first_share = lax.psum((second_parts, first_parts), "seq")
     grad_w_first = weights(first_share)
     grad_w_second = weights(second_share)

time: 220 us -> 216 us (0.982)
  waiting for transfers between devices: 104 us -> 83.9 us
  blocking collectives: 42.9 us -> 53.2 us
  Pallas kernels: 35.1 us -> 38.9 us
    ppermute x36 -> x38, waiting for transfers between devices: 104 us -> 83.9 us  [swap(): return lax.ppermute(x, axis, [(i, i ^ bit) for i in range(n)])]
    all_to_all x4, blocking collectives: 42.9 us -> 53.2 us  [share(): return lax.all_to_all(stats, 'seq', 0, 0, tiled=True)]
    pallas_call x5 -> x8, Pallas kernels: 7.75 us -> 11.4 us  [the longest x3 7.55 us: weight_parts(): call(functools.partial(weight_kernel, True), [shape(4, half, half, dtype=...]
    ppermute x36 -> x38, starting transfers between devices: 29.6 us -> 31.6 us  [swap(): return lax.ppermute(x, axis, [(i, i ^ bit) for i in range(n)])]
  transfers between devices with their start and end apart: 36 -> 38, of which waited for: 24 -> 15; matrix products, arithmetic and copies ran while one was open for 1% -> 1% of each run, Pallas kernels for 7% -> 9%
where the time goes in v3:
time: 216 us; the launch traced here: 215 us
  waiting for transfers between devices  83.9 us (39%)
  blocking collectives  53.2 us (25%)
  Pallas kernels  38.9 us (18%)
  starting transfers between devices  31.6 us (15%)
  local copies, waits for them, and re-layouts  3.78 us (2%)
  other arithmetic  2.67 us (1%)
    ppermute x38, waiting for transfers between devices, swap(): return lax.ppermute(x, axis, [(i, i ^ bit) for i in range(n)])  83.9 us
    all_to_all x4, blocking collectives, share(): return lax.all_to_all(stats, 'seq', 0, 0, tiled=True)  53.2 us
    ppermute x38, starting transfers between devices, swap(): return lax.ppermute(x, axis, [(i, i ^ bit) for i in range(n)])  31.6 us
    pallas_call x3, Pallas kernels, weight_parts(): call(functools.partial(weight_kernel, True), [shape(4, half, half, dtype=...  7.55 us
    pallas_call x1, Pallas kernels, per_device(): call(turn_kernel, [shape(length, real, dtype=BF16), shape(length, width),...  7.4 us
    pallas_call x1, Pallas kernels, per_device(): call(forward_kernel, [shape(length, real, dtype=BF16), shape(length, widt...  5.28 us
    pallas_call x2, Pallas kernels, weights(): call(functools.partial(spread_kernel, True), shape(4 * real, real), [pltp...  4.93 us
  transfers between devices with their start and end apart: 38, of which 15 were waited for; matrix products, arithmetic and copies ran while one was open for 1% of the time, Pallas kernels for 9%

profile of v3, /device:TPU:0, one launch (start us, length us, event | category | flops | bytes accessed | tf_op | source)
XLA Modules:
  0.0 215.2 jit_solution(2476045832352975538)
XLA Ops:
  1.2 2.6 %collective-permute-start = (bf16[704,500]{1,0:T(8,128)(2,1)}, bf16[704,500]{1,0:T(8,128)(2,1)S(1)}, u32[]{:S(2)}, u32[]{:S(2)}) collective-permute-start(bf16[704,500]{1,0:T(8,128)(2,1)} %bitcast.13), channel_id=1, source_target_pairs={{0,2},{1,3},{2,0},{3,1},{4,6},{5,7},{6,4},{7,5},{8,10},{9,11},{10,... | collective-permute-start | bytes 2112008 | tf_op jit(solution)/shard_map/ppermute | solution.py:691
  3.7 1.6 copy-done.2
  8.8 11.9 %collective-permute-done.far_ref = bf16[704,500]{1,0:T(8,128)(2,1)S(1)} collective-permute-done((bf16[704,500]{1,0:T(8,128)(2,1)}, bf16[704,500]{1,0:T(8,128)(2,1)S(1)}, u32[]{:S(2)}, u32[]{:S(2)}) %collective-permute-start) | collective-permute-done | bytes 704032 | tf_op jit(solution)/shard_map/ppermute | solution.py:691
  20.7 2.2 %collective-permute-done.2.cross_ref = bf16[704,500]{1,0:T(8,128)(2,1)S(1)} collective-permute-done((bf16[704,500]{1,0:T(8,128)(2,1)S(1)}, bf16[704,500]{1,0:T(8,128)(2,1)S(1)}, u32[]{:S(2)}, u32[]{:S(2)}) %collective-permute-start.2) | collective-permute-done | bytes 704032 | tf_op jit(solution)/shard_map/ppermute | solution.py:691
  24.2 13.4 %all_to_all.20.stats_ref = f32[8,8,512]{2,1,0:T(8,128)S(1)} all-to-all(f32[8,8,512]{2,1,0:T(8,128)S(1)} %get-tuple-element.127), channel_id=1, replica_groups=mesh['seq'=8,'neur'=4] {'seq'}, dimensions={0} | all-to-all | bytes 262144 | tf_op jit(solution)/shard_map/all_to_all | solution.py:746
  37.6 5.3 %shard_map.198 = (bf16[704,500]{1,0:T(8,128)(2,1)}, f32[704,512]{1,0:T(8,128)S(1)}, f32[8,512]{1,0:T(8,128)S(1)}, bf16[704,512]{1,0:T(8,128)(2,1)S(1)}, f32[8,512]{1,0:T(8,128)S(1)}) custom-call(f32[8,8,512]{2,1,0:T(8,128)S(1)} %all_to_all.20.stats_ref, f32[704,512]{1,0:T(8,128)S(1)} %get-tuple-element.128.proj_ref, f32[8,512]{1,0:T(8,128)S(1)} %get-tuple-element.129.par_ref), custom_call_target="tpu_custom_call" | custom-call | tf_op jit(solution)/shard_map/pallas_call | solution.py:807
  45.5 2.5 %shard_map.201 = (bf16[4,256,256]{2,1,0:T(8,128)(2,1)S(1)}, bf16[4,256,256]{2,1,0:T(8,128)(2,1)S(1)}, bf16[4,256,256]{2,1,0:T(8,128)(2,1)S(1)}, bf16[4,256,256]{2,1,0:T(8,128)(2,1)S(1)}) custom-call(bf16[704,500]{1,0:T(8,128)(2,1)S(1)} %bitcast.15, bf16[704,500]{1,0:T(8,128)(2,1)S(1)} %collective-permute-done.1.mate_ref, ...), custom_call_target="tpu_custom_call" | custom-call | tf_op jit(solution)/shard_map/pallas_call | solution.py:786
  48.4 1.7 collective-permute-start.8
  51.2 11.1 %collective-permute-done.3.far_ref = bf16[704,500]{1,0:T(8,128)(2,1)S(1)} collective-permute-done((bf16[704,500]{1,0:T(8,128)(2,1)S(1)}, bf16[704,500]{1,0:T(8,128)(2,1)S(1)}, u32[]{:S(2)}, u32[]{:S(2)}) %collective-permute-start.3) | collective-permute-done | bytes 704032 | tf_op jit(solution)/shard_map/ppermute | solution.py:691
  62.4 2.2 %collective-permute-done.9.cross_ref = bf16[704,500]{1,0:T(8,128)(2,1)S(1)} collective-permute-done((bf16[704,500]{1,0:T(8,128)(2,1)S(1)}, bf16[704,500]{1,0:T(8,128)(2,1)S(1)}, u32[]{:S(2)}, u32[]{:S(2)}) %collective-permute-start.9) | collective-permute-done | bytes 704032 | tf_op jit(solution)/shard_map/ppermute | solution.py:691
  65.9 10.0 %all_to_all.21.stats_ref = f32[8,8,512]{2,1,0:T(8,128)S(1)} all-to-all(f32[8,8,512]{2,1,0:T(8,128)S(1)} %get-tuple-element.150), channel_id=1, replica_groups=mesh['seq'=8,'neur'=4] {'seq'}, dimensions={0} | all-to-all | bytes 262144 | tf_op jit(solution)/shard_map/all_to_all | solution.py:746
  75.9 7.4 %shard_map.203 = (bf16[704,500]{1,0:T(8,128)(2,1)}, f32[704,512]{1,0:T(8,128)S(1)}, f32[8,8,512]{2,1,0:T(8,128)S(1)}, f32[8,512]{1,0:T(8,128)S(1)}, f32[2,500]{1,0:T(2,128)}, /*index=5*/f32[2,500]{1,0:T(2,128)}) custom-call(f32[8,8,512]{2,1,0:T(8,128)S(1)} %all_to_all.21.stats_ref, f32[704,512]{1,0:T(8,128)S(1)} %get-tuple-element.151.proj_ref, ...), custom_call_target="tpu_custom_call" | custom-call | tf_op jit(solution)/shard_map/pallas_call | solution.py:832
  83.3 9.8 %all_to_all.22.sums_ref = f32[8,8,512]{2,1,0:T(8,128)S(1)} all-to-all(f32[8,8,512]{2,1,0:T(8,128)S(1)} %get-tuple-element.154), channel_id=1, replica_groups=mesh['seq'=8,'neur'=4] {'seq'}, dimensions={0} | all-to-all | bytes 262144 | tf_op jit(solution)/shard_map/all_to_all | solution.py:746
  93.6 2.5 %shard_map.205 = (bf16[4,256,256]{2,1,0:T(8,128)(2,1)S(1)}, bf16[4,256,256]{2,1,0:T(8,128)(2,1)S(1)}, bf16[4,256,256]{2,1,0:T(8,128)(2,1)S(1)}, bf16[4,256,256]{2,1,0:T(8,128)(2,1)S(1)}) custom-call(bf16[704,500]{1,0:T(8,128)(2,1)S(1)} %copy-done.1, bf16[704,500]{1,0:T(8,128)(2,1)S(1)} %collective-permute-done.4.mate_ref, ...), custom_call_target="tpu_custom_call" | custom-call | tf_op jit(solution)/shard_map/pallas_call | solution.py:786
  97.1 1.6 collective-permute-start.11
  100.9 11.8 %collective-permute-done.12.got_left_ref = bf16[4,256,256]{2,1,0:T(8,128)(2,1)S(1)} collective-permute-done((bf16[4,256,256]{2,1,0:T(8,128)(2,1)S(1)}, bf16[4,256,256]{2,1,0:T(8,128)(2,1)S(1)}, u32[]{:S(2)}, u32[]{:S(2)}) %collective-permute-start.12) | collective-permute-done | bytes 524320 | tf_op jit(solution)/shard_map/ppermute | solution.py:691
  115.7 2.6 %shard_map.209 = (f32[704,512]{1,0:T(8,128)S(1)}, f32[8,8,512]{2,1,0:T(8,128)S(1)}, bf16[704,512]{1,0:T(8,128)(2,1)S(1)}) custom-call(f32[704,512]{1,0:T(8,128)S(1)} %shard_map.207.keep_ref, bf16[704,512]{1,0:T(8,128)(2,1)S(1)} %collective-permute-done.11.got_ref, f32[704,512]{1,0:T(8,128)S(1)} %get-tuple-element.128.proj_ref, ...), custom_call_target="tpu_custom_call" | custom-call | tf_op jit(solution)/shard_map/pallas_call | solution.py:867
  118.3 2.5 %shard_map.211 = (bf16[4,256,256]{2,1,0:T(8,128)(2,1)S(1)}, bf16[4,256,256]{2,1,0:T(8,128)(2,1)S(1)}, bf16[4,256,256]{2,1,0:T(8,128)(2,1)S(1)}, bf16[4,256,256]{2,1,0:T(8,128)(2,1)S(1)}) custom-call(bf16[704,500]{1,0:T(8,128)(2,1)S(1)} %bitcast.16, bf16[704,500]{1,0:T(8,128)(2,1)S(1)} %collective-permute-done.1.mate_ref, ...), custom_call_target="tpu_custom_call" | custom-call | tf_op jit(solution)/shard_map/pallas_call | solution.py:786
  123.2 20.1 %all_to_all.23.sums_ref = f32[8,8,512]{2,1,0:T(8,128)S(1)} all-to-all(f32[8,8,512]{2,1,0:T(8,128)S(1)} %get-tuple-element.185), channel_id=1, replica_groups=mesh['seq'=8,'neur'=4] {'seq'}, dimensions={0} | all-to-all | bytes 262144 | tf_op jit(solution)/shard_map/all_to_all | solution.py:746
  147.3 1.6 collective-permute-start.33
  149.7 9.8 %collective-permute-done.20.got_left_ref = bf16[2,256,256]{2,1,0:T(8,128)(2,1)S(1)} collective-permute-done((bf16[2,256,256]{2,1,0:T(8,128)(2,1)S(1)}, bf16[2,256,256]{2,1,0:T(8,128)(2,1)S(1)}, u32[]{:S(2)}, u32[]{:S(2)}) %collective-permute-start.20) | collective-permute-done | bytes 262176 | tf_op jit(solution)/shard_map/ppermute | solution.py:691
  159.7 5.1 %collective-permute-done.32.refs_2_ = bf16[256,512]{1,0:T(8,128)(2,1)S(1)} collective-permute-done((bf16[256,512]{1,0:T(8,128)(2,1)S(1)}, bf16[256,512]{1,0:T(8,128)(2,1)S(1)}, u32[]{:S(2)}, u32[]{:S(2)}) %collective-permute-start.32) | collective-permute-done | bytes 262176 | tf_op jit(solution)/shard_map/ppermute | solution.py:691
  169.4 6.8 %collective-permute-done.22 = bf16[256,512]{1,0:T(8,128)(2,1)S(1)} collective-permute-done((bf16[256,512]{1,0:T(8,128)(2,1)S(1)}, bf16[256,512]{1,0:T(8,128)(2,1)S(1)}, u32[]{:S(2)}, u32[]{:S(2)}) %collective-permute-start.22) | collective-permute-done | bytes 262176 | tf_op jit(solution)/shard_map/ppermute | solution.py:691
  177.7 1.8 collective-permute-start.24
  180.9 7.4 %collective-permute-done.25.refs_2_ = bf16[256,512]{1,0:T(8,128)(2,1)S(1)} collective-permute-done((bf16[256,512]{1,0:T(8,128)(2,1)S(1)}, bf16[256,512]{1,0:T(8,128)(2,1)S(1)}, u32[]{:S(2)}, u32[]{:S(2)}) %collective-permute-start.25) | collective-permute-done | bytes 262176 | tf_op jit(solution)/shard_map/ppermute | solution.py:691
  190.4 1.8 collective-permute-done.24.refs_1_
  193.4 4.2 %collective-permute-done.37.refs_7_ = bf16[256,512]{1,0:T(8,128)(2,1)S(1)} collective-permute-done((bf16[256,512]{1,0:T(8,128)(2,1)S(1)}, bf16[256,512]{1,0:T(8,128)(2,1)S(1)}, u32[]{:S(2)}, u32[]{:S(2)}) %collective-permute-start.37) | collective-permute-done | bytes 262176 | tf_op jit(solution)/shard_map/ppermute | solution.py:691
  197.6 2.5 %shard_map.218 = f32[2000,500]{1,0:T(8,128)} custom-call(bf16[256,512]{1,0:T(8,128)(2,1)S(1)} %add_convert_fusion.refs_0_, bf16[256,512]{1,0:T(8,128)(2,1)S(1)} %collective-permute-done.31.refs_1_, bf16[256,512]{1,0:T(8,128)(2,1)S(1)} %collective-permute-done.32.refs_2_, bf16[256,512]{1,0:T(8,128)(2,1)S(1)} %collective-permute-done.34.refs_3_, ...), custom_call_target="tpu_custom_call" | custom-call | tf_op jit(solution)/shard_map/pallas_call | solution.py:795
  201.3 1.9 collective-permute-done.28.refs_6_
  205.8 3.5 %collective-permute-done.29.refs_5_ = bf16[256,512]{1,0:T(8,128)(2,1)S(1)} collective-permute-done((bf16[256,512]{1,0:T(8,128)(2,1)S(1)}, bf16[256,512]{1,0:T(8,128)(2,1)S(1)}, u32[]{:S(2)}, u32[]{:S(2)}) %collective-permute-start.29) | collective-permute-done | bytes 262176 | tf_op jit(solution)/shard_map/ppermute | solution.py:691
  209.3 3.4 %collective-permute-done.30.refs_7_ = bf16[256,512]{1,0:T(8,128)(2,1)S(1)} collective-permute-done((bf16[256,512]{1,0:T(8,128)(2,1)S(1)}, bf16[256,512]{1,0:T(8,128)(2,1)S(1)}, u32[]{:S(2)}, u32[]{:S(2)}) %collective-permute-start.30) | collective-permute-done | bytes 262176 | tf_op jit(solution)/shard_map/ppermute | solution.py:691
  212.7 2.5 %shard_map.217 = f32[2000,500]{1,0:T(8,128)} custom-call(bf16[256,512]{1,0:T(8,128)(2,1)S(1)} %add_convert_fusion.1.refs_0_, bf16[256,512]{1,0:T(8,128)(2,1)S(1)} %collective-permute-done.24.refs_1_, bf16[256,512]{1,0:T(8,128)(2,1)S(1)} %collective-permute-done.25.refs_2_, bf16[256,512]{1,0:T(8,128)(2,1)S(1)} %collective-permute-done.27.refs_3_, ...), custom_call_target="tpu_custom_call" | custom-call | tf_op jit(solution)/shard_map/pallas_call | solution.py:795
  (106 shorter events, 39.2 us)
Async XLA Ops:
  1.2 19.5 %collective-permute-start = (bf16[704,500]{1,0:T(8,128)(2,1)}, bf16[704,500]{1,0:T(8,128)(2,1)S(1)}, u32[]{:S(2)}, u32[]{:S(2)}) collective-permute-start(bf16[704,500]{1,0:T(8,128)(2,1)} %bitcast.13), channel_id=1, source_target_pairs={{0,2},{1,3},{2,0},{3,1},{4,6},{5,7},{6,4},{7,5},{8,10},{9,11},{10,... | collective-permute-start | bytes 2112008 | tf_op jit(solution)/shard_map/ppermute | solution.py:691
  43.2 19.1 %collective-permute-start.6 = (bf16[2,512,512]{2,1,0:T(8,128)(2,1)S(1)}, bf16[2,512,512]{2,1,0:T(8,128)(2,1)S(1)}, u32[]{:S(2)}, u32[]{:S(2)}) collective-permute-start(bf16[2,512,512]{2,1,0:T(8,128)(2,1)S(1)} %get-tuple-element.138), channel_id=1, source_target_pairs={{0,1},{1,0},{2,3},{3,2},{4,5},{5,4},{6,7},{7,6},{8,9},{9,8},{10,11... | collective-permute-start | bytes 3145736 | tf_op jit(solution)/shard_map/ppermute | solution.py:691
  43.8 18.6 %collective-permute-start.5 = (bf16[2,512,512]{2,1,0:T(8,128)(2,1)S(1)}, bf16[2,512,512]{2,1,0:T(8,128)(2,1)S(1)}, u32[]{:S(2)}, u32[]{:S(2)}) collective-permute-start(bf16[2,512,512]{2,1,0:T(8,128)(2,1)S(1)} %get-tuple-element.136), channel_id=1, source_target_pairs={{0,1},{1,0},{2,3},{3,2},{4,5},{5,4},{6,7},{7,6},{8,9},{9,8},{10,11... | collective-permute-start | bytes 3145736 | tf_op jit(solution)/shard_map/ppermute | solution.py:691
  44.0 18.4 %collective-permute-start.3 = (bf16[704,500]{1,0:T(8,128)(2,1)S(1)}, bf16[704,500]{1,0:T(8,128)(2,1)S(1)}, u32[]{:S(2)}, u32[]{:S(2)}) collective-permute-start(bf16[704,500]{1,0:T(8,128)(2,1)S(1)} %copy-done.1), channel_id=1, source_target_pairs={{0,2},{1,3},{2,0},{3,1},{4,6},{5,7},{6,4},{7,5},{8,10},{9,11},{10,... | collective-permute-start | bytes 2112008 | tf_op jit(solution)/shard_map/ppermute | solution.py:691
  48.0 14.4 %collective-permute-start.7 = (bf16[4,256,256]{2,1,0:T(8,128)(2,1)S(1)}, bf16[4,256,256]{2,1,0:T(8,128)(2,1)S(1)}, u32[]{:S(2)}, u32[]{:S(2)}) collective-permute-start(bf16[4,256,256]{2,1,0:T(8,128)(2,1)S(1)} %get-tuple-element.144), channel_id=1, source_target_pairs={{0,4},{4,0},{8,12},{12,8},{16,20},{20,16},{24,28},{28,24},{1,5},{5... | collective-permute-start | bytes 1572872 | tf_op jit(solution)/shard_map/ppermute | solution.py:691
  48.4 13.9 %collective-permute-start.8 = (bf16[4,256,256]{2,1,0:T(8,128)(2,1)S(1)}, bf16[4,256,256]{2,1,0:T(8,128)(2,1)S(1)}, u32[]{:S(2)}, u32[]{:S(2)}) collective-permute-start(bf16[4,256,256]{2,1,0:T(8,128)(2,1)S(1)} %get-tuple-element.146), channel_id=1, source_target_pairs={{0,8},{4,12},{8,0},{12,4},{16,24},{20,28},{24,16},{28,20},{1,9},{5... | collective-permute-start | bytes 1572872 | tf_op jit(solution)/shard_map/ppermute | solution.py:691
  97.1 18.6 %collective-permute-start.11 = (bf16[704,512]{1,0:T(8,128)(2,1)S(1)}, bf16[704,512]{1,0:T(8,128)(2,1)S(1)}, u32[]{:S(2)}, u32[]{:S(2)}) collective-permute-start(bf16[704,512]{1,0:T(8,128)(2,1)S(1)} %shard_map.206), channel_id=1, source_target_pairs={{0,2},{1,3},{2,0},{3,1},{4,6},{5,7},{6,4},{7,5},{8,10},{9,11},{10,... | collective-permute-start | bytes 2162696 | tf_op jit(solution)/shard_map/ppermute | solution.py:691
  98.6 14.0 %collective-permute-start.12 = (bf16[4,256,256]{2,1,0:T(8,128)(2,1)S(1)}, bf16[4,256,256]{2,1,0:T(8,128)(2,1)S(1)}, u32[]{:S(2)}, u32[]{:S(2)}) collective-permute-start(bf16[4,256,256]{2,1,0:T(8,128)(2,1)S(1)} %get-tuple-element.169), channel_id=1, source_target_pairs={{0,4},{4,0},{8,12},{12,8},{16,20},{20,16},{24,28},{28,24},{1,5},{5... | collective-permute-start | bytes 1572872 | tf_op jit(solution)/shard_map/ppermute | solution.py:691
  98.9 13.8 %collective-permute-start.13 = (bf16[4,256,256]{2,1,0:T(8,128)(2,1)S(1)}, bf16[4,256,256]{2,1,0:T(8,128)(2,1)S(1)}, u32[]{:S(2)}, u32[]{:S(2)}) collective-permute-start(bf16[4,256,256]{2,1,0:T(8,128)(2,1)S(1)} %get-tuple-element.170), channel_id=1, source_target_pairs={{0,8},{4,12},{8,0},{12,4},{16,24},{20,28},{24,16},{28,20},{1,9},{5... | collective-permute-start | bytes 1572872 | tf_op jit(solution)/shard_map/ppermute | solution.py:691
  112.9 9.3 %collective-permute-start.14 = (bf16[2,256,256]{2,1,0:T(8,128)(2,1)S(1)}, bf16[2,256,256]{2,1,0:T(8,128)(2,1)S(1)}, u32[]{:S(2)}, u32[]{:S(2)}) collective-permute-start(bf16[2,256,256]{2,1,0:T(8,128)(2,1)S(1)} %get-tuple-element.180), channel_id=1, source_target_pairs={{0,8},{4,12},{8,0},{12,4},{16,24},{20,28},{24,16},{28,20},{1,9},{5... | collective-permute-start | bytes 786440 | tf_op jit(solution)/shard_map/ppermute | solution.py:691
  114.0 8.2 %collective-permute-start.15 = (bf16[2,256,256]{2,1,0:T(8,128)(2,1)S(1)}, bf16[2,256,256]{2,1,0:T(8,128)(2,1)S(1)}, u32[]{:S(2)}, u32[]{:S(2)}) collective-permute-start(bf16[2,256,256]{2,1,0:T(8,128)(2,1)S(1)} %get-tuple-element.182), channel_id=1, source_target_pairs={{0,4},{4,0},{8,12},{12,8},{16,20},{20,16},{24,28},{28,24},{1,5},{5... | collective-permute-start | bytes 786440 | tf_op jit(solution)/shard_map/ppermute | solution.py:691
  120.8 22.5 %collective-permute-start.17 = (bf16[4,256,256]{2,1,0:T(8,128)(2,1)S(1)}, bf16[4,256,256]{2,1,0:T(8,128)(2,1)S(1)}, u32[]{:S(2)}, u32[]{:S(2)}) collective-permute-start(bf16[4,256,256]{2,1,0:T(8,128)(2,1)S(1)} %get-tuple-element.188), channel_id=1, source_target_pairs={{0,4},{4,0},{8,12},{12,8},{16,20},{20,16},{24,28},{28,24},{1,5},{5... | collective-permute-start | bytes 1572872 | tf_op jit(solution)/shard_map/ppermute | solution.py:691
  121.2 22.1 %collective-permute-start.18 = (bf16[4,256,256]{2,1,0:T(8,128)(2,1)S(1)}, bf16[4,256,256]{2,1,0:T(8,128)(2,1)S(1)}, u32[]{:S(2)}, u32[]{:S(2)}) collective-permute-start(bf16[4,256,256]{2,1,0:T(8,128)(2,1)S(1)} %get-tuple-element.189), channel_id=1, source_target_pairs={{0,8},{4,12},{8,0},{12,4},{16,24},{20,28},{24,16},{28,20},{1,9},{5... | collective-permute-start | bytes 1572872 | tf_op jit(solution)/shard_map/ppermute | solution.py:691
  122.3 21.0 %collective-permute-start.16 = (bf16[256,512]{1,0:T(8,128)(2,1)S(1)}, bf16[256,512]{1,0:T(8,128)(2,1)S(1)}, u32[]{:S(2)}, u32[]{:S(2)}) collective-permute-start(bf16[256,512]{1,0:T(8,128)(2,1)S(1)} %get-tuple-element.186), channel_id=1, source_target_pairs={{0,16},{4,20},{8,24},{12,28},{16,0},{20,4},{24,8},{28,12},{1,17},{... | collective-permute-start | bytes 786440 | tf_op jit(solution)/shard_map/ppermute | solution.py:691
  144.7 14.8 %collective-permute-start.20 = (bf16[2,256,256]{2,1,0:T(8,128)(2,1)S(1)}, bf16[2,256,256]{2,1,0:T(8,128)(2,1)S(1)}, u32[]{:S(2)}, u32[]{:S(2)}) collective-permute-start(bf16[2,256,256]{2,1,0:T(8,128)(2,1)S(1)} %get-tuple-element.207), channel_id=1, source_target_pairs={{0,8},{4,12},{8,0},{12,4},{16,24},{20,28},{24,16},{28,20},{1,9},{5... | collective-permute-start | bytes 786440 | tf_op jit(solution)/shard_map/ppermute | solution.py:691
  144.9 14.6 %collective-permute-start.21 = (bf16[2,256,256]{2,1,0:T(8,128)(2,1)S(1)}, bf16[2,256,256]{2,1,0:T(8,128)(2,1)S(1)}, u32[]{:S(2)}, u32[]{:S(2)}) collective-permute-start(bf16[2,256,256]{2,1,0:T(8,128)(2,1)S(1)} %get-tuple-element.209), channel_id=1, source_target_pairs={{0,4},{4,0},{8,12},{12,8},{16,20},{20,16},{24,28},{28,24},{1,5},{5... | collective-permute-start | bytes 786440 | tf_op jit(solution)/shard_map/ppermute | solution.py:691
  145.8 19.0 %collective-permute-start.32 = (bf16[256,512]{1,0:T(8,128)(2,1)S(1)}, bf16[256,512]{1,0:T(8,128)(2,1)S(1)}, u32[]{:S(2)}, u32[]{:S(2)}) collective-permute-start(bf16[256,512]{1,0:T(8,128)(2,1)S(1)} %add_convert_fusion.refs_0_), channel_id=1, source_target_pairs={{0,8},{4,12},{8,0},{12,4},{16,24},{20,28},{24,16},{28,20},{1,9},{5... | collective-permute-start | bytes 786440 | tf_op jit(solution)/shard_map/ppermute | solution.py:691
  147.3 17.5 %collective-permute-start.33 = (bf16[256,512]{1,0:T(8,128)(2,1)S(1)}, bf16[256,512]{1,0:T(8,128)(2,1)S(1)}, u32[]{:S(2)}, u32[]{:S(2)}) collective-permute-start(bf16[256,512]{1,0:T(8,128)(2,1)S(1)} %add_convert_fusion.refs_0_), channel_id=1, source_target_pairs={{0,4},{4,0},{8,12},{12,8},{16,20},{20,16},{24,28},{28,24},{1,5},{5... | collective-permute-start | bytes 786440 | tf_op jit(solution)/shard_map/ppermute | solution.py:691
  149.0 16.2 %collective-permute-start.31 = (bf16[256,512]{1,0:T(8,128)(2,1)S(1)}, bf16[256,512]{1,0:T(8,128)(2,1)S(1)}, u32[]{:S(2)}, u32[]{:S(2)}) collective-permute-start(bf16[256,512]{1,0:T(8,128)(2,1)S(1)} %add_convert_fusion.refs_0_), channel_id=1, source_target_pairs={{0,16},{4,20},{8,24},{12,28},{16,0},{20,4},{24,8},{28,12},{1,17},{... | collective-permute-start | bytes 786440 | tf_op jit(solution)/shard_map/ppermute | solution.py:691
  159.6 16.6 %collective-permute-start.22 = (bf16[256,512]{1,0:T(8,128)(2,1)S(1)}, bf16[256,512]{1,0:T(8,128)(2,1)S(1)}, u32[]{:S(2)}, u32[]{:S(2)}) collective-permute-start(bf16[256,512]{1,0:T(8,128)(2,1)S(1)} %get-tuple-element.211), channel_id=1, source_target_pairs={{0,16},{4,20},{8,24},{12,28},{16,0},{20,4},{24,8},{28,12},{1,17},{... | collective-permute-start | bytes 786440 | tf_op jit(solution)/shard_map/ppermute | solution.py:691
  164.8 12.9 %collective-permute-start.35 = (bf16[256,512]{1,0:T(8,128)(2,1)S(1)}, bf16[256,512]{1,0:T(8,128)(2,1)S(1)}, u32[]{:S(2)}, u32[]{:S(2)}) collective-permute-start(bf16[256,512]{1,0:T(8,128)(2,1)S(1)} %collective-permute-done.32.refs_2_), channel_id=1, source_target_pairs={{0,4},{4,0},{8,12},{12,8},{16,20},{20,16},{24,28},{28,24},{1,5},{5... | collective-permute-start | bytes 786440 | tf_op jit(solution)/shard_map/ppermute | solution.py:691
  165.2 14.3 %collective-permute-start.34 = (bf16[256,512]{1,0:T(8,128)(2,1)S(1)}, bf16[256,512]{1,0:T(8,128)(2,1)S(1)}, u32[]{:S(2)}, u32[]{:S(2)}) collective-permute-start(bf16[256,512]{1,0:T(8,128)(2,1)S(1)} %collective-permute-done.31.refs_1_), channel_id=1, source_target_pairs={{0,8},{4,12},{8,0},{12,4},{16,24},{20,28},{24,16},{28,20},{1,9},{5... | collective-permute-start | bytes 786440 | tf_op jit(solution)/shard_map/ppermute | solution.py:691
  166.9 37.6 %collective-permute-start.23 = (bf16[704,512]{1,0:T(8,128)(2,1)S(1)}, bf16[704,512]{1,0:T(8,128)(2,1)S(1)}, u32[]{:S(2)}, u32[]{:S(2)}) collective-permute-start(bf16[704,512]{1,0:T(8,128)(2,1)S(1)} %shard_map.214), channel_id=1, source_target_pairs={{0,2},{1,3},{2,0},{3,1},{4,6},{5,7},{6,4},{7,5},{8,10},{9,11},{10,... | collective-permute-start | bytes 2162696 | tf_op jit(solution)/shard_map/ppermute | solution.py:691
  176.3 12.1 %collective-permute-start.25 = (bf16[256,512]{1,0:T(8,128)(2,1)S(1)}, bf16[256,512]{1,0:T(8,128)(2,1)S(1)}, u32[]{:S(2)}, u32[]{:S(2)}) collective-permute-start(bf16[256,512]{1,0:T(8,128)(2,1)S(1)} %add_convert_fusion.1.refs_0_), channel_id=1, source_target_pairs={{0,8},{4,12},{8,0},{12,4},{16,24},{20,28},{24,16},{28,20},{1,9},{5... | collective-permute-start | bytes 786440 | tf_op jit(solution)/shard_map/ppermute | solution.py:691
  176.4 13.2 %collective-permute-start.26 = (bf16[256,512]{1,0:T(8,128)(2,1)S(1)}, bf16[256,512]{1,0:T(8,128)(2,1)S(1)}, u32[]{:S(2)}, u32[]{:S(2)}) collective-permute-start(bf16[256,512]{1,0:T(8,128)(2,1)S(1)} %add_convert_fusion.1.refs_0_), channel_id=1, source_target_pairs={{0,4},{4,0},{8,12},{12,8},{16,20},{20,16},{24,28},{28,24},{1,5},{5... | collective-permute-start | bytes 786440 | tf_op jit(solution)/shard_map/ppermute | solution.py:691
  177.7 14.4 %collective-permute-start.24 = (bf16[256,512]{1,0:T(8,128)(2,1)S(1)}, bf16[256,512]{1,0:T(8,128)(2,1)S(1)}, u32[]{:S(2)}, u32[]{:S(2)}) collective-permute-start(bf16[256,512]{1,0:T(8,128)(2,1)S(1)} %add_convert_fusion.1.refs_0_), channel_id=1, source_target_pairs={{0,16},{4,20},{8,24},{12,28},{16,0},{20,4},{24,8},{28,12},{1,17},{... | collective-permute-start | bytes 786440 | tf_op jit(solution)/shard_map/ppermute | solution.py:691
  179.5 13.9 %collective-permute-start.36 = (bf16[256,512]{1,0:T(8,128)(2,1)S(1)}, bf16[256,512]{1,0:T(8,128)(2,1)S(1)}, u32[]{:S(2)}, u32[]{:S(2)}) collective-permute-start(bf16[256,512]{1,0:T(8,128)(2,1)S(1)} %collective-permute-done.31.refs_1_), channel_id=1, source_target_pairs={{0,4},{4,0},{8,12},{12,8},{16,20},{20,16},{24,28},{28,24},{1,5},{5... | collective-permute-start | bytes 786440 | tf_op jit(solution)/shard_map/ppermute | solution.py:691
  188.4 9.2 %collective-permute-start.37 = (bf16[256,512]{1,0:T(8,128)(2,1)S(1)}, bf16[256,512]{1,0:T(8,128)(2,1)S(1)}, u32[]{:S(2)}, u32[]{:S(2)}) collective-permute-start(bf16[256,512]{1,0:T(8,128)(2,1)S(1)} %collective-permute-done.34.refs_3_), channel_id=1, source_target_pairs={{0,4},{4,0},{8,12},{12,8},{16,20},{20,16},{24,28},{28,24},{1,5},{5... | collective-permute-start | bytes 786440 | tf_op jit(solution)/shard_map/ppermute | solution.py:691
  189.6 13.6 %collective-permute-start.28 = (bf16[256,512]{1,0:T(8,128)(2,1)S(1)}, bf16[256,512]{1,0:T(8,128)(2,1)S(1)}, u32[]{:S(2)}, u32[]{:S(2)}) collective-permute-start(bf16[256,512]{1,0:T(8,128)(2,1)S(1)} %collective-permute-done.25.refs_2_), channel_id=1, source_target_pairs={{0,4},{4,0},{8,12},{12,8},{16,20},{20,16},{24,28},{28,24},{1,5},{5... | collective-permute-start | bytes 786440 | tf_op jit(solution)/shard_map/ppermute | solution.py:691
  192.2 11.1 %collective-permute-start.27 = (bf16[256,512]{1,0:T(8,128)(2,1)S(1)}, bf16[256,512]{1,0:T(8,128)(2,1)S(1)}, u32[]{:S(2)}, u32[]{:S(2)}) collective-permute-start(bf16[256,512]{1,0:T(8,128)(2,1)S(1)} %collective-permute-done.24.refs_1_), channel_id=1, source_target_pairs={{0,8},{4,12},{8,0},{12,4},{16,24},{20,28},{24,16},{28,20},{1,9},{5... | collective-permute-start | bytes 786440 | tf_op jit(solution)/shard_map/ppermute | solution.py:691
  200.1 9.2 %collective-permute-start.29 = (bf16[256,512]{1,0:T(8,128)(2,1)S(1)}, bf16[256,512]{1,0:T(8,128)(2,1)S(1)}, u32[]{:S(2)}, u32[]{:S(2)}) collective-permute-start(bf16[256,512]{1,0:T(8,128)(2,1)S(1)} %collective-permute-done.24.refs_1_), channel_id=1, source_target_pairs={{0,4},{4,0},{8,12},{12,8},{16,20},{20,16},{24,28},{28,24},{1,5},{5... | collective-permute-start | bytes 786440 | tf_op jit(solution)/shard_map/ppermute | solution.py:691
  203.3 9.4 %collective-permute-start.30 = (bf16[256,512]{1,0:T(8,128)(2,1)S(1)}, bf16[256,512]{1,0:T(8,128)(2,1)S(1)}, u32[]{:S(2)}, u32[]{:S(2)}) collective-permute-start(bf16[256,512]{1,0:T(8,128)(2,1)S(1)} %collective-permute-done.27.refs_3_), channel_id=1, source_target_pairs={{0,4},{4,0},{8,12},{12,8},{16,20},{20,16},{24,28},{28,24},{1,5},{5... | collective-permute-start | bytes 786440 | tf_op jit(solution)/shard_map/ppermute | solution.py:691
  (19 other events, 143.6 us)

commit v4 on v3

--- a/solution.py
+++ b/solution.py
@@ -78,23 +78,28 @@
         )
 
 
-def project_late(part_ref, means_ref, far_ref, cross_ref, w_ref, proj_ref, stats_ref):
+def project_middle(part_ref, means_ref, far_ref, w_ref, out_ref, out_means_ref):
     here = lax.axis_index("neur")
     k = far_ref.shape[1]
+    out_means_ref[...] = means_ref[...]
+    out_means_ref[2:3, :k] = means_of(far_ref)
+    for c in range(0, part_ref.shape[1], 256):
+        out_ref[:, c : c + 256] = part_ref[:, c : c + 256] + dot(
+            far_ref[...], w_ref[here ^ 2, :k, c : c + 256]
+        )
+
+
+def project_late(part_ref, means_ref, cross_ref, w_ref, proj_ref, stats_ref):
+    here = lax.axis_index("neur")
+    k = cross_ref.shape[1]
     peers, _, width = stats_ref.shape
-    far, cross = means_of(far_ref), means_of(cross_ref)
+    cross = means_of(cross_ref)
     for p in range(peers):
-        stats_ref[p, 2:4, :] = means_ref[0:2, :]
-        stats_ref[p, 4:8, :] = jnp.zeros((4, width), F32)
-        stats_ref[p, 4:5, :k] = far
+        stats_ref[p, 2:8, :] = means_ref[0:6, :]
         stats_ref[p, 5:6, :k] = cross
     length = proj_ref.shape[0]
     for c in range(0, part_ref.shape[1], 256):
-        y = (
-            part_ref[:, c : c + 256]
-            + dot(far_ref[...], w_ref[here ^ 2, :k, c : c + 256])
-            + dot(cross_ref[...], w_ref[here ^ 3, :k, c : c + 256])
-        )
+        y = part_ref[:, c : c + 256] + dot(cross_ref[...], w_ref[here ^ 3, :k, c : c + 256])
         proj_ref[:, c : c + 256] = y
         mean = jnp.sum(y, axis=0, keepdims=True) * (1.0 / length)
         off = y - mean
@@ -390,7 +395,7 @@
     lax.fori_loop(0, out_ref.shape[0] // 16, body, 0, unroll=4)
 
 
-def forward_kernel(stats_ref, proj_ref, par_ref, out_ref, wide_ref, sum_ref, norm_ref, total_ref, drive, state):
+def forward_kernel(stats_ref, proj_ref, par_ref, out_ref, wide_ref, sum_ref, drive, state):
     length, width = proj_ref.shape
     tiles = tiles_of(width)
     outs = tiles_of(out_ref.shape[1])
@@ -400,15 +405,20 @@
     clear(state, tiles)
     solve(drive, state, decay, tiles)
     put_states(state, out_ref, outs, wide_ref)
+
+
+def norm_kernel(proj_ref, sum_ref, norm_ref, total_ref):
+    length = proj_ref.shape[0]
+    mean, inverse = sum_ref[0:1, :], sum_ref[2:3, :]
     total_ref[...] = jnp.zeros(total_ref.shape, F32)
     total_ref[7:8, :] = length * (sum_ref[3:4, :] - mean) * inverse
 
-    def put_norm(i, _):
+    def body(i, _):
         rows = pl.ds(pl.multiple_of(i * 16, 16), 16)
         norm_ref[rows, :] = ((proj_ref[rows, :] - mean) * inverse).astype(BF16)
         return 0
 
-    lax.fori_loop(0, length // 16, put_norm, 0, unroll=4)
+    lax.fori_loop(0, length // 16, body, 0, unroll=4)
 
 
 def turn_kernel(
@@ -758,8 +768,9 @@
         extra = aside(mate) if aside else ()
         far, part, par, gives, extra = lax.optimization_barrier((far, part, par, gives, extra))
         cross = swap(far, 1, "neur")
+        part, means = call(project_middle, [shape(length, width), shape(8, width)])(part, means, far, w4)
         proj, stats = call(project_late, [shape(length, width), shape(peers, 8, width)])(
-            part, means, far, cross, w4
+            part, means, cross, w4
         )
         return (own, mate, far, cross), proj, share(stats), w4, gives, par, extra
 
@@ -804,15 +815,9 @@
     first_x, first_proj, first_stats, first_w, give, first_par, _ = project(
         tokens, w_first, (gain_first, shift_first, decay_first)
     )
-    first_out, first_wide, first_sum, first_norm, norm_total = call(
+    first_out, first_wide, first_sum = call(
         forward_kernel,
-        [
-            shape(length, real, dtype=BF16),
-            shape(length, width),
-            shape(8, width),
-            shape(length, width, dtype=BF16),
-            shape(8, width),
-        ],
+        [shape(length, real, dtype=BF16), shape(length, width), shape(8, width)],
         scans,
     )(first_stats, first_proj, first_par)
 
@@ -822,7 +827,9 @@
     def leaning(mate):
         if peers != 8:
             return ()
-        norm = after(first_norm, mate)
+        norm, norm_total = call(norm_kernel, [shape(length, width, dtype=BF16), shape(8, width)])(
+            first_proj, after(first_sum, mate)
+        )
         left, give_left, right, give_right = weight_parts(*first_x, norm, first_sum, norm_total)
         return left, swap(give_left, LEVEL[4]), right, swap(give_right, LEVEL[2])
 

time: 216 us -> 215 us (level)
  transfers between devices with their start and end apart: 38 -> 38, of which waited for: 15 -> 16; matrix products, arithmetic and copies ran while one was open for 1% -> 1% of each run, Pallas kernels for 9% -> 10%
where the time goes in v4:
time: 215 us
  waiting for transfers between devices  83.6 us (39%)
  blocking collectives  53.3 us (25%)
  Pallas kernels  39.3 us (18%)
  starting transfers between devices  31.1 us (14%)
  local copies, waits for them, and re-layouts  3.78 us (2%)
  other arithmetic  2.67 us (1%)
    ppermute x38, waiting for transfers between devices, swap(): return lax.ppermute(x, axis, [(i, i ^ bit) for i in range(n)])  83.6 us
    all_to_all x4, blocking collectives, share(): return lax.all_to_all(stats, 'seq', 0, 0, tiled=True)  53.3 us
    ppermute x38, starting transfers between devices, swap(): return lax.ppermute(x, axis, [(i, i ^ bit) for i in range(n)])  31.1 us
    pallas_call x3, Pallas kernels, weight_parts(): call(functools.partial(weight_kernel, True), [shape(4, half, half, dtype=...  7.56 us
    pallas_call x1, Pallas kernels, per_device(): call(turn_kernel, [shape(length, real, dtype=BF16), shape(length, width),...  7.4 us
    pallas_call x1, Pallas kernels, per_device(): call(forward_kernel, [shape(length, real, dtype=BF16), shape(length, widt...  5.1 us
    pallas_call x2, Pallas kernels, weights(): call(functools.partial(spread_kernel, True), shape(4 * real, real), [pltp...  4.93 us
  transfers between devices with their start and end apart: 38, of which 16 were waited for; matrix products, arithmetic and copies ran while one was open for 1% of the time, Pallas kernels for 10%

profile of v4, /device:TPU:0, one launch (start us, length us, event | category | flops | bytes accessed | tf_op | source)
XLA Modules:
  0.0 214.6 jit_solution(8372630734480917057)
XLA Ops:
  1.2 2.6 %collective-permute-start = (bf16[704,500]{1,0:T(8,128)(2,1)}, bf16[704,500]{1,0:T(8,128)(2,1)S(1)}, u32[]{:S(2)}, u32[]{:S(2)}) collective-permute-start(bf16[704,500]{1,0:T(8,128)(2,1)} %bitcast.13), channel_id=1, source_target_pairs={{0,2},{1,3},{2,0},{3,1},{4,6},{5,7},{6,4},{7,5},{8,10},{9,11},{10,... | collective-permute-start | bytes 2112008 | tf_op jit(solution)/shard_map/ppermute | solution.py:701
  3.7 1.6 copy-done.2
  8.8 11.9 %collective-permute-done.far_ref = bf16[704,500]{1,0:T(8,128)(2,1)S(1)} collective-permute-done((bf16[704,500]{1,0:T(8,128)(2,1)}, bf16[704,500]{1,0:T(8,128)(2,1)S(1)}, u32[]{:S(2)}, u32[]{:S(2)}) %collective-permute-start) | collective-permute-done | bytes 704032 | tf_op jit(solution)/shard_map/ppermute | solution.py:701
  21.3 1.6 collective-permute-done.2.cross_ref
  23.8 13.4 %all_to_all.20.stats_ref = f32[8,8,512]{2,1,0:T(8,128)S(1)} all-to-all(f32[8,8,512]{2,1,0:T(8,128)S(1)} %get-tuple-element.133), channel_id=1, replica_groups=mesh['seq'=8,'neur'=4] {'seq'}, dimensions={0} | all-to-all | bytes 262144 | tf_op jit(solution)/shard_map/all_to_all | solution.py:756
  37.1 5.1 %shard_map.199 = (bf16[704,500]{1,0:T(8,128)(2,1)}, f32[704,512]{1,0:T(8,128)S(1)}, f32[8,512]{1,0:T(8,128)S(1)}) custom-call(f32[8,8,512]{2,1,0:T(8,128)S(1)} %all_to_all.20.stats_ref, f32[704,512]{1,0:T(8,128)S(1)} %get-tuple-element.134.proj_ref, f32[8,512]{1,0:T(8,128)S(1)} %get-tuple-element.135.par_ref), custom_call_target="tpu_custom_call" | custom-call | tf_op jit(solution)/shard_map/pallas_call | solution.py:818
  43.3 1.5 collective-permute-start.3
  45.0 2.5 %shard_map.203 = (bf16[4,256,256]{2,1,0:T(8,128)(2,1)S(1)}, bf16[4,256,256]{2,1,0:T(8,128)(2,1)S(1)}, bf16[4,256,256]{2,1,0:T(8,128)(2,1)S(1)}, bf16[4,256,256]{2,1,0:T(8,128)(2,1)S(1)}) custom-call(bf16[704,500]{1,0:T(8,128)(2,1)S(1)} %bitcast.15, bf16[704,500]{1,0:T(8,128)(2,1)S(1)} %collective-permute-done.1.mate_ref, ...), custom_call_target="tpu_custom_call" | custom-call | tf_op jit(solution)/shard_map/pallas_call | solution.py:797
  50.6 11.1 %collective-permute-done.3.far_ref = bf16[704,500]{1,0:T(8,128)(2,1)S(1)} collective-permute-done((bf16[704,500]{1,0:T(8,128)(2,1)S(1)}, bf16[704,500]{1,0:T(8,128)(2,1)S(1)}, u32[]{:S(2)}, u32[]{:S(2)}) %collective-permute-start.3) | collective-permute-done | bytes 704032 | tf_op jit(solution)/shard_map/ppermute | solution.py:701
  63.0 1.6 collective-permute-done.9.cross_ref
  65.4 10.0 %all_to_all.21.stats_ref = f32[8,8,512]{2,1,0:T(8,128)S(1)} all-to-all(f32[8,8,512]{2,1,0:T(8,128)S(1)} %get-tuple-element.158), channel_id=1, replica_groups=mesh['seq'=8,'neur'=4] {'seq'}, dimensions={0} | all-to-all | bytes 262144 | tf_op jit(solution)/shard_map/all_to_all | solution.py:756
  75.4 7.4 %shard_map.206 = (bf16[704,500]{1,0:T(8,128)(2,1)}, f32[704,512]{1,0:T(8,128)S(1)}, f32[8,8,512]{2,1,0:T(8,128)S(1)}, f32[8,512]{1,0:T(8,128)S(1)}, f32[2,500]{1,0:T(2,128)}, /*index=5*/f32[2,500]{1,0:T(2,128)}) custom-call(f32[8,8,512]{2,1,0:T(8,128)S(1)} %all_to_all.21.stats_ref, f32[704,512]{1,0:T(8,128)S(1)} %get-tuple-element.159.proj_ref, ...), custom_call_target="tpu_custom_call" | custom-call | tf_op jit(solution)/shard_map/pallas_call | solution.py:839
  82.8 9.8 %all_to_all.22.sums_ref = f32[8,8,512]{2,1,0:T(8,128)S(1)} all-to-all(f32[8,8,512]{2,1,0:T(8,128)S(1)} %get-tuple-element.162), channel_id=1, replica_groups=mesh['seq'=8,'neur'=4] {'seq'}, dimensions={0} | all-to-all | bytes 262144 | tf_op jit(solution)/shard_map/all_to_all | solution.py:756
  93.1 2.5 %shard_map.208 = (bf16[4,256,256]{2,1,0:T(8,128)(2,1)S(1)}, bf16[4,256,256]{2,1,0:T(8,128)(2,1)S(1)}, bf16[4,256,256]{2,1,0:T(8,128)(2,1)S(1)}, bf16[4,256,256]{2,1,0:T(8,128)(2,1)S(1)}) custom-call(bf16[704,500]{1,0:T(8,128)(2,1)S(1)} %copy-done.1, bf16[704,500]{1,0:T(8,128)(2,1)S(1)} %collective-permute-done.4.mate_ref, ...), custom_call_target="tpu_custom_call" | custom-call | tf_op jit(solution)/shard_map/pallas_call | solution.py:797
  100.2 11.8 %collective-permute-done.12.got_left_ref = bf16[4,256,256]{2,1,0:T(8,128)(2,1)S(1)} collective-permute-done((bf16[4,256,256]{2,1,0:T(8,128)(2,1)S(1)}, bf16[4,256,256]{2,1,0:T(8,128)(2,1)S(1)}, u32[]{:S(2)}, u32[]{:S(2)}) %collective-permute-start.12) | collective-permute-done | bytes 524320 | tf_op jit(solution)/shard_map/ppermute | solution.py:701
  115.2 2.6 %shard_map.212 = (f32[704,512]{1,0:T(8,128)S(1)}, f32[8,8,512]{2,1,0:T(8,128)S(1)}, bf16[704,512]{1,0:T(8,128)(2,1)S(1)}) custom-call(f32[704,512]{1,0:T(8,128)S(1)} %shard_map.210.keep_ref, bf16[704,512]{1,0:T(8,128)(2,1)S(1)} %collective-permute-done.11.got_ref, f32[704,512]{1,0:T(8,128)S(1)} %get-tuple-element.134.proj_ref, ...), custom_call_target="tpu_custom_call" | custom-call | tf_op jit(solution)/shard_map/pallas_call | solution.py:874
  117.7 2.5 %shard_map.214 = (bf16[4,256,256]{2,1,0:T(8,128)(2,1)S(1)}, bf16[4,256,256]{2,1,0:T(8,128)(2,1)S(1)}, bf16[4,256,256]{2,1,0:T(8,128)(2,1)S(1)}, bf16[4,256,256]{2,1,0:T(8,128)(2,1)S(1)}) custom-call(bf16[704,500]{1,0:T(8,128)(2,1)S(1)} %bitcast.16, bf16[704,500]{1,0:T(8,128)(2,1)S(1)} %collective-permute-done.1.mate_ref, ...), custom_call_target="tpu_custom_call" | custom-call | tf_op jit(solution)/shard_map/pallas_call | solution.py:797
  122.7 20.1 %all_to_all.23.sums_ref = f32[8,8,512]{2,1,0:T(8,128)S(1)} all-to-all(f32[8,8,512]{2,1,0:T(8,128)S(1)} %get-tuple-element.193), channel_id=1, replica_groups=mesh['seq'=8,'neur'=4] {'seq'}, dimensions={0} | all-to-all | bytes 262144 | tf_op jit(solution)/shard_map/all_to_all | solution.py:756
  145.3 1.5 collective-permute-start.32
  146.8 1.6 collective-permute-start.33
  149.2 9.8 %collective-permute-done.20.got_left_ref = bf16[2,256,256]{2,1,0:T(8,128)(2,1)S(1)} collective-permute-done((bf16[2,256,256]{2,1,0:T(8,128)(2,1)S(1)}, bf16[2,256,256]{2,1,0:T(8,128)(2,1)S(1)}, u32[]{:S(2)}, u32[]{:S(2)}) %collective-permute-start.20) | collective-permute-done | bytes 262176 | tf_op jit(solution)/shard_map/ppermute | solution.py:701
  159.1 5.1 %collective-permute-done.32.refs_2_ = bf16[256,512]{1,0:T(8,128)(2,1)S(1)} collective-permute-done((bf16[256,512]{1,0:T(8,128)(2,1)S(1)}, bf16[256,512]{1,0:T(8,128)(2,1)S(1)}, u32[]{:S(2)}, u32[]{:S(2)}) %collective-permute-start.32) | collective-permute-done | bytes 262176 | tf_op jit(solution)/shard_map/ppermute | solution.py:701
  168.7 7.0 %collective-permute-done.22 = bf16[256,512]{1,0:T(8,128)(2,1)S(1)} collective-permute-done((bf16[256,512]{1,0:T(8,128)(2,1)S(1)}, bf16[256,512]{1,0:T(8,128)(2,1)S(1)}, u32[]{:S(2)}, u32[]{:S(2)}) %collective-permute-start.22) | collective-permute-done | bytes 262176 | tf_op jit(solution)/shard_map/ppermute | solution.py:701
  177.2 1.8 collective-permute-start.24
  180.4 7.4 %collective-permute-done.25.refs_2_ = bf16[256,512]{1,0:T(8,128)(2,1)S(1)} collective-permute-done((bf16[256,512]{1,0:T(8,128)(2,1)S(1)}, bf16[256,512]{1,0:T(8,128)(2,1)S(1)}, u32[]{:S(2)}, u32[]{:S(2)}) %collective-permute-start.25) | collective-permute-done | bytes 262176 | tf_op jit(solution)/shard_map/ppermute | solution.py:701
  189.9 1.8 collective-permute-done.24.refs_1_
  192.9 4.2 %collective-permute-done.37.refs_7_ = bf16[256,512]{1,0:T(8,128)(2,1)S(1)} collective-permute-done((bf16[256,512]{1,0:T(8,128)(2,1)S(1)}, bf16[256,512]{1,0:T(8,128)(2,1)S(1)}, u32[]{:S(2)}, u32[]{:S(2)}) %collective-permute-start.37) | collective-permute-done | bytes 262176 | tf_op jit(solution)/shard_map/ppermute | solution.py:701
  197.1 2.5 %shard_map.221 = f32[2000,500]{1,0:T(8,128)} custom-call(bf16[256,512]{1,0:T(8,128)(2,1)S(1)} %add_convert_fusion.refs_0_, bf16[256,512]{1,0:T(8,128)(2,1)S(1)} %collective-permute-done.31.refs_1_, bf16[256,512]{1,0:T(8,128)(2,1)S(1)} %collective-permute-done.32.refs_2_, bf16[256,512]{1,0:T(8,128)(2,1)S(1)} %collective-permute-done.34.refs_3_, ...), custom_call_target="tpu_custom_call" | custom-call | tf_op jit(solution)/shard_map/pallas_call | solution.py:806
  200.8 1.9 collective-permute-done.28.refs_6_
  205.2 3.6 %collective-permute-done.29.refs_5_ = bf16[256,512]{1,0:T(8,128)(2,1)S(1)} collective-permute-done((bf16[256,512]{1,0:T(8,128)(2,1)S(1)}, bf16[256,512]{1,0:T(8,128)(2,1)S(1)}, u32[]{:S(2)}, u32[]{:S(2)}) %collective-permute-start.29) | collective-permute-done | bytes 262176 | tf_op jit(solution)/shard_map/ppermute | solution.py:701
  208.8 3.4 %collective-permute-done.30.refs_7_ = bf16[256,512]{1,0:T(8,128)(2,1)S(1)} collective-permute-done((bf16[256,512]{1,0:T(8,128)(2,1)S(1)}, bf16[256,512]{1,0:T(8,128)(2,1)S(1)}, u32[]{:S(2)}, u32[]{:S(2)}) %collective-permute-start.30) | collective-permute-done | bytes 262176 | tf_op jit(solution)/shard_map/ppermute | solution.py:701
  212.2 2.5 %shard_map.220 = f32[2000,500]{1,0:T(8,128)} custom-call(bf16[256,512]{1,0:T(8,128)(2,1)S(1)} %add_convert_fusion.1.refs_0_, bf16[256,512]{1,0:T(8,128)(2,1)S(1)} %collective-permute-done.24.refs_1_, bf16[256,512]{1,0:T(8,128)(2,1)S(1)} %collective-permute-done.25.refs_2_, bf16[256,512]{1,0:T(8,128)(2,1)S(1)} %collective-permute-done.27.refs_3_, ...), custom_call_target="tpu_custom_call" | custom-call | tf_op jit(solution)/shard_map/pallas_call | solution.py:806
  (109 shorter events, 40.2 us)
Async XLA Ops:
  1.2 19.5 %collective-permute-start = (bf16[704,500]{1,0:T(8,128)(2,1)}, bf16[704,500]{1,0:T(8,128)(2,1)S(1)}, u32[]{:S(2)}, u32[]{:S(2)}) collective-permute-start(bf16[704,500]{1,0:T(8,128)(2,1)} %bitcast.13), channel_id=1, source_target_pairs={{0,2},{1,3},{2,0},{3,1},{4,6},{5,7},{6,4},{7,5},{8,10},{9,11},{10,... | collective-permute-start | bytes 2112008 | tf_op jit(solution)/shard_map/ppermute | solution.py:701
  42.6 19.1 %collective-permute-start.6 = (bf16[2,512,512]{2,1,0:T(8,128)(2,1)S(1)}, bf16[2,512,512]{2,1,0:T(8,128)(2,1)S(1)}, u32[]{:S(2)}, u32[]{:S(2)}) collective-permute-start(bf16[2,512,512]{2,1,0:T(8,128)(2,1)S(1)} %get-tuple-element.144), channel_id=1, source_target_pairs={{0,1},{1,0},{2,3},{3,2},{4,5},{5,4},{6,7},{7,6},{8,9},{9,8},{10,11... | collective-permute-start | bytes 3145736 | tf_op jit(solution)/shard_map/ppermute | solution.py:701
  43.2 18.6 %collective-permute-start.5 = (bf16[2,512,512]{2,1,0:T(8,128)(2,1)S(1)}, bf16[2,512,512]{2,1,0:T(8,128)(2,1)S(1)}, u32[]{:S(2)}, u32[]{:S(2)}) collective-permute-start(bf16[2,512,512]{2,1,0:T(8,128)(2,1)S(1)} %get-tuple-element.142), channel_id=1, source_target_pairs={{0,1},{1,0},{2,3},{3,2},{4,5},{5,4},{6,7},{7,6},{8,9},{9,8},{10,11... | collective-permute-start | bytes 3145736 | tf_op jit(solution)/shard_map/ppermute | solution.py:701
  43.3 18.4 %collective-permute-start.3 = (bf16[704,500]{1,0:T(8,128)(2,1)S(1)}, bf16[704,500]{1,0:T(8,128)(2,1)S(1)}, u32[]{:S(2)}, u32[]{:S(2)}) collective-permute-start(bf16[704,500]{1,0:T(8,128)(2,1)S(1)} %copy-done.1), channel_id=1, source_target_pairs={{0,2},{1,3},{2,0},{3,1},{4,6},{5,7},{6,4},{7,5},{8,10},{9,11},{10,... | collective-permute-start | bytes 2112008 | tf_op jit(solution)/shard_map/ppermute | solution.py:701
  47.6 14.2 %collective-permute-start.7 = (bf16[4,256,256]{2,1,0:T(8,128)(2,1)S(1)}, bf16[4,256,256]{2,1,0:T(8,128)(2,1)S(1)}, u32[]{:S(2)}, u32[]{:S(2)}) collective-permute-start(bf16[4,256,256]{2,1,0:T(8,128)(2,1)S(1)} %get-tuple-element.150), channel_id=1, source_target_pairs={{0,4},{4,0},{8,12},{12,8},{16,20},{20,16},{24,28},{28,24},{1,5},{5... | collective-permute-start | bytes 1572872 | tf_op jit(solution)/shard_map/ppermute | solution.py:701
  48.8 13.6 %collective-permute-start.8 = (bf16[4,256,256]{2,1,0:T(8,128)(2,1)S(1)}, bf16[4,256,256]{2,1,0:T(8,128)(2,1)S(1)}, u32[]{:S(2)}, u32[]{:S(2)}) collective-permute-start(bf16[4,256,256]{2,1,0:T(8,128)(2,1)S(1)} %get-tuple-element.152), channel_id=1, source_target_pairs={{0,8},{4,12},{8,0},{12,4},{16,24},{20,28},{24,16},{28,20},{1,9},{5... | collective-permute-start | bytes 1572872 | tf_op jit(solution)/shard_map/ppermute | solution.py:701
  96.6 18.6 %collective-permute-start.11 = (bf16[704,512]{1,0:T(8,128)(2,1)S(1)}, bf16[704,512]{1,0:T(8,128)(2,1)S(1)}, u32[]{:S(2)}, u32[]{:S(2)}) collective-permute-start(bf16[704,512]{1,0:T(8,128)(2,1)S(1)} %shard_map.209), channel_id=1, source_target_pairs={{0,2},{1,3},{2,0},{3,1},{4,6},{5,7},{6,4},{7,5},{8,10},{9,11},{10,... | collective-permute-start | bytes 2162696 | tf_op jit(solution)/shard_map/ppermute | solution.py:701
  98.0 14.0 %collective-permute-start.12 = (bf16[4,256,256]{2,1,0:T(8,128)(2,1)S(1)}, bf16[4,256,256]{2,1,0:T(8,128)(2,1)S(1)}, u32[]{:S(2)}, u32[]{:S(2)}) collective-permute-start(bf16[4,256,256]{2,1,0:T(8,128)(2,1)S(1)} %get-tuple-element.177), channel_id=1, source_target_pairs={{0,4},{4,0},{8,12},{12,8},{16,20},{20,16},{24,28},{28,24},{1,5},{5... | collective-permute-start | bytes 1572872 | tf_op jit(solution)/shard_map/ppermute | solution.py:701
  98.2 13.8 %collective-permute-start.13 = (bf16[4,256,256]{2,1,0:T(8,128)(2,1)S(1)}, bf16[4,256,256]{2,1,0:T(8,128)(2,1)S(1)}, u32[]{:S(2)}, u32[]{:S(2)}) collective-permute-start(bf16[4,256,256]{2,1,0:T(8,128)(2,1)S(1)} %get-tuple-element.178), channel_id=1, source_target_pairs={{0,8},{4,12},{8,0},{12,4},{16,24},{20,28},{24,16},{28,20},{1,9},{5... | collective-permute-start | bytes 1572872 | tf_op jit(solution)/shard_map/ppermute | solution.py:701
  112.3 9.4 %collective-permute-start.14 = (bf16[2,256,256]{2,1,0:T(8,128)(2,1)S(1)}, bf16[2,256,256]{2,1,0:T(8,128)(2,1)S(1)}, u32[]{:S(2)}, u32[]{:S(2)}) collective-permute-start(bf16[2,256,256]{2,1,0:T(8,128)(2,1)S(1)} %get-tuple-element.188), channel_id=1, source_target_pairs={{0,8},{4,12},{8,0},{12,4},{16,24},{20,28},{24,16},{28,20},{1,9},{5... | collective-permute-start | bytes 786440 | tf_op jit(solution)/shard_map/ppermute | solution.py:701
  113.4 8.3 %collective-permute-start.15 = (bf16[2,256,256]{2,1,0:T(8,128)(2,1)S(1)}, bf16[2,256,256]{2,1,0:T(8,128)(2,1)S(1)}, u32[]{:S(2)}, u32[]{:S(2)}) collective-permute-start(bf16[2,256,256]{2,1,0:T(8,128)(2,1)S(1)} %get-tuple-element.190), channel_id=1, source_target_pairs={{0,4},{4,0},{8,12},{12,8},{16,20},{20,16},{24,28},{28,24},{1,5},{5... | collective-permute-start | bytes 786440 | tf_op jit(solution)/shard_map/ppermute | solution.py:701
  120.3 22.5 %collective-permute-start.17 = (bf16[4,256,256]{2,1,0:T(8,128)(2,1)S(1)}, bf16[4,256,256]{2,1,0:T(8,128)(2,1)S(1)}, u32[]{:S(2)}, u32[]{:S(2)}) collective-permute-start(bf16[4,256,256]{2,1,0:T(8,128)(2,1)S(1)} %get-tuple-element.196), channel_id=1, source_target_pairs={{0,4},{4,0},{8,12},{12,8},{16,20},{20,16},{24,28},{28,24},{1,5},{5... | collective-permute-start | bytes 1572872 | tf_op jit(solution)/shard_map/ppermute | solution.py:701
  120.6 22.2 %collective-permute-start.18 = (bf16[4,256,256]{2,1,0:T(8,128)(2,1)S(1)}, bf16[4,256,256]{2,1,0:T(8,128)(2,1)S(1)}, u32[]{:S(2)}, u32[]{:S(2)}) collective-permute-start(bf16[4,256,256]{2,1,0:T(8,128)(2,1)S(1)} %get-tuple-element.197), channel_id=1, source_target_pairs={{0,8},{4,12},{8,0},{12,4},{16,24},{20,28},{24,16},{28,20},{1,9},{5... | collective-permute-start | bytes 1572872 | tf_op jit(solution)/shard_map/ppermute | solution.py:701
  121.7 21.1 %collective-permute-start.16 = (bf16[256,512]{1,0:T(8,128)(2,1)S(1)}, bf16[256,512]{1,0:T(8,128)(2,1)S(1)}, u32[]{:S(2)}, u32[]{:S(2)}) collective-permute-start(bf16[256,512]{1,0:T(8,128)(2,1)S(1)} %get-tuple-element.194), channel_id=1, source_target_pairs={{0,16},{4,20},{8,24},{12,28},{16,0},{20,4},{24,8},{28,12},{1,17},{... | collective-permute-start | bytes 786440 | tf_op jit(solution)/shard_map/ppermute | solution.py:701
  144.2 14.8 %collective-permute-start.20 = (bf16[2,256,256]{2,1,0:T(8,128)(2,1)S(1)}, bf16[2,256,256]{2,1,0:T(8,128)(2,1)S(1)}, u32[]{:S(2)}, u32[]{:S(2)}) collective-permute-start(bf16[2,256,256]{2,1,0:T(8,128)(2,1)S(1)} %get-tuple-element.215), channel_id=1, source_target_pairs={{0,8},{4,12},{8,0},{12,4},{16,24},{20,28},{24,16},{28,20},{1,9},{5... | collective-permute-start | bytes 786440 | tf_op jit(solution)/shard_map/ppermute | solution.py:701
  144.3 14.6 %collective-permute-start.21 = (bf16[2,256,256]{2,1,0:T(8,128)(2,1)S(1)}, bf16[2,256,256]{2,1,0:T(8,128)(2,1)S(1)}, u32[]{:S(2)}, u32[]{:S(2)}) collective-permute-start(bf16[2,256,256]{2,1,0:T(8,128)(2,1)S(1)} %get-tuple-element.217), channel_id=1, source_target_pairs={{0,4},{4,0},{8,12},{12,8},{16,20},{20,16},{24,28},{28,24},{1,5},{5... | collective-permute-start | bytes 786440 | tf_op jit(solution)/shard_map/ppermute | solution.py:701
  145.3 19.0 %collective-permute-start.32 = (bf16[256,512]{1,0:T(8,128)(2,1)S(1)}, bf16[256,512]{1,0:T(8,128)(2,1)S(1)}, u32[]{:S(2)}, u32[]{:S(2)}) collective-permute-start(bf16[256,512]{1,0:T(8,128)(2,1)S(1)} %add_convert_fusion.refs_0_), channel_id=1, source_target_pairs={{0,8},{4,12},{8,0},{12,4},{16,24},{20,28},{24,16},{28,20},{1,9},{5... | collective-permute-start | bytes 786440 | tf_op jit(solution)/shard_map/ppermute | solution.py:701
  146.8 17.5 %collective-permute-start.33 = (bf16[256,512]{1,0:T(8,128)(2,1)S(1)}, bf16[256,512]{1,0:T(8,128)(2,1)S(1)}, u32[]{:S(2)}, u32[]{:S(2)}) collective-permute-start(bf16[256,512]{1,0:T(8,128)(2,1)S(1)} %add_convert_fusion.refs_0_), channel_id=1, source_target_pairs={{0,4},{4,0},{8,12},{12,8},{16,20},{20,16},{24,28},{28,24},{1,5},{5... | collective-permute-start | bytes 786440 | tf_op jit(solution)/shard_map/ppermute | solution.py:701
  148.4 16.2 %collective-permute-start.31 = (bf16[256,512]{1,0:T(8,128)(2,1)S(1)}, bf16[256,512]{1,0:T(8,128)(2,1)S(1)}, u32[]{:S(2)}, u32[]{:S(2)}) collective-permute-start(bf16[256,512]{1,0:T(8,128)(2,1)S(1)} %add_convert_fusion.refs_0_), channel_id=1, source_target_pairs={{0,16},{4,20},{8,24},{12,28},{16,0},{20,4},{24,8},{28,12},{1,17},{... | collective-permute-start | bytes 786440 | tf_op jit(solution)/shard_map/ppermute | solution.py:701
  159.0 16.6 %collective-permute-start.22 = (bf16[256,512]{1,0:T(8,128)(2,1)S(1)}, bf16[256,512]{1,0:T(8,128)(2,1)S(1)}, u32[]{:S(2)}, u32[]{:S(2)}) collective-permute-start(bf16[256,512]{1,0:T(8,128)(2,1)S(1)} %get-tuple-element.219), channel_id=1, source_target_pairs={{0,16},{4,20},{8,24},{12,28},{16,0},{20,4},{24,8},{28,12},{1,17},{... | collective-permute-start | bytes 786440 | tf_op jit(solution)/shard_map/ppermute | solution.py:701
  164.3 12.9 %collective-permute-start.35 = (bf16[256,512]{1,0:T(8,128)(2,1)S(1)}, bf16[256,512]{1,0:T(8,128)(2,1)S(1)}, u32[]{:S(2)}, u32[]{:S(2)}) collective-permute-start(bf16[256,512]{1,0:T(8,128)(2,1)S(1)} %collective-permute-done.32.refs_2_), channel_id=1, source_target_pairs={{0,4},{4,0},{8,12},{12,8},{16,20},{20,16},{24,28},{28,24},{1,5},{5... | collective-permute-start | bytes 786440 | tf_op jit(solution)/shard_map/ppermute | solution.py:701
  164.7 14.3 %collective-permute-start.34 = (bf16[256,512]{1,0:T(8,128)(2,1)S(1)}, bf16[256,512]{1,0:T(8,128)(2,1)S(1)}, u32[]{:S(2)}, u32[]{:S(2)}) collective-permute-start(bf16[256,512]{1,0:T(8,128)(2,1)S(1)} %collective-permute-done.31.refs_1_), channel_id=1, source_target_pairs={{0,8},{4,12},{8,0},{12,4},{16,24},{20,28},{24,16},{28,20},{1,9},{5... | collective-permute-start | bytes 786440 | tf_op jit(solution)/shard_map/ppermute | solution.py:701
  166.4 37.6 %collective-permute-start.23 = (bf16[704,512]{1,0:T(8,128)(2,1)S(1)}, bf16[704,512]{1,0:T(8,128)(2,1)S(1)}, u32[]{:S(2)}, u32[]{:S(2)}) collective-permute-start(bf16[704,512]{1,0:T(8,128)(2,1)S(1)} %shard_map.217), channel_id=1, source_target_pairs={{0,2},{1,3},{2,0},{3,1},{4,6},{5,7},{6,4},{7,5},{8,10},{9,11},{10,... | collective-permute-start | bytes 2162696 | tf_op jit(solution)/shard_map/ppermute | solution.py:701
  175.8 12.1 %collective-permute-start.25 = (bf16[256,512]{1,0:T(8,128)(2,1)S(1)}, bf16[256,512]{1,0:T(8,128)(2,1)S(1)}, u32[]{:S(2)}, u32[]{:S(2)}) collective-permute-start(bf16[256,512]{1,0:T(8,128)(2,1)S(1)} %add_convert_fusion.1.refs_0_), channel_id=1, source_target_pairs={{0,8},{4,12},{8,0},{12,4},{16,24},{20,28},{24,16},{28,20},{1,9},{5... | collective-permute-start | bytes 786440 | tf_op jit(solution)/shard_map/ppermute | solution.py:701
  175.8 13.2 %collective-permute-start.26 = (bf16[256,512]{1,0:T(8,128)(2,1)S(1)}, bf16[256,512]{1,0:T(8,128)(2,1)S(1)}, u32[]{:S(2)}, u32[]{:S(2)}) collective-permute-start(bf16[256,512]{1,0:T(8,128)(2,1)S(1)} %add_convert_fusion.1.refs_0_), channel_id=1, source_target_pairs={{0,4},{4,0},{8,12},{12,8},{16,20},{20,16},{24,28},{28,24},{1,5},{5... | collective-permute-start | bytes 786440 | tf_op jit(solution)/shard_map/ppermute | solution.py:701
  177.2 14.5 %collective-permute-start.24 = (bf16[256,512]{1,0:T(8,128)(2,1)S(1)}, bf16[256,512]{1,0:T(8,128)(2,1)S(1)}, u32[]{:S(2)}, u32[]{:S(2)}) collective-permute-start(bf16[256,512]{1,0:T(8,128)(2,1)S(1)} %add_convert_fusion.1.refs_0_), channel_id=1, source_target_pairs={{0,16},{4,20},{8,24},{12,28},{16,0},{20,4},{24,8},{28,12},{1,17},{... | collective-permute-start | bytes 786440 | tf_op jit(solution)/shard_map/ppermute | solution.py:701
  179.0 13.9 %collective-permute-start.36 = (bf16[256,512]{1,0:T(8,128)(2,1)S(1)}, bf16[256,512]{1,0:T(8,128)(2,1)S(1)}, u32[]{:S(2)}, u32[]{:S(2)}) collective-permute-start(bf16[256,512]{1,0:T(8,128)(2,1)S(1)} %collective-permute-done.31.refs_1_), channel_id=1, source_target_pairs={{0,4},{4,0},{8,12},{12,8},{16,20},{20,16},{24,28},{28,24},{1,5},{5... | collective-permute-start | bytes 786440 | tf_op jit(solution)/shard_map/ppermute | solution.py:701
  187.9 9.2 %collective-permute-start.37 = (bf16[256,512]{1,0:T(8,128)(2,1)S(1)}, bf16[256,512]{1,0:T(8,128)(2,1)S(1)}, u32[]{:S(2)}, u32[]{:S(2)}) collective-permute-start(bf16[256,512]{1,0:T(8,128)(2,1)S(1)} %collective-permute-done.34.refs_3_), channel_id=1, source_target_pairs={{0,4},{4,0},{8,12},{12,8},{16,20},{20,16},{24,28},{28,24},{1,5},{5... | collective-permute-start | bytes 786440 | tf_op jit(solution)/shard_map/ppermute | solution.py:701
  189.1 13.7 %collective-permute-start.28 = (bf16[256,512]{1,0:T(8,128)(2,1)S(1)}, bf16[256,512]{1,0:T(8,128)(2,1)S(1)}, u32[]{:S(2)}, u32[]{:S(2)}) collective-permute-start(bf16[256,512]{1,0:T(8,128)(2,1)S(1)} %collective-permute-done.25.refs_2_), channel_id=1, source_target_pairs={{0,4},{4,0},{8,12},{12,8},{16,20},{20,16},{24,28},{28,24},{1,5},{5... | collective-permute-start | bytes 786440 | tf_op jit(solution)/shard_map/ppermute | solution.py:701
  191.6 11.1 %collective-permute-start.27 = (bf16[256,512]{1,0:T(8,128)(2,1)S(1)}, bf16[256,512]{1,0:T(8,128)(2,1)S(1)}, u32[]{:S(2)}, u32[]{:S(2)}) collective-permute-start(bf16[256,512]{1,0:T(8,128)(2,1)S(1)} %collective-permute-done.24.refs_1_), channel_id=1, source_target_pairs={{0,8},{4,12},{8,0},{12,4},{16,24},{20,28},{24,16},{28,20},{1,9},{5... | collective-permute-start | bytes 786440 | tf_op jit(solution)/shard_map/ppermute | solution.py:701
  199.6 9.2 %collective-permute-start.29 = (bf16[256,512]{1,0:T(8,128)(2,1)S(1)}, bf16[256,512]{1,0:T(8,128)(2,1)S(1)}, u32[]{:S(2)}, u32[]{:S(2)}) collective-permute-start(bf16[256,512]{1,0:T(8,128)(2,1)S(1)} %collective-permute-done.24.refs_1_), channel_id=1, source_target_pairs={{0,4},{4,0},{8,12},{12,8},{16,20},{20,16},{24,28},{28,24},{1,5},{5... | collective-permute-start | bytes 786440 | tf_op jit(solution)/shard_map/ppermute | solution.py:701
  202.7 9.4 %collective-permute-start.30 = (bf16[256,512]{1,0:T(8,128)(2,1)S(1)}, bf16[256,512]{1,0:T(8,128)(2,1)S(1)}, u32[]{:S(2)}, u32[]{:S(2)}) collective-permute-start(bf16[256,512]{1,0:T(8,128)(2,1)S(1)} %collective-permute-done.27.refs_3_), channel_id=1, source_target_pairs={{0,4},{4,0},{8,12},{12,8},{16,20},{20,16},{24,28},{28,24},{1,5},{5... | collective-permute-start | bytes 786440 | tf_op jit(solution)/shard_map/ppermute | solution.py:701
  (19 other events, 141.0 us)

commit v5 on v4

--- a/solution.py
+++ b/solution.py
@@ -13,7 +13,7 @@
 LANE = 128
 CHUNKS = 32
 GROUPS = CHUNKS // 8
-TOLERANCE = 1e-5
+TOLERANCE = 2e-5
 LOG2E = math.log2(math.e)
 LN2 = math.log(2.0)
 F32 = jnp.float32

time: 215 us -> 215 us (level)
  starting transfers between devices: 31.1 us -> 28.8 us
    ppermute x38, starting transfers between devices: 31.1 us -> 28.8 us  [swap(): return lax.ppermute(x, axis, [(i, i ^ bit) for i in range(n)])]
where the time goes in v5:
time: 215 us
  waiting for transfers between devices  85.3 us (40%)
  blocking collectives  53.3 us (25%)
  Pallas kernels  40.1 us (19%)
  starting transfers between devices  28.8 us (13%)
  local copies, waits for them, and re-layouts  3.78 us (2%)
  other arithmetic  2.67 us (1%)
    ppermute x38, waiting for transfers between devices, swap(): return lax.ppermute(x, axis, [(i, i ^ bit) for i in range(n)])  85.3 us
    all_to_all x4, blocking collectives, share(): return lax.all_to_all(stats, 'seq', 0, 0, tiled=True)  53.3 us
    ppermute x38, starting transfers between devices, swap(): return lax.ppermute(x, axis, [(i, i ^ bit) for i in range(n)])  28.8 us
    pallas_call x3, Pallas kernels, weight_parts(): call(functools.partial(weight_kernel, True), [shape(4, half, half, dtype=...  7.56 us
    pallas_call x1, Pallas kernels, per_device(): call(turn_kernel, [shape(length, real, dtype=BF16), shape(length, width),...  7.4 us
    pallas_call x1, Pallas kernels, per_device(): call(forward_kernel, [shape(length, real, dtype=BF16), shape(length, widt...  5.88 us
    pallas_call x2, Pallas kernels, weights(): call(functools.partial(spread_kernel, True), shape(4 * real, real), [pltp...  4.93 us
  transfers between devices with their start and end apart: 38, of which 16 were waited for; matrix products, arithmetic and copies ran while one was open for 1% of the time, Pallas kernels for 10%

profile of v5, /device:TPU:0, one launch (start us, length us, event | category | flops | bytes accessed | tf_op | source)
XLA Modules:
  0.0 214.8 jit_solution(6003542032017773935)
XLA Ops:
  1.2 2.6 %collective-permute-start = (bf16[704,500]{1,0:T(8,128)(2,1)}, bf16[704,500]{1,0:T(8,128)(2,1)S(1)}, u32[]{:S(2)}, u32[]{:S(2)}) collective-permute-start(bf16[704,500]{1,0:T(8,128)(2,1)} %bitcast.13), channel_id=1, source_target_pairs={{0,2},{1,3},{2,0},{3,1},{4,6},{5,7},{6,4},{7,5},{8,10},{9,11},{10,... | collective-permute-start | bytes 2112008 | tf_op jit(solution)/shard_map/ppermute | solution.py:701
  3.7 1.6 copy-done.2
  8.8 11.9 %collective-permute-done.far_ref = bf16[704,500]{1,0:T(8,128)(2,1)S(1)} collective-permute-done((bf16[704,500]{1,0:T(8,128)(2,1)}, bf16[704,500]{1,0:T(8,128)(2,1)S(1)}, u32[]{:S(2)}, u32[]{:S(2)}) %collective-permute-start) | collective-permute-done | bytes 704032 | tf_op jit(solution)/shard_map/ppermute | solution.py:701
  21.3 1.6 collective-permute-done.2.cross_ref
  23.8 13.4 %all_to_all.20.stats_ref = f32[8,8,512]{2,1,0:T(8,128)S(1)} all-to-all(f32[8,8,512]{2,1,0:T(8,128)S(1)} %get-tuple-element.133), channel_id=1, replica_groups=mesh['seq'=8,'neur'=4] {'seq'}, dimensions={0} | all-to-all | bytes 262144 | tf_op jit(solution)/shard_map/all_to_all | solution.py:756
  37.1 5.9 %shard_map.199 = (bf16[704,500]{1,0:T(8,128)(2,1)}, f32[704,512]{1,0:T(8,128)S(1)}, f32[8,512]{1,0:T(8,128)S(1)}) custom-call(f32[8,8,512]{2,1,0:T(8,128)S(1)} %all_to_all.20.stats_ref, f32[704,512]{1,0:T(8,128)S(1)} %get-tuple-element.134.proj_ref, f32[8,512]{1,0:T(8,128)S(1)} %get-tuple-element.135.par_ref), custom_call_target="tpu_custom_call" | custom-call | tf_op jit(solution)/shard_map/pallas_call | solution.py:818
  45.6 2.5 %shard_map.203 = (bf16[4,256,256]{2,1,0:T(8,128)(2,1)S(1)}, bf16[4,256,256]{2,1,0:T(8,128)(2,1)S(1)}, bf16[4,256,256]{2,1,0:T(8,128)(2,1)S(1)}, bf16[4,256,256]{2,1,0:T(8,128)(2,1)S(1)}) custom-call(bf16[704,500]{1,0:T(8,128)(2,1)S(1)} %bitcast.15, bf16[704,500]{1,0:T(8,128)(2,1)S(1)} %collective-permute-done.1.mate_ref, ...), custom_call_target="tpu_custom_call" | custom-call | tf_op jit(solution)/shard_map/pallas_call | solution.py:797
  50.0 12.5 %collective-permute-done.3.far_ref = bf16[704,500]{1,0:T(8,128)(2,1)S(1)} collective-permute-done((bf16[704,500]{1,0:T(8,128)(2,1)S(1)}, bf16[704,500]{1,0:T(8,128)(2,1)S(1)}, u32[]{:S(2)}, u32[]{:S(2)}) %collective-permute-start.3) | collective-permute-done | bytes 704032 | tf_op jit(solution)/shard_map/ppermute | solution.py:701
  63.2 1.5 collective-permute-done.9.cross_ref
  65.6 10.0 %all_to_all.21.stats_ref = f32[8,8,512]{2,1,0:T(8,128)S(1)} all-to-all(f32[8,8,512]{2,1,0:T(8,128)S(1)} %get-tuple-element.158), channel_id=1, replica_groups=mesh['seq'=8,'neur'=4] {'seq'}, dimensions={0} | all-to-all | bytes 262144 | tf_op jit(solution)/shard_map/all_to_all | solution.py:756
  75.6 7.4 %shard_map.206 = (bf16[704,500]{1,0:T(8,128)(2,1)}, f32[704,512]{1,0:T(8,128)S(1)}, f32[8,8,512]{2,1,0:T(8,128)S(1)}, f32[8,512]{1,0:T(8,128)S(1)}, f32[2,500]{1,0:T(2,128)}, /*index=5*/f32[2,500]{1,0:T(2,128)}) custom-call(f32[8,8,512]{2,1,0:T(8,128)S(1)} %all_to_all.21.stats_ref, f32[704,512]{1,0:T(8,128)S(1)} %get-tuple-element.159.proj_ref, ...), custom_call_target="tpu_custom_call" | custom-call | tf_op jit(solution)/shard_map/pallas_call | solution.py:839
  83.0 9.8 %all_to_all.22.sums_ref = f32[8,8,512]{2,1,0:T(8,128)S(1)} all-to-all(f32[8,8,512]{2,1,0:T(8,128)S(1)} %get-tuple-element.162), channel_id=1, replica_groups=mesh['seq'=8,'neur'=4] {'seq'}, dimensions={0} | all-to-all | bytes 262144 | tf_op jit(solution)/shard_map/all_to_all | solution.py:756
  93.3 2.5 %shard_map.208 = (bf16[4,256,256]{2,1,0:T(8,128)(2,1)S(1)}, bf16[4,256,256]{2,1,0:T(8,128)(2,1)S(1)}, bf16[4,256,256]{2,1,0:T(8,128)(2,1)S(1)}, bf16[4,256,256]{2,1,0:T(8,128)(2,1)S(1)}) custom-call(bf16[704,500]{1,0:T(8,128)(2,1)S(1)} %copy-done.1, bf16[704,500]{1,0:T(8,128)(2,1)S(1)} %collective-permute-done.4.mate_ref, ...), custom_call_target="tpu_custom_call" | custom-call | tf_op jit(solution)/shard_map/pallas_call | solution.py:797
  100.2 11.8 %collective-permute-done.12.got_left_ref = bf16[4,256,256]{2,1,0:T(8,128)(2,1)S(1)} collective-permute-done((bf16[4,256,256]{2,1,0:T(8,128)(2,1)S(1)}, bf16[4,256,256]{2,1,0:T(8,128)(2,1)S(1)}, u32[]{:S(2)}, u32[]{:S(2)}) %collective-permute-start.12) | collective-permute-done | bytes 524320 | tf_op jit(solution)/shard_map/ppermute | solution.py:701
  115.4 2.6 %shard_map.212 = (f32[704,512]{1,0:T(8,128)S(1)}, f32[8,8,512]{2,1,0:T(8,128)S(1)}, bf16[704,512]{1,0:T(8,128)(2,1)S(1)}) custom-call(f32[704,512]{1,0:T(8,128)S(1)} %shard_map.210.keep_ref, bf16[704,512]{1,0:T(8,128)(2,1)S(1)} %collective-permute-done.11.got_ref, f32[704,512]{1,0:T(8,128)S(1)} %get-tuple-element.134.proj_ref, ...), custom_call_target="tpu_custom_call" | custom-call | tf_op jit(solution)/shard_map/pallas_call | solution.py:874
  118.0 2.5 %shard_map.214 = (bf16[4,256,256]{2,1,0:T(8,128)(2,1)S(1)}, bf16[4,256,256]{2,1,0:T(8,128)(2,1)S(1)}, bf16[4,256,256]{2,1,0:T(8,128)(2,1)S(1)}, bf16[4,256,256]{2,1,0:T(8,128)(2,1)S(1)}) custom-call(bf16[704,500]{1,0:T(8,128)(2,1)S(1)} %bitcast.16, bf16[704,500]{1,0:T(8,128)(2,1)S(1)} %collective-permute-done.1.mate_ref, ...), custom_call_target="tpu_custom_call" | custom-call | tf_op jit(solution)/shard_map/pallas_call | solution.py:797
  122.9 20.1 %all_to_all.23.sums_ref = f32[8,8,512]{2,1,0:T(8,128)S(1)} all-to-all(f32[8,8,512]{2,1,0:T(8,128)S(1)} %get-tuple-element.193), channel_id=1, replica_groups=mesh['seq'=8,'neur'=4] {'seq'}, dimensions={0} | all-to-all | bytes 262144 | tf_op jit(solution)/shard_map/all_to_all | solution.py:756
  145.5 1.5 collective-permute-start.32
  147.0 1.6 collective-permute-start.33
  149.4 9.8 %collective-permute-done.20.got_left_ref = bf16[2,256,256]{2,1,0:T(8,128)(2,1)S(1)} collective-permute-done((bf16[2,256,256]{2,1,0:T(8,128)(2,1)S(1)}, bf16[2,256,256]{2,1,0:T(8,128)(2,1)S(1)}, u32[]{:S(2)}, u32[]{:S(2)}) %collective-permute-start.20) | collective-permute-done | bytes 262176 | tf_op jit(solution)/shard_map/ppermute | solution.py:701
  159.3 5.1 %collective-permute-done.32.refs_2_ = bf16[256,512]{1,0:T(8,128)(2,1)S(1)} collective-permute-done((bf16[256,512]{1,0:T(8,128)(2,1)S(1)}, bf16[256,512]{1,0:T(8,128)(2,1)S(1)}, u32[]{:S(2)}, u32[]{:S(2)}) %collective-permute-start.32) | collective-permute-done | bytes 262176 | tf_op jit(solution)/shard_map/ppermute | solution.py:701
  168.7 7.2 %collective-permute-done.22 = bf16[256,512]{1,0:T(8,128)(2,1)S(1)} collective-permute-done((bf16[256,512]{1,0:T(8,128)(2,1)S(1)}, bf16[256,512]{1,0:T(8,128)(2,1)S(1)}, u32[]{:S(2)}, u32[]{:S(2)}) %collective-permute-start.22) | collective-permute-done | bytes 262176 | tf_op jit(solution)/shard_map/ppermute | solution.py:701
  177.4 1.8 collective-permute-start.24
  179.2 1.4 collective-permute-start.36
  180.6 7.4 %collective-permute-done.25.refs_2_ = bf16[256,512]{1,0:T(8,128)(2,1)S(1)} collective-permute-done((bf16[256,512]{1,0:T(8,128)(2,1)S(1)}, bf16[256,512]{1,0:T(8,128)(2,1)S(1)}, u32[]{:S(2)}, u32[]{:S(2)}) %collective-permute-start.25) | collective-permute-done | bytes 262176 | tf_op jit(solution)/shard_map/ppermute | solution.py:701
  190.1 1.8 collective-permute-done.24.refs_1_
  193.1 4.2 %collective-permute-done.37.refs_7_ = bf16[256,512]{1,0:T(8,128)(2,1)S(1)} collective-permute-done((bf16[256,512]{1,0:T(8,128)(2,1)S(1)}, bf16[256,512]{1,0:T(8,128)(2,1)S(1)}, u32[]{:S(2)}, u32[]{:S(2)}) %collective-permute-start.37) | collective-permute-done | bytes 262176 | tf_op jit(solution)/shard_map/ppermute | solution.py:701
  197.3 2.5 %shard_map.221 = f32[2000,500]{1,0:T(8,128)} custom-call(bf16[256,512]{1,0:T(8,128)(2,1)S(1)} %add_convert_fusion.refs_0_, bf16[256,512]{1,0:T(8,128)(2,1)S(1)} %collective-permute-done.31.refs_1_, bf16[256,512]{1,0:T(8,128)(2,1)S(1)} %collective-permute-done.32.refs_2_, bf16[256,512]{1,0:T(8,128)(2,1)S(1)} %collective-permute-done.34.refs_3_, ...), custom_call_target="tpu_custom_call" | custom-call | tf_op jit(solution)/shard_map/pallas_call | solution.py:806
  201.0 1.9 collective-permute-done.28.refs_6_
  205.5 3.6 %collective-permute-done.29.refs_5_ = bf16[256,512]{1,0:T(8,128)(2,1)S(1)} collective-permute-done((bf16[256,512]{1,0:T(8,128)(2,1)S(1)}, bf16[256,512]{1,0:T(8,128)(2,1)S(1)}, u32[]{:S(2)}, u32[]{:S(2)}) %collective-permute-start.29) | collective-permute-done | bytes 262176 | tf_op jit(solution)/shard_map/ppermute | solution.py:701
  209.0 3.4 %collective-permute-done.30.refs_7_ = bf16[256,512]{1,0:T(8,128)(2,1)S(1)} collective-permute-done((bf16[256,512]{1,0:T(8,128)(2,1)S(1)}, bf16[256,512]{1,0:T(8,128)(2,1)S(1)}, u32[]{:S(2)}, u32[]{:S(2)}) %collective-permute-start.30) | collective-permute-done | bytes 262176 | tf_op jit(solution)/shard_map/ppermute | solution.py:701
  212.4 2.5 %shard_map.220 = f32[2000,500]{1,0:T(8,128)} custom-call(bf16[256,512]{1,0:T(8,128)(2,1)S(1)} %add_convert_fusion.1.refs_0_, bf16[256,512]{1,0:T(8,128)(2,1)S(1)} %collective-permute-done.24.refs_1_, bf16[256,512]{1,0:T(8,128)(2,1)S(1)} %collective-permute-done.25.refs_2_, bf16[256,512]{1,0:T(8,128)(2,1)S(1)} %collective-permute-done.27.refs_3_, ...), custom_call_target="tpu_custom_call" | custom-call | tf_op jit(solution)/shard_map/pallas_call | solution.py:806
  (109 shorter events, 38.1 us)
Async XLA Ops:
  1.2 19.5 %collective-permute-start = (bf16[704,500]{1,0:T(8,128)(2,1)}, bf16[704,500]{1,0:T(8,128)(2,1)S(1)}, u32[]{:S(2)}, u32[]{:S(2)}) collective-permute-start(bf16[704,500]{1,0:T(8,128)(2,1)} %bitcast.13), channel_id=1, source_target_pairs={{0,2},{1,3},{2,0},{3,1},{4,6},{5,7},{6,4},{7,5},{8,10},{9,11},{10,... | collective-permute-start | bytes 2112008 | tf_op jit(solution)/shard_map/ppermute | solution.py:701
  43.4 19.1 %collective-permute-start.6 = (bf16[2,512,512]{2,1,0:T(8,128)(2,1)S(1)}, bf16[2,512,512]{2,1,0:T(8,128)(2,1)S(1)}, u32[]{:S(2)}, u32[]{:S(2)}) collective-permute-start(bf16[2,512,512]{2,1,0:T(8,128)(2,1)S(1)} %get-tuple-element.144), channel_id=1, source_target_pairs={{0,1},{1,0},{2,3},{3,2},{4,5},{5,4},{6,7},{7,6},{8,9},{9,8},{10,11... | collective-permute-start | bytes 3145736 | tf_op jit(solution)/shard_map/ppermute | solution.py:701
  43.9 18.6 %collective-permute-start.5 = (bf16[2,512,512]{2,1,0:T(8,128)(2,1)S(1)}, bf16[2,512,512]{2,1,0:T(8,128)(2,1)S(1)}, u32[]{:S(2)}, u32[]{:S(2)}) collective-permute-start(bf16[2,512,512]{2,1,0:T(8,128)(2,1)S(1)} %get-tuple-element.142), channel_id=1, source_target_pairs={{0,1},{1,0},{2,3},{3,2},{4,5},{5,4},{6,7},{7,6},{8,9},{9,8},{10,11... | collective-permute-start | bytes 3145736 | tf_op jit(solution)/shard_map/ppermute | solution.py:701
  44.1 18.4 %collective-permute-start.3 = (bf16[704,500]{1,0:T(8,128)(2,1)S(1)}, bf16[704,500]{1,0:T(8,128)(2,1)S(1)}, u32[]{:S(2)}, u32[]{:S(2)}) collective-permute-start(bf16[704,500]{1,0:T(8,128)(2,1)S(1)} %copy-done.1), channel_id=1, source_target_pairs={{0,2},{1,3},{2,0},{3,1},{4,6},{5,7},{6,4},{7,5},{8,10},{9,11},{10,... | collective-permute-start | bytes 2112008 | tf_op jit(solution)/shard_map/ppermute | solution.py:701
  48.1 14.4 %collective-permute-start.7 = (bf16[4,256,256]{2,1,0:T(8,128)(2,1)S(1)}, bf16[4,256,256]{2,1,0:T(8,128)(2,1)S(1)}, u32[]{:S(2)}, u32[]{:S(2)}) collective-permute-start(bf16[4,256,256]{2,1,0:T(8,128)(2,1)S(1)} %get-tuple-element.150), channel_id=1, source_target_pairs={{0,4},{4,0},{8,12},{12,8},{16,20},{20,16},{24,28},{28,24},{1,5},{5... | collective-permute-start | bytes 1572872 | tf_op jit(solution)/shard_map/ppermute | solution.py:701
  48.8 13.7 %collective-permute-start.8 = (bf16[4,256,256]{2,1,0:T(8,128)(2,1)S(1)}, bf16[4,256,256]{2,1,0:T(8,128)(2,1)S(1)}, u32[]{:S(2)}, u32[]{:S(2)}) collective-permute-start(bf16[4,256,256]{2,1,0:T(8,128)(2,1)S(1)} %get-tuple-element.152), channel_id=1, source_target_pairs={{0,8},{4,12},{8,0},{12,4},{16,24},{20,28},{24,16},{28,20},{1,9},{5... | collective-permute-start | bytes 1572872 | tf_op jit(solution)/shard_map/ppermute | solution.py:701
  96.8 18.6 %collective-permute-start.11 = (bf16[704,512]{1,0:T(8,128)(2,1)S(1)}, bf16[704,512]{1,0:T(8,128)(2,1)S(1)}, u32[]{:S(2)}, u32[]{:S(2)}) collective-permute-start(bf16[704,512]{1,0:T(8,128)(2,1)S(1)} %shard_map.209), channel_id=1, source_target_pairs={{0,2},{1,3},{2,0},{3,1},{4,6},{5,7},{6,4},{7,5},{8,10},{9,11},{10,... | collective-permute-start | bytes 2162696 | tf_op jit(solution)/shard_map/ppermute | solution.py:701
  98.0 14.0 %collective-permute-start.12 = (bf16[4,256,256]{2,1,0:T(8,128)(2,1)S(1)}, bf16[4,256,256]{2,1,0:T(8,128)(2,1)S(1)}, u32[]{:S(2)}, u32[]{:S(2)}) collective-permute-start(bf16[4,256,256]{2,1,0:T(8,128)(2,1)S(1)} %get-tuple-element.177), channel_id=1, source_target_pairs={{0,4},{4,0},{8,12},{12,8},{16,20},{20,16},{24,28},{28,24},{1,5},{5... | collective-permute-start | bytes 1572872 | tf_op jit(solution)/shard_map/ppermute | solution.py:701
  98.2 13.8 %collective-permute-start.13 = (bf16[4,256,256]{2,1,0:T(8,128)(2,1)S(1)}, bf16[4,256,256]{2,1,0:T(8,128)(2,1)S(1)}, u32[]{:S(2)}, u32[]{:S(2)}) collective-permute-start(bf16[4,256,256]{2,1,0:T(8,128)(2,1)S(1)} %get-tuple-element.178), channel_id=1, source_target_pairs={{0,8},{4,12},{8,0},{12,4},{16,24},{20,28},{24,16},{28,20},{1,9},{5... | collective-permute-start | bytes 1572872 | tf_op jit(solution)/shard_map/ppermute | solution.py:701
  112.3 9.6 %collective-permute-start.14 = (bf16[2,256,256]{2,1,0:T(8,128)(2,1)S(1)}, bf16[2,256,256]{2,1,0:T(8,128)(2,1)S(1)}, u32[]{:S(2)}, u32[]{:S(2)}) collective-permute-start(bf16[2,256,256]{2,1,0:T(8,128)(2,1)S(1)} %get-tuple-element.188), channel_id=1, source_target_pairs={{0,8},{4,12},{8,0},{12,4},{16,24},{20,28},{24,16},{28,20},{1,9},{5... | collective-permute-start | bytes 786440 | tf_op jit(solution)/shard_map/ppermute | solution.py:701
  113.4 8.5 %collective-permute-start.15 = (bf16[2,256,256]{2,1,0:T(8,128)(2,1)S(1)}, bf16[2,256,256]{2,1,0:T(8,128)(2,1)S(1)}, u32[]{:S(2)}, u32[]{:S(2)}) collective-permute-start(bf16[2,256,256]{2,1,0:T(8,128)(2,1)S(1)} %get-tuple-element.190), channel_id=1, source_target_pairs={{0,4},{4,0},{8,12},{12,8},{16,20},{20,16},{24,28},{28,24},{1,5},{5... | collective-permute-start | bytes 786440 | tf_op jit(solution)/shard_map/ppermute | solution.py:701
  120.5 22.5 %collective-permute-start.17 = (bf16[4,256,256]{2,1,0:T(8,128)(2,1)S(1)}, bf16[4,256,256]{2,1,0:T(8,128)(2,1)S(1)}, u32[]{:S(2)}, u32[]{:S(2)}) collective-permute-start(bf16[4,256,256]{2,1,0:T(8,128)(2,1)S(1)} %get-tuple-element.196), channel_id=1, source_target_pairs={{0,4},{4,0},{8,12},{12,8},{16,20},{20,16},{24,28},{28,24},{1,5},{5... | collective-permute-start | bytes 1572872 | tf_op jit(solution)/shard_map/ppermute | solution.py:701
  120.8 22.3 %collective-permute-start.18 = (bf16[4,256,256]{2,1,0:T(8,128)(2,1)S(1)}, bf16[4,256,256]{2,1,0:T(8,128)(2,1)S(1)}, u32[]{:S(2)}, u32[]{:S(2)}) collective-permute-start(bf16[4,256,256]{2,1,0:T(8,128)(2,1)S(1)} %get-tuple-element.197), channel_id=1, source_target_pairs={{0,8},{4,12},{8,0},{12,4},{16,24},{20,28},{24,16},{28,20},{1,9},{5... | collective-permute-start | bytes 1572872 | tf_op jit(solution)/shard_map/ppermute | solution.py:701
  121.9 21.1 %collective-permute-start.16 = (bf16[256,512]{1,0:T(8,128)(2,1)S(1)}, bf16[256,512]{1,0:T(8,128)(2,1)S(1)}, u32[]{:S(2)}, u32[]{:S(2)}) collective-permute-start(bf16[256,512]{1,0:T(8,128)(2,1)S(1)} %get-tuple-element.194), channel_id=1, source_target_pairs={{0,16},{4,20},{8,24},{12,28},{16,0},{20,4},{24,8},{28,12},{1,17},{... | collective-permute-start | bytes 786440 | tf_op jit(solution)/shard_map/ppermute | solution.py:701
  144.4 14.8 %collective-permute-start.20 = (bf16[2,256,256]{2,1,0:T(8,128)(2,1)S(1)}, bf16[2,256,256]{2,1,0:T(8,128)(2,1)S(1)}, u32[]{:S(2)}, u32[]{:S(2)}) collective-permute-start(bf16[2,256,256]{2,1,0:T(8,128)(2,1)S(1)} %get-tuple-element.215), channel_id=1, source_target_pairs={{0,8},{4,12},{8,0},{12,4},{16,24},{20,28},{24,16},{28,20},{1,9},{5... | collective-permute-start | bytes 786440 | tf_op jit(solution)/shard_map/ppermute | solution.py:701
  144.6 14.6 %collective-permute-start.21 = (bf16[2,256,256]{2,1,0:T(8,128)(2,1)S(1)}, bf16[2,256,256]{2,1,0:T(8,128)(2,1)S(1)}, u32[]{:S(2)}, u32[]{:S(2)}) collective-permute-start(bf16[2,256,256]{2,1,0:T(8,128)(2,1)S(1)} %get-tuple-element.217), channel_id=1, source_target_pairs={{0,4},{4,0},{8,12},{12,8},{16,20},{20,16},{24,28},{28,24},{1,5},{5... | collective-permute-start | bytes 786440 | tf_op jit(solution)/shard_map/ppermute | solution.py:701
  145.5 19.0 %collective-permute-start.32 = (bf16[256,512]{1,0:T(8,128)(2,1)S(1)}, bf16[256,512]{1,0:T(8,128)(2,1)S(1)}, u32[]{:S(2)}, u32[]{:S(2)}) collective-permute-start(bf16[256,512]{1,0:T(8,128)(2,1)S(1)} %add_convert_fusion.refs_0_), channel_id=1, source_target_pairs={{0,8},{4,12},{8,0},{12,4},{16,24},{20,28},{24,16},{28,20},{1,9},{5... | collective-permute-start | bytes 786440 | tf_op jit(solution)/shard_map/ppermute | solution.py:701
  147.0 17.5 %collective-permute-start.33 = (bf16[256,512]{1,0:T(8,128)(2,1)S(1)}, bf16[256,512]{1,0:T(8,128)(2,1)S(1)}, u32[]{:S(2)}, u32[]{:S(2)}) collective-permute-start(bf16[256,512]{1,0:T(8,128)(2,1)S(1)} %add_convert_fusion.refs_0_), channel_id=1, source_target_pairs={{0,4},{4,0},{8,12},{12,8},{16,20},{20,16},{24,28},{28,24},{1,5},{5... | collective-permute-start | bytes 786440 | tf_op jit(solution)/shard_map/ppermute | solution.py:701
  148.6 16.2 %collective-permute-start.31 = (bf16[256,512]{1,0:T(8,128)(2,1)S(1)}, bf16[256,512]{1,0:T(8,128)(2,1)S(1)}, u32[]{:S(2)}, u32[]{:S(2)}) collective-permute-start(bf16[256,512]{1,0:T(8,128)(2,1)S(1)} %add_convert_fusion.refs_0_), channel_id=1, source_target_pairs={{0,16},{4,20},{8,24},{12,28},{16,0},{20,4},{24,8},{28,12},{1,17},{... | collective-permute-start | bytes 786440 | tf_op jit(solution)/shard_map/ppermute | solution.py:701
  159.3 16.6 %collective-permute-start.22 = (bf16[256,512]{1,0:T(8,128)(2,1)S(1)}, bf16[256,512]{1,0:T(8,128)(2,1)S(1)}, u32[]{:S(2)}, u32[]{:S(2)}) collective-permute-start(bf16[256,512]{1,0:T(8,128)(2,1)S(1)} %get-tuple-element.219), channel_id=1, source_target_pairs={{0,16},{4,20},{8,24},{12,28},{16,0},{20,4},{24,8},{28,12},{1,17},{... | collective-permute-start | bytes 786440 | tf_op jit(solution)/shard_map/ppermute | solution.py:701
  164.5 12.9 %collective-permute-start.35 = (bf16[256,512]{1,0:T(8,128)(2,1)S(1)}, bf16[256,512]{1,0:T(8,128)(2,1)S(1)}, u32[]{:S(2)}, u32[]{:S(2)}) collective-permute-start(bf16[256,512]{1,0:T(8,128)(2,1)S(1)} %collective-permute-done.32.refs_2_), channel_id=1, source_target_pairs={{0,4},{4,0},{8,12},{12,8},{16,20},{20,16},{24,28},{28,24},{1,5},{5... | collective-permute-start | bytes 786440 | tf_op jit(solution)/shard_map/ppermute | solution.py:701
  164.9 14.3 %collective-permute-start.34 = (bf16[256,512]{1,0:T(8,128)(2,1)S(1)}, bf16[256,512]{1,0:T(8,128)(2,1)S(1)}, u32[]{:S(2)}, u32[]{:S(2)}) collective-permute-start(bf16[256,512]{1,0:T(8,128)(2,1)S(1)} %collective-permute-done.31.refs_1_), channel_id=1, source_target_pairs={{0,8},{4,12},{8,0},{12,4},{16,24},{20,28},{24,16},{28,20},{1,9},{5... | collective-permute-start | bytes 786440 | tf_op jit(solution)/shard_map/ppermute | solution.py:701
  166.6 37.6 %collective-permute-start.23 = (bf16[704,512]{1,0:T(8,128)(2,1)S(1)}, bf16[704,512]{1,0:T(8,128)(2,1)S(1)}, u32[]{:S(2)}, u32[]{:S(2)}) collective-permute-start(bf16[704,512]{1,0:T(8,128)(2,1)S(1)} %shard_map.217), channel_id=1, source_target_pairs={{0,2},{1,3},{2,0},{3,1},{4,6},{5,7},{6,4},{7,5},{8,10},{9,11},{10,... | collective-permute-start | bytes 2162696 | tf_op jit(solution)/shard_map/ppermute | solution.py:701
  176.0 12.1 %collective-permute-start.25 = (bf16[256,512]{1,0:T(8,128)(2,1)S(1)}, bf16[256,512]{1,0:T(8,128)(2,1)S(1)}, u32[]{:S(2)}, u32[]{:S(2)}) collective-permute-start(bf16[256,512]{1,0:T(8,128)(2,1)S(1)} %add_convert_fusion.1.refs_0_), channel_id=1, source_target_pairs={{0,8},{4,12},{8,0},{12,4},{16,24},{20,28},{24,16},{28,20},{1,9},{5... | collective-permute-start | bytes 786440 | tf_op jit(solution)/shard_map/ppermute | solution.py:701
  176.1 13.2 %collective-permute-start.26 = (bf16[256,512]{1,0:T(8,128)(2,1)S(1)}, bf16[256,512]{1,0:T(8,128)(2,1)S(1)}, u32[]{:S(2)}, u32[]{:S(2)}) collective-permute-start(bf16[256,512]{1,0:T(8,128)(2,1)S(1)} %add_convert_fusion.1.refs_0_), channel_id=1, source_target_pairs={{0,4},{4,0},{8,12},{12,8},{16,20},{20,16},{24,28},{28,24},{1,5},{5... | collective-permute-start | bytes 786440 | tf_op jit(solution)/shard_map/ppermute | solution.py:701
  177.4 14.4 %collective-permute-start.24 = (bf16[256,512]{1,0:T(8,128)(2,1)S(1)}, bf16[256,512]{1,0:T(8,128)(2,1)S(1)}, u32[]{:S(2)}, u32[]{:S(2)}) collective-permute-start(bf16[256,512]{1,0:T(8,128)(2,1)S(1)} %add_convert_fusion.1.refs_0_), channel_id=1, source_target_pairs={{0,16},{4,20},{8,24},{12,28},{16,0},{20,4},{24,8},{28,12},{1,17},{... | collective-permute-start | bytes 786440 | tf_op jit(solution)/shard_map/ppermute | solution.py:701
  179.2 13.9 %collective-permute-start.36 = (bf16[256,512]{1,0:T(8,128)(2,1)S(1)}, bf16[256,512]{1,0:T(8,128)(2,1)S(1)}, u32[]{:S(2)}, u32[]{:S(2)}) collective-permute-start(bf16[256,512]{1,0:T(8,128)(2,1)S(1)} %collective-permute-done.31.refs_1_), channel_id=1, source_target_pairs={{0,4},{4,0},{8,12},{12,8},{16,20},{20,16},{24,28},{28,24},{1,5},{5... | collective-permute-start | bytes 786440 | tf_op jit(solution)/shard_map/ppermute | solution.py:701
  188.1 9.2 %collective-permute-start.37 = (bf16[256,512]{1,0:T(8,128)(2,1)S(1)}, bf16[256,512]{1,0:T(8,128)(2,1)S(1)}, u32[]{:S(2)}, u32[]{:S(2)}) collective-permute-start(bf16[256,512]{1,0:T(8,128)(2,1)S(1)} %collective-permute-done.34.refs_3_), channel_id=1, source_target_pairs={{0,4},{4,0},{8,12},{12,8},{16,20},{20,16},{24,28},{28,24},{1,5},{5... | collective-permute-start | bytes 786440 | tf_op jit(solution)/shard_map/ppermute | solution.py:701
  189.3 13.7 %collective-permute-start.28 = (bf16[256,512]{1,0:T(8,128)(2,1)S(1)}, bf16[256,512]{1,0:T(8,128)(2,1)S(1)}, u32[]{:S(2)}, u32[]{:S(2)}) collective-permute-start(bf16[256,512]{1,0:T(8,128)(2,1)S(1)} %collective-permute-done.25.refs_2_), channel_id=1, source_target_pairs={{0,4},{4,0},{8,12},{12,8},{16,20},{20,16},{24,28},{28,24},{1,5},{5... | collective-permute-start | bytes 786440 | tf_op jit(solution)/shard_map/ppermute | solution.py:701
  191.9 11.1 %collective-permute-start.27 = (bf16[256,512]{1,0:T(8,128)(2,1)S(1)}, bf16[256,512]{1,0:T(8,128)(2,1)S(1)}, u32[]{:S(2)}, u32[]{:S(2)}) collective-permute-start(bf16[256,512]{1,0:T(8,128)(2,1)S(1)} %collective-permute-done.24.refs_1_), channel_id=1, source_target_pairs={{0,8},{4,12},{8,0},{12,4},{16,24},{20,28},{24,16},{28,20},{1,9},{5... | collective-permute-start | bytes 786440 | tf_op jit(solution)/shard_map/ppermute | solution.py:701
  199.8 9.2 %collective-permute-start.29 = (bf16[256,512]{1,0:T(8,128)(2,1)S(1)}, bf16[256,512]{1,0:T(8,128)(2,1)S(1)}, u32[]{:S(2)}, u32[]{:S(2)}) collective-permute-start(bf16[256,512]{1,0:T(8,128)(2,1)S(1)} %collective-permute-done.24.refs_1_), channel_id=1, source_target_pairs={{0,4},{4,0},{8,12},{12,8},{16,20},{20,16},{24,28},{28,24},{1,5},{5... | collective-permute-start | bytes 786440 | tf_op jit(solution)/shard_map/ppermute | solution.py:701
  202.9 9.4 %collective-permute-start.30 = (bf16[256,512]{1,0:T(8,128)(2,1)S(1)}, bf16[256,512]{1,0:T(8,128)(2,1)S(1)}, u32[]{:S(2)}, u32[]{:S(2)}) collective-permute-start(bf16[256,512]{1,0:T(8,128)(2,1)S(1)} %collective-permute-done.27.refs_3_), channel_id=1, source_target_pairs={{0,4},{4,0},{8,12},{12,8},{16,20},{20,16},{24,28},{28,24},{1,5},{5... | collective-permute-start | bytes 786440 | tf_op jit(solution)/shard_map/ppermute | solution.py:701
  (19 other events, 144.0 us)

commit v6 on v5

--- a/solution.py
+++ b/solution.py
@@ -230,7 +230,7 @@
         return state, line
 
     zero = [jnp.zeros((8, LANE), F32) for _ in u]
-    state, line = lax.fori_loop(0, steps, body, (zero, zero), unroll=11)
+    state, line = lax.fori_loop(0, steps, body, (zero, zero), unroll=True)
     return state, [a * LN2 for a in line]
 
 
@@ -303,7 +303,7 @@
         return z, [p * (s * a) for p, s, a in zip(prod, sig, u)]
 
     ones = [] if store else [jnp.ones((8, LANE), F32) for _ in start]
-    return lax.fori_loop(0, steps, body, (start, ones), unroll=11)
+    return lax.fori_loop(0, steps, body, (start, ones), unroll=True)
 
 
 def solve_back(grad_ref, sigma_ref, decay_row, tiles):

time: 215 us -> 214 us (level)
  transfers between devices with their start and end apart: 38 -> 38, of which waited for: 16 -> 15; matrix products, arithmetic and copies ran while one was open for 1% -> 1% of each run, Pallas kernels for 10% -> 10%
where the time goes in v6:
time: 214 us; the launch traced here: 213 us
  waiting for transfers between devices  83.3 us (39%)
  blocking collectives  53.3 us (25%)
  Pallas kernels  38.4 us (18%)
  starting transfers between devices  30.8 us (14%)
  local copies, waits for them, and re-layouts  3.78 us (2%)
  other arithmetic  2.67 us (1%)
    ppermute x38, waiting for transfers between devices, swap(): return lax.ppermute(x, axis, [(i, i ^ bit) for i in range(n)])  83.3 us
    all_to_all x4, blocking collectives, share(): return lax.all_to_all(stats, 'seq', 0, 0, tiled=True)  53.3 us
    ppermute x38, starting transfers between devices, swap(): return lax.ppermute(x, axis, [(i, i ^ bit) for i in range(n)])  30.8 us
    pallas_call x3, Pallas kernels, weight_parts(): call(functools.partial(weight_kernel, True), [shape(4, half, half, dtype=...  7.55 us
    pallas_call x1, Pallas kernels, per_device(): call(turn_kernel, [shape(length, real, dtype=BF16), shape(length, width),...  6.94 us
    pallas_call x1, Pallas kernels, per_device(): call(forward_kernel, [shape(length, real, dtype=BF16), shape(length, widt...  5.08 us
    pallas_call x2, Pallas kernels, weights(): call(functools.partial(spread_kernel, True), shape(4 * real, real), [pltp...  4.93 us
  transfers between devices with their start and end apart: 38, of which 15 were waited for; matrix products, arithmetic and copies ran while one was open for 1% of the time, Pallas kernels for 10%

profile of v6, /device:TPU:0, one launch (start us, length us, event | category | flops | bytes accessed | tf_op | source)
XLA Modules:
  0.0 213.2 jit_solution(13293549336016097404)
XLA Ops:
  1.2 2.6 %collective-permute-start = (bf16[704,500]{1,0:T(8,128)(2,1)}, bf16[704,500]{1,0:T(8,128)(2,1)S(1)}, u32[]{:S(2)}, u32[]{:S(2)}) collective-permute-start(bf16[704,500]{1,0:T(8,128)(2,1)} %bitcast.13), channel_id=1, source_target_pairs={{0,2},{1,3},{2,0},{3,1},{4,6},{5,7},{6,4},{7,5},{8,10},{9,11},{10,... | collective-permute-start | bytes 2112008 | tf_op jit(solution)/shard_map/ppermute | solution.py:701
  3.7 1.6 copy-done.2
  8.8 11.9 %collective-permute-done.far_ref = bf16[704,500]{1,0:T(8,128)(2,1)S(1)} collective-permute-done((bf16[704,500]{1,0:T(8,128)(2,1)}, bf16[704,500]{1,0:T(8,128)(2,1)S(1)}, u32[]{:S(2)}, u32[]{:S(2)}) %collective-permute-start) | collective-permute-done | bytes 704032 | tf_op jit(solution)/shard_map/ppermute | solution.py:701
  21.3 1.6 collective-permute-done.2.cross_ref
  23.8 13.4 %all_to_all.20.stats_ref = f32[8,8,512]{2,1,0:T(8,128)S(1)} all-to-all(f32[8,8,512]{2,1,0:T(8,128)S(1)} %get-tuple-element.133), channel_id=1, replica_groups=mesh['seq'=8,'neur'=4] {'seq'}, dimensions={0} | all-to-all | bytes 262144 | tf_op jit(solution)/shard_map/all_to_all | solution.py:756
  37.1 5.1 %shard_map.199 = (bf16[704,500]{1,0:T(8,128)(2,1)}, f32[704,512]{1,0:T(8,128)S(1)}, f32[8,512]{1,0:T(8,128)S(1)}) custom-call(f32[8,8,512]{2,1,0:T(8,128)S(1)} %all_to_all.20.stats_ref, f32[704,512]{1,0:T(8,128)S(1)} %get-tuple-element.134.proj_ref, f32[8,512]{1,0:T(8,128)S(1)} %get-tuple-element.135.par_ref), custom_call_target="tpu_custom_call" | custom-call | tf_op jit(solution)/shard_map/pallas_call | solution.py:818
  45.0 2.5 %shard_map.203 = (bf16[4,256,256]{2,1,0:T(8,128)(2,1)S(1)}, bf16[4,256,256]{2,1,0:T(8,128)(2,1)S(1)}, bf16[4,256,256]{2,1,0:T(8,128)(2,1)S(1)}, bf16[4,256,256]{2,1,0:T(8,128)(2,1)S(1)}) custom-call(bf16[704,500]{1,0:T(8,128)(2,1)S(1)} %bitcast.15, bf16[704,500]{1,0:T(8,128)(2,1)S(1)} %collective-permute-done.1.mate_ref, ...), custom_call_target="tpu_custom_call" | custom-call | tf_op jit(solution)/shard_map/pallas_call | solution.py:797
  50.0 11.7 %collective-permute-done.3.far_ref = bf16[704,500]{1,0:T(8,128)(2,1)S(1)} collective-permute-done((bf16[704,500]{1,0:T(8,128)(2,1)S(1)}, bf16[704,500]{1,0:T(8,128)(2,1)S(1)}, u32[]{:S(2)}, u32[]{:S(2)}) %collective-permute-start.3) | collective-permute-done | bytes 704032 | tf_op jit(solution)/shard_map/ppermute | solution.py:701
  62.4 1.5 collective-permute-done.9.cross_ref
  64.8 10.0 %all_to_all.21.stats_ref = f32[8,8,512]{2,1,0:T(8,128)S(1)} all-to-all(f32[8,8,512]{2,1,0:T(8,128)S(1)} %get-tuple-element.158), channel_id=1, replica_groups=mesh['seq'=8,'neur'=4] {'seq'}, dimensions={0} | all-to-all | bytes 262144 | tf_op jit(solution)/shard_map/all_to_all | solution.py:756
  74.9 6.9 %shard_map.206 = (bf16[704,500]{1,0:T(8,128)(2,1)}, f32[704,512]{1,0:T(8,128)S(1)}, f32[8,8,512]{2,1,0:T(8,128)S(1)}, f32[8,512]{1,0:T(8,128)S(1)}, f32[2,500]{1,0:T(2,128)}, /*index=5*/f32[2,500]{1,0:T(2,128)}) custom-call(f32[8,8,512]{2,1,0:T(8,128)S(1)} %all_to_all.21.stats_ref, f32[704,512]{1,0:T(8,128)S(1)} %get-tuple-element.159.proj_ref, ...), custom_call_target="tpu_custom_call" | custom-call | tf_op jit(solution)/shard_map/pallas_call | solution.py:839
  81.8 9.8 %all_to_all.22.sums_ref = f32[8,8,512]{2,1,0:T(8,128)S(1)} all-to-all(f32[8,8,512]{2,1,0:T(8,128)S(1)} %get-tuple-element.162), channel_id=1, replica_groups=mesh['seq'=8,'neur'=4] {'seq'}, dimensions={0} | all-to-all | bytes 262144 | tf_op jit(solution)/shard_map/all_to_all | solution.py:756
  92.1 2.5 %shard_map.208 = (bf16[4,256,256]{2,1,0:T(8,128)(2,1)S(1)}, bf16[4,256,256]{2,1,0:T(8,128)(2,1)S(1)}, bf16[4,256,256]{2,1,0:T(8,128)(2,1)S(1)}, bf16[4,256,256]{2,1,0:T(8,128)(2,1)S(1)}) custom-call(bf16[704,500]{1,0:T(8,128)(2,1)S(1)} %copy-done.1, bf16[704,500]{1,0:T(8,128)(2,1)S(1)} %collective-permute-done.4.mate_ref, ...), custom_call_target="tpu_custom_call" | custom-call | tf_op jit(solution)/shard_map/pallas_call | solution.py:797
  99.3 11.8 %collective-permute-done.12.got_left_ref = bf16[4,256,256]{2,1,0:T(8,128)(2,1)S(1)} collective-permute-done((bf16[4,256,256]{2,1,0:T(8,128)(2,1)S(1)}, bf16[4,256,256]{2,1,0:T(8,128)(2,1)S(1)}, u32[]{:S(2)}, u32[]{:S(2)}) %collective-permute-start.12) | collective-permute-done | bytes 524320 | tf_op jit(solution)/shard_map/ppermute | solution.py:701
  114.1 2.1 shard_map.212
  116.3 2.5 %shard_map.214 = (bf16[4,256,256]{2,1,0:T(8,128)(2,1)S(1)}, bf16[4,256,256]{2,1,0:T(8,128)(2,1)S(1)}, bf16[4,256,256]{2,1,0:T(8,128)(2,1)S(1)}, bf16[4,256,256]{2,1,0:T(8,128)(2,1)S(1)}) custom-call(bf16[704,500]{1,0:T(8,128)(2,1)S(1)} %bitcast.16, bf16[704,500]{1,0:T(8,128)(2,1)S(1)} %collective-permute-done.1.mate_ref, ...), custom_call_target="tpu_custom_call" | custom-call | tf_op jit(solution)/shard_map/pallas_call | solution.py:797
  121.2 20.1 %all_to_all.23.sums_ref = f32[8,8,512]{2,1,0:T(8,128)S(1)} all-to-all(f32[8,8,512]{2,1,0:T(8,128)S(1)} %get-tuple-element.193), channel_id=1, replica_groups=mesh['seq'=8,'neur'=4] {'seq'}, dimensions={0} | all-to-all | bytes 262144 | tf_op jit(solution)/shard_map/all_to_all | solution.py:756
  143.8 1.5 collective-permute-start.32
  145.3 1.6 collective-permute-start.33
  147.7 9.8 %collective-permute-done.20.got_left_ref = bf16[2,256,256]{2,1,0:T(8,128)(2,1)S(1)} collective-permute-done((bf16[2,256,256]{2,1,0:T(8,128)(2,1)S(1)}, bf16[2,256,256]{2,1,0:T(8,128)(2,1)S(1)}, u32[]{:S(2)}, u32[]{:S(2)}) %collective-permute-start.20) | collective-permute-done | bytes 262176 | tf_op jit(solution)/shard_map/ppermute | solution.py:701
  157.7 5.1 %collective-permute-done.32.refs_2_ = bf16[256,512]{1,0:T(8,128)(2,1)S(1)} collective-permute-done((bf16[256,512]{1,0:T(8,128)(2,1)S(1)}, bf16[256,512]{1,0:T(8,128)(2,1)S(1)}, u32[]{:S(2)}, u32[]{:S(2)}) %collective-permute-start.32) | collective-permute-done | bytes 262176 | tf_op jit(solution)/shard_map/ppermute | solution.py:701
  164.9 1.5 collective-permute-start.23
  167.4 6.9 %collective-permute-done.22 = bf16[256,512]{1,0:T(8,128)(2,1)S(1)} collective-permute-done((bf16[256,512]{1,0:T(8,128)(2,1)S(1)}, bf16[256,512]{1,0:T(8,128)(2,1)S(1)}, u32[]{:S(2)}, u32[]{:S(2)}) %collective-permute-start.22) | collective-permute-done | bytes 262176 | tf_op jit(solution)/shard_map/ppermute | solution.py:701
  175.7 1.8 collective-permute-start.24
  178.9 7.4 %collective-permute-done.25.refs_2_ = bf16[256,512]{1,0:T(8,128)(2,1)S(1)} collective-permute-done((bf16[256,512]{1,0:T(8,128)(2,1)S(1)}, bf16[256,512]{1,0:T(8,128)(2,1)S(1)}, u32[]{:S(2)}, u32[]{:S(2)}) %collective-permute-start.25) | collective-permute-done | bytes 262176 | tf_op jit(solution)/shard_map/ppermute | solution.py:701
  188.4 1.8 collective-permute-done.24.refs_1_
  191.4 4.2 %collective-permute-done.37.refs_7_ = bf16[256,512]{1,0:T(8,128)(2,1)S(1)} collective-permute-done((bf16[256,512]{1,0:T(8,128)(2,1)S(1)}, bf16[256,512]{1,0:T(8,128)(2,1)S(1)}, u32[]{:S(2)}, u32[]{:S(2)}) %collective-permute-start.37) | collective-permute-done | bytes 262176 | tf_op jit(solution)/shard_map/ppermute | solution.py:701
  195.6 2.5 %shard_map.221 = f32[2000,500]{1,0:T(8,128)} custom-call(bf16[256,512]{1,0:T(8,128)(2,1)S(1)} %add_convert_fusion.refs_0_, bf16[256,512]{1,0:T(8,128)(2,1)S(1)} %collective-permute-done.31.refs_1_, bf16[256,512]{1,0:T(8,128)(2,1)S(1)} %collective-permute-done.32.refs_2_, bf16[256,512]{1,0:T(8,128)(2,1)S(1)} %collective-permute-done.34.refs_3_, ...), custom_call_target="tpu_custom_call" | custom-call | tf_op jit(solution)/shard_map/pallas_call | solution.py:806
  199.3 1.9 collective-permute-done.28.refs_6_
  203.8 3.5 %collective-permute-done.29.refs_5_ = bf16[256,512]{1,0:T(8,128)(2,1)S(1)} collective-permute-done((bf16[256,512]{1,0:T(8,128)(2,1)S(1)}, bf16[256,512]{1,0:T(8,128)(2,1)S(1)}, u32[]{:S(2)}, u32[]{:S(2)}) %collective-permute-start.29) | collective-permute-done | bytes 262176 | tf_op jit(solution)/shard_map/ppermute | solution.py:701
  207.3 3.4 %collective-permute-done.30.refs_7_ = bf16[256,512]{1,0:T(8,128)(2,1)S(1)} collective-permute-done((bf16[256,512]{1,0:T(8,128)(2,1)S(1)}, bf16[256,512]{1,0:T(8,128)(2,1)S(1)}, u32[]{:S(2)}, u32[]{:S(2)}) %collective-permute-start.30) | collective-permute-done | bytes 262176 | tf_op jit(solution)/shard_map/ppermute | solution.py:701
  210.7 2.5 %shard_map.220 = f32[2000,500]{1,0:T(8,128)} custom-call(bf16[256,512]{1,0:T(8,128)(2,1)S(1)} %add_convert_fusion.1.refs_0_, bf16[256,512]{1,0:T(8,128)(2,1)S(1)} %collective-permute-done.24.refs_1_, bf16[256,512]{1,0:T(8,128)(2,1)S(1)} %collective-permute-done.25.refs_2_, bf16[256,512]{1,0:T(8,128)(2,1)S(1)} %collective-permute-done.27.refs_3_, ...), custom_call_target="tpu_custom_call" | custom-call | tf_op jit(solution)/shard_map/pallas_call | solution.py:806
  (109 shorter events, 39.1 us)
Async XLA Ops:
  1.2 19.5 %collective-permute-start = (bf16[704,500]{1,0:T(8,128)(2,1)}, bf16[704,500]{1,0:T(8,128)(2,1)S(1)}, u32[]{:S(2)}, u32[]{:S(2)}) collective-permute-start(bf16[704,500]{1,0:T(8,128)(2,1)} %bitcast.13), channel_id=1, source_target_pairs={{0,2},{1,3},{2,0},{3,1},{4,6},{5,7},{6,4},{7,5},{8,10},{9,11},{10,... | collective-permute-start | bytes 2112008 | tf_op jit(solution)/shard_map/ppermute | solution.py:701
  42.6 19.1 %collective-permute-start.6 = (bf16[2,512,512]{2,1,0:T(8,128)(2,1)S(1)}, bf16[2,512,512]{2,1,0:T(8,128)(2,1)S(1)}, u32[]{:S(2)}, u32[]{:S(2)}) collective-permute-start(bf16[2,512,512]{2,1,0:T(8,128)(2,1)S(1)} %get-tuple-element.144), channel_id=1, source_target_pairs={{0,1},{1,0},{2,3},{3,2},{4,5},{5,4},{6,7},{7,6},{8,9},{9,8},{10,11... | collective-permute-start | bytes 3145736 | tf_op jit(solution)/shard_map/ppermute | solution.py:701
  43.1 18.6 %collective-permute-start.5 = (bf16[2,512,512]{2,1,0:T(8,128)(2,1)S(1)}, bf16[2,512,512]{2,1,0:T(8,128)(2,1)S(1)}, u32[]{:S(2)}, u32[]{:S(2)}) collective-permute-start(bf16[2,512,512]{2,1,0:T(8,128)(2,1)S(1)} %get-tuple-element.142), channel_id=1, source_target_pairs={{0,1},{1,0},{2,3},{3,2},{4,5},{5,4},{6,7},{7,6},{8,9},{9,8},{10,11... | collective-permute-start | bytes 3145736 | tf_op jit(solution)/shard_map/ppermute | solution.py:701
  43.3 18.4 %collective-permute-start.3 = (bf16[704,500]{1,0:T(8,128)(2,1)S(1)}, bf16[704,500]{1,0:T(8,128)(2,1)S(1)}, u32[]{:S(2)}, u32[]{:S(2)}) collective-permute-start(bf16[704,500]{1,0:T(8,128)(2,1)S(1)} %copy-done.1), channel_id=1, source_target_pairs={{0,2},{1,3},{2,0},{3,1},{4,6},{5,7},{6,4},{7,5},{8,10},{9,11},{10,... | collective-permute-start | bytes 2112008 | tf_op jit(solution)/shard_map/ppermute | solution.py:701
  47.5 14.2 %collective-permute-start.7 = (bf16[4,256,256]{2,1,0:T(8,128)(2,1)S(1)}, bf16[4,256,256]{2,1,0:T(8,128)(2,1)S(1)}, u32[]{:S(2)}, u32[]{:S(2)}) collective-permute-start(bf16[4,256,256]{2,1,0:T(8,128)(2,1)S(1)} %get-tuple-element.150), channel_id=1, source_target_pairs={{0,4},{4,0},{8,12},{12,8},{16,20},{20,16},{24,28},{28,24},{1,5},{5... | collective-permute-start | bytes 1572872 | tf_op jit(solution)/shard_map/ppermute | solution.py:701
  48.0 13.7 %collective-permute-start.8 = (bf16[4,256,256]{2,1,0:T(8,128)(2,1)S(1)}, bf16[4,256,256]{2,1,0:T(8,128)(2,1)S(1)}, u32[]{:S(2)}, u32[]{:S(2)}) collective-permute-start(bf16[4,256,256]{2,1,0:T(8,128)(2,1)S(1)} %get-tuple-element.152), channel_id=1, source_target_pairs={{0,8},{4,12},{8,0},{12,4},{16,24},{20,28},{24,16},{28,20},{1,9},{5... | collective-permute-start | bytes 1572872 | tf_op jit(solution)/shard_map/ppermute | solution.py:701
  95.5 18.6 %collective-permute-start.11 = (bf16[704,512]{1,0:T(8,128)(2,1)S(1)}, bf16[704,512]{1,0:T(8,128)(2,1)S(1)}, u32[]{:S(2)}, u32[]{:S(2)}) collective-permute-start(bf16[704,512]{1,0:T(8,128)(2,1)S(1)} %shard_map.209), channel_id=1, source_target_pairs={{0,2},{1,3},{2,0},{3,1},{4,6},{5,7},{6,4},{7,5},{8,10},{9,11},{10,... | collective-permute-start | bytes 2162696 | tf_op jit(solution)/shard_map/ppermute | solution.py:701
  97.1 14.0 %collective-permute-start.12 = (bf16[4,256,256]{2,1,0:T(8,128)(2,1)S(1)}, bf16[4,256,256]{2,1,0:T(8,128)(2,1)S(1)}, u32[]{:S(2)}, u32[]{:S(2)}) collective-permute-start(bf16[4,256,256]{2,1,0:T(8,128)(2,1)S(1)} %get-tuple-element.177), channel_id=1, source_target_pairs={{0,4},{4,0},{8,12},{12,8},{16,20},{20,16},{24,28},{28,24},{1,5},{5... | collective-permute-start | bytes 1572872 | tf_op jit(solution)/shard_map/ppermute | solution.py:701
  97.3 13.8 %collective-permute-start.13 = (bf16[4,256,256]{2,1,0:T(8,128)(2,1)S(1)}, bf16[4,256,256]{2,1,0:T(8,128)(2,1)S(1)}, u32[]{:S(2)}, u32[]{:S(2)}) collective-permute-start(bf16[4,256,256]{2,1,0:T(8,128)(2,1)S(1)} %get-tuple-element.178), channel_id=1, source_target_pairs={{0,8},{4,12},{8,0},{12,4},{16,24},{20,28},{24,16},{28,20},{1,9},{5... | collective-permute-start | bytes 1572872 | tf_op jit(solution)/shard_map/ppermute | solution.py:701
  111.3 8.8 %collective-permute-start.14 = (bf16[2,256,256]{2,1,0:T(8,128)(2,1)S(1)}, bf16[2,256,256]{2,1,0:T(8,128)(2,1)S(1)}, u32[]{:S(2)}, u32[]{:S(2)}) collective-permute-start(bf16[2,256,256]{2,1,0:T(8,128)(2,1)S(1)} %get-tuple-element.188), channel_id=1, source_target_pairs={{0,8},{4,12},{8,0},{12,4},{16,24},{20,28},{24,16},{28,20},{1,9},{5... | collective-permute-start | bytes 786440 | tf_op jit(solution)/shard_map/ppermute | solution.py:701
  112.4 7.8 %collective-permute-start.15 = (bf16[2,256,256]{2,1,0:T(8,128)(2,1)S(1)}, bf16[2,256,256]{2,1,0:T(8,128)(2,1)S(1)}, u32[]{:S(2)}, u32[]{:S(2)}) collective-permute-start(bf16[2,256,256]{2,1,0:T(8,128)(2,1)S(1)} %get-tuple-element.190), channel_id=1, source_target_pairs={{0,4},{4,0},{8,12},{12,8},{16,20},{20,16},{24,28},{28,24},{1,5},{5... | collective-permute-start | bytes 786440 | tf_op jit(solution)/shard_map/ppermute | solution.py:701
  118.8 22.5 %collective-permute-start.17 = (bf16[4,256,256]{2,1,0:T(8,128)(2,1)S(1)}, bf16[4,256,256]{2,1,0:T(8,128)(2,1)S(1)}, u32[]{:S(2)}, u32[]{:S(2)}) collective-permute-start(bf16[4,256,256]{2,1,0:T(8,128)(2,1)S(1)} %get-tuple-element.196), channel_id=1, source_target_pairs={{0,4},{4,0},{8,12},{12,8},{16,20},{20,16},{24,28},{28,24},{1,5},{5... | collective-permute-start | bytes 1572872 | tf_op jit(solution)/shard_map/ppermute | solution.py:701
  119.2 22.2 %collective-permute-start.18 = (bf16[4,256,256]{2,1,0:T(8,128)(2,1)S(1)}, bf16[4,256,256]{2,1,0:T(8,128)(2,1)S(1)}, u32[]{:S(2)}, u32[]{:S(2)}) collective-permute-start(bf16[4,256,256]{2,1,0:T(8,128)(2,1)S(1)} %get-tuple-element.197), channel_id=1, source_target_pairs={{0,8},{4,12},{8,0},{12,4},{16,24},{20,28},{24,16},{28,20},{1,9},{5... | collective-permute-start | bytes 1572872 | tf_op jit(solution)/shard_map/ppermute | solution.py:701
  120.3 21.0 %collective-permute-start.16 = (bf16[256,512]{1,0:T(8,128)(2,1)S(1)}, bf16[256,512]{1,0:T(8,128)(2,1)S(1)}, u32[]{:S(2)}, u32[]{:S(2)}) collective-permute-start(bf16[256,512]{1,0:T(8,128)(2,1)S(1)} %get-tuple-element.194), channel_id=1, source_target_pairs={{0,16},{4,20},{8,24},{12,28},{16,0},{20,4},{24,8},{28,12},{1,17},{... | collective-permute-start | bytes 786440 | tf_op jit(solution)/shard_map/ppermute | solution.py:701
  142.7 14.8 %collective-permute-start.20 = (bf16[2,256,256]{2,1,0:T(8,128)(2,1)S(1)}, bf16[2,256,256]{2,1,0:T(8,128)(2,1)S(1)}, u32[]{:S(2)}, u32[]{:S(2)}) collective-permute-start(bf16[2,256,256]{2,1,0:T(8,128)(2,1)S(1)} %get-tuple-element.215), channel_id=1, source_target_pairs={{0,8},{4,12},{8,0},{12,4},{16,24},{20,28},{24,16},{28,20},{1,9},{5... | collective-permute-start | bytes 786440 | tf_op jit(solution)/shard_map/ppermute | solution.py:701
  142.9 14.6 %collective-permute-start.21 = (bf16[2,256,256]{2,1,0:T(8,128)(2,1)S(1)}, bf16[2,256,256]{2,1,0:T(8,128)(2,1)S(1)}, u32[]{:S(2)}, u32[]{:S(2)}) collective-permute-start(bf16[2,256,256]{2,1,0:T(8,128)(2,1)S(1)} %get-tuple-element.217), channel_id=1, source_target_pairs={{0,4},{4,0},{8,12},{12,8},{16,20},{20,16},{24,28},{28,24},{1,5},{5... | collective-permute-start | bytes 786440 | tf_op jit(solution)/shard_map/ppermute | solution.py:701
  143.8 19.0 %collective-permute-start.32 = (bf16[256,512]{1,0:T(8,128)(2,1)S(1)}, bf16[256,512]{1,0:T(8,128)(2,1)S(1)}, u32[]{:S(2)}, u32[]{:S(2)}) collective-permute-start(bf16[256,512]{1,0:T(8,128)(2,1)S(1)} %add_convert_fusion.refs_0_), channel_id=1, source_target_pairs={{0,8},{4,12},{8,0},{12,4},{16,24},{20,28},{24,16},{28,20},{1,9},{5... | collective-permute-start | bytes 786440 | tf_op jit(solution)/shard_map/ppermute | solution.py:701
  145.3 17.5 %collective-permute-start.33 = (bf16[256,512]{1,0:T(8,128)(2,1)S(1)}, bf16[256,512]{1,0:T(8,128)(2,1)S(1)}, u32[]{:S(2)}, u32[]{:S(2)}) collective-permute-start(bf16[256,512]{1,0:T(8,128)(2,1)S(1)} %add_convert_fusion.refs_0_), channel_id=1, source_target_pairs={{0,4},{4,0},{8,12},{12,8},{16,20},{20,16},{24,28},{28,24},{1,5},{5... | collective-permute-start | bytes 786440 | tf_op jit(solution)/shard_map/ppermute | solution.py:701
  147.0 16.2 %collective-permute-start.31 = (bf16[256,512]{1,0:T(8,128)(2,1)S(1)}, bf16[256,512]{1,0:T(8,128)(2,1)S(1)}, u32[]{:S(2)}, u32[]{:S(2)}) collective-permute-start(bf16[256,512]{1,0:T(8,128)(2,1)S(1)} %add_convert_fusion.refs_0_), channel_id=1, source_target_pairs={{0,16},{4,20},{8,24},{12,28},{16,0},{20,4},{24,8},{28,12},{1,17},{... | collective-permute-start | bytes 786440 | tf_op jit(solution)/shard_map/ppermute | solution.py:701
  157.6 16.6 %collective-permute-start.22 = (bf16[256,512]{1,0:T(8,128)(2,1)S(1)}, bf16[256,512]{1,0:T(8,128)(2,1)S(1)}, u32[]{:S(2)}, u32[]{:S(2)}) collective-permute-start(bf16[256,512]{1,0:T(8,128)(2,1)S(1)} %get-tuple-element.219), channel_id=1, source_target_pairs={{0,16},{4,20},{8,24},{12,28},{16,0},{20,4},{24,8},{28,12},{1,17},{... | collective-permute-start | bytes 786440 | tf_op jit(solution)/shard_map/ppermute | solution.py:701
  162.8 12.9 %collective-permute-start.35 = (bf16[256,512]{1,0:T(8,128)(2,1)S(1)}, bf16[256,512]{1,0:T(8,128)(2,1)S(1)}, u32[]{:S(2)}, u32[]{:S(2)}) collective-permute-start(bf16[256,512]{1,0:T(8,128)(2,1)S(1)} %collective-permute-done.32.refs_2_), channel_id=1, source_target_pairs={{0,4},{4,0},{8,12},{12,8},{16,20},{20,16},{24,28},{28,24},{1,5},{5... | collective-permute-start | bytes 786440 | tf_op jit(solution)/shard_map/ppermute | solution.py:701
  163.2 14.3 %collective-permute-start.34 = (bf16[256,512]{1,0:T(8,128)(2,1)S(1)}, bf16[256,512]{1,0:T(8,128)(2,1)S(1)}, u32[]{:S(2)}, u32[]{:S(2)}) collective-permute-start(bf16[256,512]{1,0:T(8,128)(2,1)S(1)} %collective-permute-done.31.refs_1_), channel_id=1, source_target_pairs={{0,8},{4,12},{8,0},{12,4},{16,24},{20,28},{24,16},{28,20},{1,9},{5... | collective-permute-start | bytes 786440 | tf_op jit(solution)/shard_map/ppermute | solution.py:701
  164.9 37.6 %collective-permute-start.23 = (bf16[704,512]{1,0:T(8,128)(2,1)S(1)}, bf16[704,512]{1,0:T(8,128)(2,1)S(1)}, u32[]{:S(2)}, u32[]{:S(2)}) collective-permute-start(bf16[704,512]{1,0:T(8,128)(2,1)S(1)} %shard_map.217), channel_id=1, source_target_pairs={{0,2},{1,3},{2,0},{3,1},{4,6},{5,7},{6,4},{7,5},{8,10},{9,11},{10,... | collective-permute-start | bytes 2162696 | tf_op jit(solution)/shard_map/ppermute | solution.py:701
  174.3 12.1 %collective-permute-start.25 = (bf16[256,512]{1,0:T(8,128)(2,1)S(1)}, bf16[256,512]{1,0:T(8,128)(2,1)S(1)}, u32[]{:S(2)}, u32[]{:S(2)}) collective-permute-start(bf16[256,512]{1,0:T(8,128)(2,1)S(1)} %add_convert_fusion.1.refs_0_), channel_id=1, source_target_pairs={{0,8},{4,12},{8,0},{12,4},{16,24},{20,28},{24,16},{28,20},{1,9},{5... | collective-permute-start | bytes 786440 | tf_op jit(solution)/shard_map/ppermute | solution.py:701
  174.4 13.2 %collective-permute-start.26 = (bf16[256,512]{1,0:T(8,128)(2,1)S(1)}, bf16[256,512]{1,0:T(8,128)(2,1)S(1)}, u32[]{:S(2)}, u32[]{:S(2)}) collective-permute-start(bf16[256,512]{1,0:T(8,128)(2,1)S(1)} %add_convert_fusion.1.refs_0_), channel_id=1, source_target_pairs={{0,4},{4,0},{8,12},{12,8},{16,20},{20,16},{24,28},{28,24},{1,5},{5... | collective-permute-start | bytes 786440 | tf_op jit(solution)/shard_map/ppermute | solution.py:701
  175.7 14.4 %collective-permute-start.24 = (bf16[256,512]{1,0:T(8,128)(2,1)S(1)}, bf16[256,512]{1,0:T(8,128)(2,1)S(1)}, u32[]{:S(2)}, u32[]{:S(2)}) collective-permute-start(bf16[256,512]{1,0:T(8,128)(2,1)S(1)} %add_convert_fusion.1.refs_0_), channel_id=1, source_target_pairs={{0,16},{4,20},{8,24},{12,28},{16,0},{20,4},{24,8},{28,12},{1,17},{... | collective-permute-start | bytes 786440 | tf_op jit(solution)/shard_map/ppermute | solution.py:701
  177.5 13.9 %collective-permute-start.36 = (bf16[256,512]{1,0:T(8,128)(2,1)S(1)}, bf16[256,512]{1,0:T(8,128)(2,1)S(1)}, u32[]{:S(2)}, u32[]{:S(2)}) collective-permute-start(bf16[256,512]{1,0:T(8,128)(2,1)S(1)} %collective-permute-done.31.refs_1_), channel_id=1, source_target_pairs={{0,4},{4,0},{8,12},{12,8},{16,20},{20,16},{24,28},{28,24},{1,5},{5... | collective-permute-start | bytes 786440 | tf_op jit(solution)/shard_map/ppermute | solution.py:701
  186.4 9.2 %collective-permute-start.37 = (bf16[256,512]{1,0:T(8,128)(2,1)S(1)}, bf16[256,512]{1,0:T(8,128)(2,1)S(1)}, u32[]{:S(2)}, u32[]{:S(2)}) collective-permute-start(bf16[256,512]{1,0:T(8,128)(2,1)S(1)} %collective-permute-done.34.refs_3_), channel_id=1, source_target_pairs={{0,4},{4,0},{8,12},{12,8},{16,20},{20,16},{24,28},{28,24},{1,5},{5... | collective-permute-start | bytes 786440 | tf_op jit(solution)/shard_map/ppermute | solution.py:701
  187.6 13.6 %collective-permute-start.28 = (bf16[256,512]{1,0:T(8,128)(2,1)S(1)}, bf16[256,512]{1,0:T(8,128)(2,1)S(1)}, u32[]{:S(2)}, u32[]{:S(2)}) collective-permute-start(bf16[256,512]{1,0:T(8,128)(2,1)S(1)} %collective-permute-done.25.refs_2_), channel_id=1, source_target_pairs={{0,4},{4,0},{8,12},{12,8},{16,20},{20,16},{24,28},{28,24},{1,5},{5... | collective-permute-start | bytes 786440 | tf_op jit(solution)/shard_map/ppermute | solution.py:701
  190.2 11.1 %collective-permute-start.27 = (bf16[256,512]{1,0:T(8,128)(2,1)S(1)}, bf16[256,512]{1,0:T(8,128)(2,1)S(1)}, u32[]{:S(2)}, u32[]{:S(2)}) collective-permute-start(bf16[256,512]{1,0:T(8,128)(2,1)S(1)} %collective-permute-done.24.refs_1_), channel_id=1, source_target_pairs={{0,8},{4,12},{8,0},{12,4},{16,24},{20,28},{24,16},{28,20},{1,9},{5... | collective-permute-start | bytes 786440 | tf_op jit(solution)/shard_map/ppermute | solution.py:701
  198.1 9.2 %collective-permute-start.29 = (bf16[256,512]{1,0:T(8,128)(2,1)S(1)}, bf16[256,512]{1,0:T(8,128)(2,1)S(1)}, u32[]{:S(2)}, u32[]{:S(2)}) collective-permute-start(bf16[256,512]{1,0:T(8,128)(2,1)S(1)} %collective-permute-done.24.refs_1_), channel_id=1, source_target_pairs={{0,4},{4,0},{8,12},{12,8},{16,20},{20,16},{24,28},{28,24},{1,5},{5... | collective-permute-start | bytes 786440 | tf_op jit(solution)/shard_map/ppermute | solution.py:701
  201.2 9.4 %collective-permute-start.30 = (bf16[256,512]{1,0:T(8,128)(2,1)S(1)}, bf16[256,512]{1,0:T(8,128)(2,1)S(1)}, u32[]{:S(2)}, u32[]{:S(2)}) collective-permute-start(bf16[256,512]{1,0:T(8,128)(2,1)S(1)} %collective-permute-done.27.refs_3_), channel_id=1, source_target_pairs={{0,4},{4,0},{8,12},{12,8},{16,20},{20,16},{24,28},{28,24},{1,5},{5... | collective-permute-start | bytes 786440 | tf_op jit(solution)/shard_map/ppermute | solution.py:701
  (19 other events, 141.2 us)

commit v7 on v6

--- a/solution.py
+++ b/solution.py
@@ -346,7 +346,7 @@
             drive_ref[j, rows, :] = 1.0 / (1.0 + jnp.exp2(-before))
         return 0
 
-    lax.fori_loop(0, length // BLOCK, body, 0)
+    lax.fori_loop(0, length // BLOCK, body, 0, unroll=2)
 
 
 def finish_back(grad_ref, state_ref, proj_ref, mean, inverse, tiles, gb_ref, sums_ref):
@@ -367,7 +367,7 @@
             )
         return tuple(shift), tuple(gain), tuple(decay)
 
-    shift, gain, decay = lax.fori_loop(0, length // BLOCK, body, (zero, zero, zero))
+    shift, gain, decay = lax.fori_loop(0, length // BLOCK, body, (zero, zero, zero), unroll=2)
     for j, c, _ in tiles:
         at = slice(c, c + LANE)
         scaled = gain[j] * inverse[:, at]

time: 214 us -> 214 us (level)
  no operation moved by 1% of the time
where the time goes in v7:
time: 214 us; the launch traced here: 213 us
  waiting for transfers between devices  83.3 us (39%)
  blocking collectives  53.3 us (25%)
  Pallas kernels  38.2 us (18%)
  starting transfers between devices  30.8 us (14%)
  local copies, waits for them, and re-layouts  3.78 us (2%)
  other arithmetic  2.67 us (1%)
    ppermute x38, waiting for transfers between devices, swap(): return lax.ppermute(x, axis, [(i, i ^ bit) for i in range(n)])  83.3 us
    all_to_all x4, blocking collectives, share(): return lax.all_to_all(stats, 'seq', 0, 0, tiled=True)  53.3 us
    ppermute x38, starting transfers between devices, swap(): return lax.ppermute(x, axis, [(i, i ^ bit) for i in range(n)])  30.8 us
    pallas_call x3, Pallas kernels, weight_parts(): call(functools.partial(weight_kernel, True), [shape(4, half, half, dtype=...  7.55 us
    pallas_call x1, Pallas kernels, per_device(): call(turn_kernel, [shape(length, real, dtype=BF16), shape(length, width),...  6.87 us
    pallas_call x1, Pallas kernels, per_device(): call(forward_kernel, [shape(length, real, dtype=BF16), shape(length, widt...  5.08 us
    pallas_call x2, Pallas kernels, weights(): call(functools.partial(spread_kernel, True), shape(4 * real, real), [pltp...  4.93 us
  transfers between devices with their start and end apart: 38, of which 15 were waited for; matrix products, arithmetic and copies ran while one was open for 1% of the time, Pallas kernels for 10%

profile of v7, /device:TPU:0, one launch (start us, length us, event | category | flops | bytes accessed | tf_op | source)
XLA Modules:
  0.0 213.0 jit_solution(7814389223018427195)
XLA Ops:
  1.2 2.6 %collective-permute-start = (bf16[704,500]{1,0:T(8,128)(2,1)}, bf16[704,500]{1,0:T(8,128)(2,1)S(1)}, u32[]{:S(2)}, u32[]{:S(2)}) collective-permute-start(bf16[704,500]{1,0:T(8,128)(2,1)} %bitcast.13), channel_id=1, source_target_pairs={{0,2},{1,3},{2,0},{3,1},{4,6},{5,7},{6,4},{7,5},{8,10},{9,11},{10,... | collective-permute-start | bytes 2112008 | tf_op jit(solution)/shard_map/ppermute | solution.py:701
  3.7 1.6 copy-done.2
  8.8 11.9 %collective-permute-done.far_ref = bf16[704,500]{1,0:T(8,128)(2,1)S(1)} collective-permute-done((bf16[704,500]{1,0:T(8,128)(2,1)}, bf16[704,500]{1,0:T(8,128)(2,1)S(1)}, u32[]{:S(2)}, u32[]{:S(2)}) %collective-permute-start) | collective-permute-done | bytes 704032 | tf_op jit(solution)/shard_map/ppermute | solution.py:701
  21.3 1.6 collective-permute-done.2.cross_ref
  23.8 13.4 %all_to_all.20.stats_ref = f32[8,8,512]{2,1,0:T(8,128)S(1)} all-to-all(f32[8,8,512]{2,1,0:T(8,128)S(1)} %get-tuple-element.133), channel_id=1, replica_groups=mesh['seq'=8,'neur'=4] {'seq'}, dimensions={0} | all-to-all | bytes 262144 | tf_op jit(solution)/shard_map/all_to_all | solution.py:756
  37.1 5.1 %shard_map.199 = (bf16[704,500]{1,0:T(8,128)(2,1)}, f32[704,512]{1,0:T(8,128)S(1)}, f32[8,512]{1,0:T(8,128)S(1)}) custom-call(f32[8,8,512]{2,1,0:T(8,128)S(1)} %all_to_all.20.stats_ref, f32[704,512]{1,0:T(8,128)S(1)} %get-tuple-element.134.proj_ref, f32[8,512]{1,0:T(8,128)S(1)} %get-tuple-element.135.par_ref), custom_call_target="tpu_custom_call" | custom-call | tf_op jit(solution)/shard_map/pallas_call | solution.py:818
  45.0 2.5 %shard_map.203 = (bf16[4,256,256]{2,1,0:T(8,128)(2,1)S(1)}, bf16[4,256,256]{2,1,0:T(8,128)(2,1)S(1)}, bf16[4,256,256]{2,1,0:T(8,128)(2,1)S(1)}, bf16[4,256,256]{2,1,0:T(8,128)(2,1)S(1)}) custom-call(bf16[704,500]{1,0:T(8,128)(2,1)S(1)} %bitcast.15, bf16[704,500]{1,0:T(8,128)(2,1)S(1)} %collective-permute-done.1.mate_ref, ...), custom_call_target="tpu_custom_call" | custom-call | tf_op jit(solution)/shard_map/pallas_call | solution.py:797
  50.0 11.7 %collective-permute-done.3.far_ref = bf16[704,500]{1,0:T(8,128)(2,1)S(1)} collective-permute-done((bf16[704,500]{1,0:T(8,128)(2,1)S(1)}, bf16[704,500]{1,0:T(8,128)(2,1)S(1)}, u32[]{:S(2)}, u32[]{:S(2)}) %collective-permute-start.3) | collective-permute-done | bytes 704032 | tf_op jit(solution)/shard_map/ppermute | solution.py:701
  62.4 1.5 collective-permute-done.9.cross_ref
  64.8 10.0 %all_to_all.21.stats_ref = f32[8,8,512]{2,1,0:T(8,128)S(1)} all-to-all(f32[8,8,512]{2,1,0:T(8,128)S(1)} %get-tuple-element.158), channel_id=1, replica_groups=mesh['seq'=8,'neur'=4] {'seq'}, dimensions={0} | all-to-all | bytes 262144 | tf_op jit(solution)/shard_map/all_to_all | solution.py:756
  74.9 6.9 %shard_map.206 = (bf16[704,500]{1,0:T(8,128)(2,1)}, f32[704,512]{1,0:T(8,128)S(1)}, f32[8,8,512]{2,1,0:T(8,128)S(1)}, f32[8,512]{1,0:T(8,128)S(1)}, f32[2,500]{1,0:T(2,128)}, /*index=5*/f32[2,500]{1,0:T(2,128)}) custom-call(f32[8,8,512]{2,1,0:T(8,128)S(1)} %all_to_all.21.stats_ref, f32[704,512]{1,0:T(8,128)S(1)} %get-tuple-element.159.proj_ref, ...), custom_call_target="tpu_custom_call" | custom-call | tf_op jit(solution)/shard_map/pallas_call | solution.py:839
  81.7 9.8 %all_to_all.22.sums_ref = f32[8,8,512]{2,1,0:T(8,128)S(1)} all-to-all(f32[8,8,512]{2,1,0:T(8,128)S(1)} %get-tuple-element.162), channel_id=1, replica_groups=mesh['seq'=8,'neur'=4] {'seq'}, dimensions={0} | all-to-all | bytes 262144 | tf_op jit(solution)/shard_map/all_to_all | solution.py:756
  92.0 2.5 %shard_map.208 = (bf16[4,256,256]{2,1,0:T(8,128)(2,1)S(1)}, bf16[4,256,256]{2,1,0:T(8,128)(2,1)S(1)}, bf16[4,256,256]{2,1,0:T(8,128)(2,1)S(1)}, bf16[4,256,256]{2,1,0:T(8,128)(2,1)S(1)}) custom-call(bf16[704,500]{1,0:T(8,128)(2,1)S(1)} %copy-done.1, bf16[704,500]{1,0:T(8,128)(2,1)S(1)} %collective-permute-done.4.mate_ref, ...), custom_call_target="tpu_custom_call" | custom-call | tf_op jit(solution)/shard_map/pallas_call | solution.py:797
  99.2 11.8 %collective-permute-done.12.got_left_ref = bf16[4,256,256]{2,1,0:T(8,128)(2,1)S(1)} collective-permute-done((bf16[4,256,256]{2,1,0:T(8,128)(2,1)S(1)}, bf16[4,256,256]{2,1,0:T(8,128)(2,1)S(1)}, u32[]{:S(2)}, u32[]{:S(2)}) %collective-permute-start.12) | collective-permute-done | bytes 524320 | tf_op jit(solution)/shard_map/ppermute | solution.py:701
  114.1 2.0 shard_map.212
  116.1 2.5 %shard_map.214 = (bf16[4,256,256]{2,1,0:T(8,128)(2,1)S(1)}, bf16[4,256,256]{2,1,0:T(8,128)(2,1)S(1)}, bf16[4,256,256]{2,1,0:T(8,128)(2,1)S(1)}, bf16[4,256,256]{2,1,0:T(8,128)(2,1)S(1)}) custom-call(bf16[704,500]{1,0:T(8,128)(2,1)S(1)} %bitcast.16, bf16[704,500]{1,0:T(8,128)(2,1)S(1)} %collective-permute-done.1.mate_ref, ...), custom_call_target="tpu_custom_call" | custom-call | tf_op jit(solution)/shard_map/pallas_call | solution.py:797
  121.1 20.1 %all_to_all.23.sums_ref = f32[8,8,512]{2,1,0:T(8,128)S(1)} all-to-all(f32[8,8,512]{2,1,0:T(8,128)S(1)} %get-tuple-element.193), channel_id=1, replica_groups=mesh['seq'=8,'neur'=4] {'seq'}, dimensions={0} | all-to-all | bytes 262144 | tf_op jit(solution)/shard_map/all_to_all | solution.py:756
  143.7 1.5 collective-permute-start.32
  145.2 1.6 collective-permute-start.33
  147.6 9.8 %collective-permute-done.20.got_left_ref = bf16[2,256,256]{2,1,0:T(8,128)(2,1)S(1)} collective-permute-done((bf16[2,256,256]{2,1,0:T(8,128)(2,1)S(1)}, bf16[2,256,256]{2,1,0:T(8,128)(2,1)S(1)}, u32[]{:S(2)}, u32[]{:S(2)}) %collective-permute-start.20) | collective-permute-done | bytes 262176 | tf_op jit(solution)/shard_map/ppermute | solution.py:701
  157.5 5.1 %collective-permute-done.32.refs_2_ = bf16[256,512]{1,0:T(8,128)(2,1)S(1)} collective-permute-done((bf16[256,512]{1,0:T(8,128)(2,1)S(1)}, bf16[256,512]{1,0:T(8,128)(2,1)S(1)}, u32[]{:S(2)}, u32[]{:S(2)}) %collective-permute-start.32) | collective-permute-done | bytes 262176 | tf_op jit(solution)/shard_map/ppermute | solution.py:701
  164.8 1.5 collective-permute-start.23
  167.2 6.9 %collective-permute-done.22 = bf16[256,512]{1,0:T(8,128)(2,1)S(1)} collective-permute-done((bf16[256,512]{1,0:T(8,128)(2,1)S(1)}, bf16[256,512]{1,0:T(8,128)(2,1)S(1)}, u32[]{:S(2)}, u32[]{:S(2)}) %collective-permute-start.22) | collective-permute-done | bytes 262176 | tf_op jit(solution)/shard_map/ppermute | solution.py:701
  175.6 1.8 collective-permute-start.24
  178.8 7.4 %collective-permute-done.25.refs_2_ = bf16[256,512]{1,0:T(8,128)(2,1)S(1)} collective-permute-done((bf16[256,512]{1,0:T(8,128)(2,1)S(1)}, bf16[256,512]{1,0:T(8,128)(2,1)S(1)}, u32[]{:S(2)}, u32[]{:S(2)}) %collective-permute-start.25) | collective-permute-done | bytes 262176 | tf_op jit(solution)/shard_map/ppermute | solution.py:701
  188.3 1.8 collective-permute-done.24.refs_1_
  191.3 4.2 %collective-permute-done.37.refs_7_ = bf16[256,512]{1,0:T(8,128)(2,1)S(1)} collective-permute-done((bf16[256,512]{1,0:T(8,128)(2,1)S(1)}, bf16[256,512]{1,0:T(8,128)(2,1)S(1)}, u32[]{:S(2)}, u32[]{:S(2)}) %collective-permute-start.37) | collective-permute-done | bytes 262176 | tf_op jit(solution)/shard_map/ppermute | solution.py:701
  195.5 2.5 %shard_map.221 = f32[2000,500]{1,0:T(8,128)} custom-call(bf16[256,512]{1,0:T(8,128)(2,1)S(1)} %add_convert_fusion.refs_0_, bf16[256,512]{1,0:T(8,128)(2,1)S(1)} %collective-permute-done.31.refs_1_, bf16[256,512]{1,0:T(8,128)(2,1)S(1)} %collective-permute-done.32.refs_2_, bf16[256,512]{1,0:T(8,128)(2,1)S(1)} %collective-permute-done.34.refs_3_, ...), custom_call_target="tpu_custom_call" | custom-call | tf_op jit(solution)/shard_map/pallas_call | solution.py:806
  199.2 1.9 collective-permute-done.28.refs_6_
  203.7 3.5 %collective-permute-done.29.refs_5_ = bf16[256,512]{1,0:T(8,128)(2,1)S(1)} collective-permute-done((bf16[256,512]{1,0:T(8,128)(2,1)S(1)}, bf16[256,512]{1,0:T(8,128)(2,1)S(1)}, u32[]{:S(2)}, u32[]{:S(2)}) %collective-permute-start.29) | collective-permute-done | bytes 262176 | tf_op jit(solution)/shard_map/ppermute | solution.py:701
  207.2 3.4 %collective-permute-done.30.refs_7_ = bf16[256,512]{1,0:T(8,128)(2,1)S(1)} collective-permute-done((bf16[256,512]{1,0:T(8,128)(2,1)S(1)}, bf16[256,512]{1,0:T(8,128)(2,1)S(1)}, u32[]{:S(2)}, u32[]{:S(2)}) %collective-permute-start.30) | collective-permute-done | bytes 262176 | tf_op jit(solution)/shard_map/ppermute | solution.py:701
  210.6 2.5 %shard_map.220 = f32[2000,500]{1,0:T(8,128)} custom-call(bf16[256,512]{1,0:T(8,128)(2,1)S(1)} %add_convert_fusion.1.refs_0_, bf16[256,512]{1,0:T(8,128)(2,1)S(1)} %collective-permute-done.24.refs_1_, bf16[256,512]{1,0:T(8,128)(2,1)S(1)} %collective-permute-done.25.refs_2_, bf16[256,512]{1,0:T(8,128)(2,1)S(1)} %collective-permute-done.27.refs_3_, ...), custom_call_target="tpu_custom_call" | custom-call | tf_op jit(solution)/shard_map/pallas_call | solution.py:806
  (109 shorter events, 39.2 us)
Async XLA Ops:
  1.2 19.5 %collective-permute-start = (bf16[704,500]{1,0:T(8,128)(2,1)}, bf16[704,500]{1,0:T(8,128)(2,1)S(1)}, u32[]{:S(2)}, u32[]{:S(2)}) collective-permute-start(bf16[704,500]{1,0:T(8,128)(2,1)} %bitcast.13), channel_id=1, source_target_pairs={{0,2},{1,3},{2,0},{3,1},{4,6},{5,7},{6,4},{7,5},{8,10},{9,11},{10,... | collective-permute-start | bytes 2112008 | tf_op jit(solution)/shard_map/ppermute | solution.py:701
  42.6 19.1 %collective-permute-start.6 = (bf16[2,512,512]{2,1,0:T(8,128)(2,1)S(1)}, bf16[2,512,512]{2,1,0:T(8,128)(2,1)S(1)}, u32[]{:S(2)}, u32[]{:S(2)}) collective-permute-start(bf16[2,512,512]{2,1,0:T(8,128)(2,1)S(1)} %get-tuple-element.144), channel_id=1, source_target_pairs={{0,1},{1,0},{2,3},{3,2},{4,5},{5,4},{6,7},{7,6},{8,9},{9,8},{10,11... | collective-permute-start | bytes 3145736 | tf_op jit(solution)/shard_map/ppermute | solution.py:701
  43.1 18.6 %collective-permute-start.5 = (bf16[2,512,512]{2,1,0:T(8,128)(2,1)S(1)}, bf16[2,512,512]{2,1,0:T(8,128)(2,1)S(1)}, u32[]{:S(2)}, u32[]{:S(2)}) collective-permute-start(bf16[2,512,512]{2,1,0:T(8,128)(2,1)S(1)} %get-tuple-element.142), channel_id=1, source_target_pairs={{0,1},{1,0},{2,3},{3,2},{4,5},{5,4},{6,7},{7,6},{8,9},{9,8},{10,11... | collective-permute-start | bytes 3145736 | tf_op jit(solution)/shard_map/ppermute | solution.py:701
  43.3 18.4 %collective-permute-start.3 = (bf16[704,500]{1,0:T(8,128)(2,1)S(1)}, bf16[704,500]{1,0:T(8,128)(2,1)S(1)}, u32[]{:S(2)}, u32[]{:S(2)}) collective-permute-start(bf16[704,500]{1,0:T(8,128)(2,1)S(1)} %copy-done.1), channel_id=1, source_target_pairs={{0,2},{1,3},{2,0},{3,1},{4,6},{5,7},{6,4},{7,5},{8,10},{9,11},{10,... | collective-permute-start | bytes 2112008 | tf_op jit(solution)/shard_map/ppermute | solution.py:701
  47.5 14.2 %collective-permute-start.7 = (bf16[4,256,256]{2,1,0:T(8,128)(2,1)S(1)}, bf16[4,256,256]{2,1,0:T(8,128)(2,1)S(1)}, u32[]{:S(2)}, u32[]{:S(2)}) collective-permute-start(bf16[4,256,256]{2,1,0:T(8,128)(2,1)S(1)} %get-tuple-element.150), channel_id=1, source_target_pairs={{0,4},{4,0},{8,12},{12,8},{16,20},{20,16},{24,28},{28,24},{1,5},{5... | collective-permute-start | bytes 1572872 | tf_op jit(solution)/shard_map/ppermute | solution.py:701
  48.0 13.7 %collective-permute-start.8 = (bf16[4,256,256]{2,1,0:T(8,128)(2,1)S(1)}, bf16[4,256,256]{2,1,0:T(8,128)(2,1)S(1)}, u32[]{:S(2)}, u32[]{:S(2)}) collective-permute-start(bf16[4,256,256]{2,1,0:T(8,128)(2,1)S(1)} %get-tuple-element.152), channel_id=1, source_target_pairs={{0,8},{4,12},{8,0},{12,4},{16,24},{20,28},{24,16},{28,20},{1,9},{5... | collective-permute-start | bytes 1572872 | tf_op jit(solution)/shard_map/ppermute | solution.py:701
  95.5 18.6 %collective-permute-start.11 = (bf16[704,512]{1,0:T(8,128)(2,1)S(1)}, bf16[704,512]{1,0:T(8,128)(2,1)S(1)}, u32[]{:S(2)}, u32[]{:S(2)}) collective-permute-start(bf16[704,512]{1,0:T(8,128)(2,1)S(1)} %shard_map.209), channel_id=1, source_target_pairs={{0,2},{1,3},{2,0},{3,1},{4,6},{5,7},{6,4},{7,5},{8,10},{9,11},{10,... | collective-permute-start | bytes 2162696 | tf_op jit(solution)/shard_map/ppermute | solution.py:701
  97.0 14.0 %collective-permute-start.12 = (bf16[4,256,256]{2,1,0:T(8,128)(2,1)S(1)}, bf16[4,256,256]{2,1,0:T(8,128)(2,1)S(1)}, u32[]{:S(2)}, u32[]{:S(2)}) collective-permute-start(bf16[4,256,256]{2,1,0:T(8,128)(2,1)S(1)} %get-tuple-element.177), channel_id=1, source_target_pairs={{0,4},{4,0},{8,12},{12,8},{16,20},{20,16},{24,28},{28,24},{1,5},{5... | collective-permute-start | bytes 1572872 | tf_op jit(solution)/shard_map/ppermute | solution.py:701
  97.2 13.8 %collective-permute-start.13 = (bf16[4,256,256]{2,1,0:T(8,128)(2,1)S(1)}, bf16[4,256,256]{2,1,0:T(8,128)(2,1)S(1)}, u32[]{:S(2)}, u32[]{:S(2)}) collective-permute-start(bf16[4,256,256]{2,1,0:T(8,128)(2,1)S(1)} %get-tuple-element.178), channel_id=1, source_target_pairs={{0,8},{4,12},{8,0},{12,4},{16,24},{20,28},{24,16},{28,20},{1,9},{5... | collective-permute-start | bytes 1572872 | tf_op jit(solution)/shard_map/ppermute | solution.py:701
  111.3 8.8 %collective-permute-start.14 = (bf16[2,256,256]{2,1,0:T(8,128)(2,1)S(1)}, bf16[2,256,256]{2,1,0:T(8,128)(2,1)S(1)}, u32[]{:S(2)}, u32[]{:S(2)}) collective-permute-start(bf16[2,256,256]{2,1,0:T(8,128)(2,1)S(1)} %get-tuple-element.188), channel_id=1, source_target_pairs={{0,8},{4,12},{8,0},{12,4},{16,24},{20,28},{24,16},{28,20},{1,9},{5... | collective-permute-start | bytes 786440 | tf_op jit(solution)/shard_map/ppermute | solution.py:701
  112.4 7.7 %collective-permute-start.15 = (bf16[2,256,256]{2,1,0:T(8,128)(2,1)S(1)}, bf16[2,256,256]{2,1,0:T(8,128)(2,1)S(1)}, u32[]{:S(2)}, u32[]{:S(2)}) collective-permute-start(bf16[2,256,256]{2,1,0:T(8,128)(2,1)S(1)} %get-tuple-element.190), channel_id=1, source_target_pairs={{0,4},{4,0},{8,12},{12,8},{16,20},{20,16},{24,28},{28,24},{1,5},{5... | collective-permute-start | bytes 786440 | tf_op jit(solution)/shard_map/ppermute | solution.py:701
  118.7 22.5 %collective-permute-start.17 = (bf16[4,256,256]{2,1,0:T(8,128)(2,1)S(1)}, bf16[4,256,256]{2,1,0:T(8,128)(2,1)S(1)}, u32[]{:S(2)}, u32[]{:S(2)}) collective-permute-start(bf16[4,256,256]{2,1,0:T(8,128)(2,1)S(1)} %get-tuple-element.196), channel_id=1, source_target_pairs={{0,4},{4,0},{8,12},{12,8},{16,20},{20,16},{24,28},{28,24},{1,5},{5... | collective-permute-start | bytes 1572872 | tf_op jit(solution)/shard_map/ppermute | solution.py:701
  119.0 22.2 %collective-permute-start.18 = (bf16[4,256,256]{2,1,0:T(8,128)(2,1)S(1)}, bf16[4,256,256]{2,1,0:T(8,128)(2,1)S(1)}, u32[]{:S(2)}, u32[]{:S(2)}) collective-permute-start(bf16[4,256,256]{2,1,0:T(8,128)(2,1)S(1)} %get-tuple-element.197), channel_id=1, source_target_pairs={{0,8},{4,12},{8,0},{12,4},{16,24},{20,28},{24,16},{28,20},{1,9},{5... | collective-permute-start | bytes 1572872 | tf_op jit(solution)/shard_map/ppermute | solution.py:701
  120.1 21.0 %collective-permute-start.16 = (bf16[256,512]{1,0:T(8,128)(2,1)S(1)}, bf16[256,512]{1,0:T(8,128)(2,1)S(1)}, u32[]{:S(2)}, u32[]{:S(2)}) collective-permute-start(bf16[256,512]{1,0:T(8,128)(2,1)S(1)} %get-tuple-element.194), channel_id=1, source_target_pairs={{0,16},{4,20},{8,24},{12,28},{16,0},{20,4},{24,8},{28,12},{1,17},{... | collective-permute-start | bytes 786440 | tf_op jit(solution)/shard_map/ppermute | solution.py:701
  142.6 14.8 %collective-permute-start.20 = (bf16[2,256,256]{2,1,0:T(8,128)(2,1)S(1)}, bf16[2,256,256]{2,1,0:T(8,128)(2,1)S(1)}, u32[]{:S(2)}, u32[]{:S(2)}) collective-permute-start(bf16[2,256,256]{2,1,0:T(8,128)(2,1)S(1)} %get-tuple-element.215), channel_id=1, source_target_pairs={{0,8},{4,12},{8,0},{12,4},{16,24},{20,28},{24,16},{28,20},{1,9},{5... | collective-permute-start | bytes 786440 | tf_op jit(solution)/shard_map/ppermute | solution.py:701
  142.7 14.6 %collective-permute-start.21 = (bf16[2,256,256]{2,1,0:T(8,128)(2,1)S(1)}, bf16[2,256,256]{2,1,0:T(8,128)(2,1)S(1)}, u32[]{:S(2)}, u32[]{:S(2)}) collective-permute-start(bf16[2,256,256]{2,1,0:T(8,128)(2,1)S(1)} %get-tuple-element.217), channel_id=1, source_target_pairs={{0,4},{4,0},{8,12},{12,8},{16,20},{20,16},{24,28},{28,24},{1,5},{5... | collective-permute-start | bytes 786440 | tf_op jit(solution)/shard_map/ppermute | solution.py:701
  143.7 19.0 %collective-permute-start.32 = (bf16[256,512]{1,0:T(8,128)(2,1)S(1)}, bf16[256,512]{1,0:T(8,128)(2,1)S(1)}, u32[]{:S(2)}, u32[]{:S(2)}) collective-permute-start(bf16[256,512]{1,0:T(8,128)(2,1)S(1)} %add_convert_fusion.refs_0_), channel_id=1, source_target_pairs={{0,8},{4,12},{8,0},{12,4},{16,24},{20,28},{24,16},{28,20},{1,9},{5... | collective-permute-start | bytes 786440 | tf_op jit(solution)/shard_map/ppermute | solution.py:701
  145.2 17.5 %collective-permute-start.33 = (bf16[256,512]{1,0:T(8,128)(2,1)S(1)}, bf16[256,512]{1,0:T(8,128)(2,1)S(1)}, u32[]{:S(2)}, u32[]{:S(2)}) collective-permute-start(bf16[256,512]{1,0:T(8,128)(2,1)S(1)} %add_convert_fusion.refs_0_), channel_id=1, source_target_pairs={{0,4},{4,0},{8,12},{12,8},{16,20},{20,16},{24,28},{28,24},{1,5},{5... | collective-permute-start | bytes 786440 | tf_op jit(solution)/shard_map/ppermute | solution.py:701
  146.8 16.2 %collective-permute-start.31 = (bf16[256,512]{1,0:T(8,128)(2,1)S(1)}, bf16[256,512]{1,0:T(8,128)(2,1)S(1)}, u32[]{:S(2)}, u32[]{:S(2)}) collective-permute-start(bf16[256,512]{1,0:T(8,128)(2,1)S(1)} %add_convert_fusion.refs_0_), channel_id=1, source_target_pairs={{0,16},{4,20},{8,24},{12,28},{16,0},{20,4},{24,8},{28,12},{1,17},{... | collective-permute-start | bytes 786440 | tf_op jit(solution)/shard_map/ppermute | solution.py:701
  157.4 16.6 %collective-permute-start.22 = (bf16[256,512]{1,0:T(8,128)(2,1)S(1)}, bf16[256,512]{1,0:T(8,128)(2,1)S(1)}, u32[]{:S(2)}, u32[]{:S(2)}) collective-permute-start(bf16[256,512]{1,0:T(8,128)(2,1)S(1)} %get-tuple-element.219), channel_id=1, source_target_pairs={{0,16},{4,20},{8,24},{12,28},{16,0},{20,4},{24,8},{28,12},{1,17},{... | collective-permute-start | bytes 786440 | tf_op jit(solution)/shard_map/ppermute | solution.py:701
  162.7 12.9 %collective-permute-start.35 = (bf16[256,512]{1,0:T(8,128)(2,1)S(1)}, bf16[256,512]{1,0:T(8,128)(2,1)S(1)}, u32[]{:S(2)}, u32[]{:S(2)}) collective-permute-start(bf16[256,512]{1,0:T(8,128)(2,1)S(1)} %collective-permute-done.32.refs_2_), channel_id=1, source_target_pairs={{0,4},{4,0},{8,12},{12,8},{16,20},{20,16},{24,28},{28,24},{1,5},{5... | collective-permute-start | bytes 786440 | tf_op jit(solution)/shard_map/ppermute | solution.py:701
  163.1 14.3 %collective-permute-start.34 = (bf16[256,512]{1,0:T(8,128)(2,1)S(1)}, bf16[256,512]{1,0:T(8,128)(2,1)S(1)}, u32[]{:S(2)}, u32[]{:S(2)}) collective-permute-start(bf16[256,512]{1,0:T(8,128)(2,1)S(1)} %collective-permute-done.31.refs_1_), channel_id=1, source_target_pairs={{0,8},{4,12},{8,0},{12,4},{16,24},{20,28},{24,16},{28,20},{1,9},{5... | collective-permute-start | bytes 786440 | tf_op jit(solution)/shard_map/ppermute | solution.py:701
  164.8 37.6 %collective-permute-start.23 = (bf16[704,512]{1,0:T(8,128)(2,1)S(1)}, bf16[704,512]{1,0:T(8,128)(2,1)S(1)}, u32[]{:S(2)}, u32[]{:S(2)}) collective-permute-start(bf16[704,512]{1,0:T(8,128)(2,1)S(1)} %shard_map.217), channel_id=1, source_target_pairs={{0,2},{1,3},{2,0},{3,1},{4,6},{5,7},{6,4},{7,5},{8,10},{9,11},{10,... | collective-permute-start | bytes 2162696 | tf_op jit(solution)/shard_map/ppermute | solution.py:701
  174.2 12.1 %collective-permute-start.25 = (bf16[256,512]{1,0:T(8,128)(2,1)S(1)}, bf16[256,512]{1,0:T(8,128)(2,1)S(1)}, u32[]{:S(2)}, u32[]{:S(2)}) collective-permute-start(bf16[256,512]{1,0:T(8,128)(2,1)S(1)} %add_convert_fusion.1.refs_0_), channel_id=1, source_target_pairs={{0,8},{4,12},{8,0},{12,4},{16,24},{20,28},{24,16},{28,20},{1,9},{5... | collective-permute-start | bytes 786440 | tf_op jit(solution)/shard_map/ppermute | solution.py:701
  174.2 13.2 %collective-permute-start.26 = (bf16[256,512]{1,0:T(8,128)(2,1)S(1)}, bf16[256,512]{1,0:T(8,128)(2,1)S(1)}, u32[]{:S(2)}, u32[]{:S(2)}) collective-permute-start(bf16[256,512]{1,0:T(8,128)(2,1)S(1)} %add_convert_fusion.1.refs_0_), channel_id=1, source_target_pairs={{0,4},{4,0},{8,12},{12,8},{16,20},{20,16},{24,28},{28,24},{1,5},{5... | collective-permute-start | bytes 786440 | tf_op jit(solution)/shard_map/ppermute | solution.py:701
  175.6 14.4 %collective-permute-start.24 = (bf16[256,512]{1,0:T(8,128)(2,1)S(1)}, bf16[256,512]{1,0:T(8,128)(2,1)S(1)}, u32[]{:S(2)}, u32[]{:S(2)}) collective-permute-start(bf16[256,512]{1,0:T(8,128)(2,1)S(1)} %add_convert_fusion.1.refs_0_), channel_id=1, source_target_pairs={{0,16},{4,20},{8,24},{12,28},{16,0},{20,4},{24,8},{28,12},{1,17},{... | collective-permute-start | bytes 786440 | tf_op jit(solution)/shard_map/ppermute | solution.py:701
  177.4 13.9 %collective-permute-start.36 = (bf16[256,512]{1,0:T(8,128)(2,1)S(1)}, bf16[256,512]{1,0:T(8,128)(2,1)S(1)}, u32[]{:S(2)}, u32[]{:S(2)}) collective-permute-start(bf16[256,512]{1,0:T(8,128)(2,1)S(1)} %collective-permute-done.31.refs_1_), channel_id=1, source_target_pairs={{0,4},{4,0},{8,12},{12,8},{16,20},{20,16},{24,28},{28,24},{1,5},{5... | collective-permute-start | bytes 786440 | tf_op jit(solution)/shard_map/ppermute | solution.py:701
  186.2 9.2 %collective-permute-start.37 = (bf16[256,512]{1,0:T(8,128)(2,1)S(1)}, bf16[256,512]{1,0:T(8,128)(2,1)S(1)}, u32[]{:S(2)}, u32[]{:S(2)}) collective-permute-start(bf16[256,512]{1,0:T(8,128)(2,1)S(1)} %collective-permute-done.34.refs_3_), channel_id=1, source_target_pairs={{0,4},{4,0},{8,12},{12,8},{16,20},{20,16},{24,28},{28,24},{1,5},{5... | collective-permute-start | bytes 786440 | tf_op jit(solution)/shard_map/ppermute | solution.py:701
  187.5 13.6 %collective-permute-start.28 = (bf16[256,512]{1,0:T(8,128)(2,1)S(1)}, bf16[256,512]{1,0:T(8,128)(2,1)S(1)}, u32[]{:S(2)}, u32[]{:S(2)}) collective-permute-start(bf16[256,512]{1,0:T(8,128)(2,1)S(1)} %collective-permute-done.25.refs_2_), channel_id=1, source_target_pairs={{0,4},{4,0},{8,12},{12,8},{16,20},{20,16},{24,28},{28,24},{1,5},{5... | collective-permute-start | bytes 786440 | tf_op jit(solution)/shard_map/ppermute | solution.py:701
  190.0 11.1 %collective-permute-start.27 = (bf16[256,512]{1,0:T(8,128)(2,1)S(1)}, bf16[256,512]{1,0:T(8,128)(2,1)S(1)}, u32[]{:S(2)}, u32[]{:S(2)}) collective-permute-start(bf16[256,512]{1,0:T(8,128)(2,1)S(1)} %collective-permute-done.24.refs_1_), channel_id=1, source_target_pairs={{0,8},{4,12},{8,0},{12,4},{16,24},{20,28},{24,16},{28,20},{1,9},{5... | collective-permute-start | bytes 786440 | tf_op jit(solution)/shard_map/ppermute | solution.py:701
  198.0 9.2 %collective-permute-start.29 = (bf16[256,512]{1,0:T(8,128)(2,1)S(1)}, bf16[256,512]{1,0:T(8,128)(2,1)S(1)}, u32[]{:S(2)}, u32[]{:S(2)}) collective-permute-start(bf16[256,512]{1,0:T(8,128)(2,1)S(1)} %collective-permute-done.24.refs_1_), channel_id=1, source_target_pairs={{0,4},{4,0},{8,12},{12,8},{16,20},{20,16},{24,28},{28,24},{1,5},{5... | collective-permute-start | bytes 786440 | tf_op jit(solution)/shard_map/ppermute | solution.py:701
  201.1 9.5 %collective-permute-start.30 = (bf16[256,512]{1,0:T(8,128)(2,1)S(1)}, bf16[256,512]{1,0:T(8,128)(2,1)S(1)}, u32[]{:S(2)}, u32[]{:S(2)}) collective-permute-start(bf16[256,512]{1,0:T(8,128)(2,1)S(1)} %collective-permute-done.27.refs_3_), channel_id=1, source_target_pairs={{0,4},{4,0},{8,12},{12,8},{16,20},{20,16},{24,28},{28,24},{1,5},{5... | collective-permute-start | bytes 786440 | tf_op jit(solution)/shard_map/ppermute | solution.py:701
  (19 other events, 141.3 us)
